TPU v7x, 32 devices: a whole 2x2x4 slice. The times are simulated.
32 devices in a mesh: ctx: 8 (over y, x, core), hd: 4 (over z).
Axes of the slice: x: 2, y: 2, z: 4, core: 2. Of those that a mesh axis runs over, the one named last changes fastest.
Arguments:
- cot: bfloat16 [32, 1024], P('ctx'), may hold values from -768 to 768
- resid: bfloat16 [32, 1024], P('ctx'), may hold values from -17 to 17
- norm_gain: bfloat16 [1024], replicated, may hold values from 0.5 to 1.5
- w_in: bfloat16 [1024, 4096], P(None, 'hd'), may hold values from -0.1875 to 0.1875
- w_out: bfloat16 [4096, 1024], P('hd'), may hold values from -0.09375 to 0.09375
- w_proj: bfloat16 [1024, 1024], P('hd', 'ctx'), may hold values from -0.1875 to 0.1875
- queries: bfloat16 [32, 1024], P('ctx', 'hd'), may hold values from -36 to 36
- keys: bfloat16 [2048, 1024], P('ctx', 'hd'), may hold values from -9 to 9
- values: bfloat16 [2048, 1024], P('ctx', 'hd'), may hold values from -6 to 6
- latent_pos: int32 [32], replicated, may hold values from 1024 to 2047, as said below
- seg_start: int32 [32], replicated, may hold values from 768 to 2046, as said below
Outputs:
- query_grad: bfloat16 [32, 1024], P('ctx', 'hd')
- key_grad: bfloat16 [2048, 1024], P('ctx', 'hd')
- value_grad: bfloat16 [2048, 1024], P('ctx', 'hd')
Inputs may be any that keep to these rules, and one draw needn't show every extreme that they name: `latent_pos`: not falling along the latents. seg_start of a latent is 1 to 256 below its latent_pos.
All inputs are finite; a program needn't handle non-finite values.
Results may differ from a plain program's by a relative error of at most 0.012.
Values may be sent and summed in bfloat16 or wider, within the bound.
No kernel may reach another device: no remote copies, remote signals or barrier semaphores. Data moves between devices by JAX's collectives and lax.ppermute only.
A program may use at most 64 MiB of HBM per device.

v0:
```python
import math

import jax
import jax.numpy as jnp
from jax import lax
from jax.sharding import PartitionSpec as P

HDIM = 64


def joined(value, axis, join):
    pieces = jax.tree.map(lambda part: lax.all_gather(part, axis), value)
    head = jax.tree.map(lambda part: part[0], pieces)
    tail = jax.tree.map(lambda part: part[1:], pieces)
    total, _ = lax.scan(lambda total, slab: (join(total, slab), None), head, tail)
    return total


def gelu_slope(values_in):
    inner = 0.7978845608028654 * (values_in + 0.044715 * values_in * values_in * values_in)
    tangent = jnp.tanh(inner)
    return 0.5 * (1.0 + tangent) + 0.5 * values_in * (
        1.0 - tangent * tangent
    ) * 0.7978845608028654 * (1.0 + 0.134145 * values_in * values_in)


def combine_totals(earlier, later):
    top_first, total_first, weight_first = earlier
    top_second, total_second, weight_second = later
    top_joint = jnp.maximum(top_first, top_second)
    factor_first = jnp.exp(top_first - top_joint)
    factor_second = jnp.exp(top_second - top_joint)
    return (
        top_joint,
        total_first * factor_first + total_second * factor_second,
        weight_first * factor_first + weight_second * factor_second,
    )


def per_device(
    cot, resid, norm_gain, w_in, w_out, w_proj, queries, keys, values, latent_pos, seg_start
):
    contract_last = (((1,), (1,)), ((), ()))
    rows_f32 = resid.astype(jnp.float32)
    inv_rms = lax.rsqrt(jnp.mean(rows_f32 * rows_f32, axis=-1, keepdims=True) + 1e-05)
    gain_f32 = norm_gain.astype(jnp.float32)
    normed = (rows_f32 * inv_rms * gain_f32).astype(jnp.bfloat16)
    pre_act = jnp.dot(normed, w_in, preferred_element_type=jnp.float32)
    hidden_grad = lax.dot_general(cot, w_out, contract_last, preferred_element_type=jnp.float32)
    pre_grad = (hidden_grad * gelu_slope(pre_act)).astype(jnp.bfloat16)
    partial_grad = lax.dot_general(
        pre_grad, w_in, contract_last, preferred_element_type=jnp.float32
    )
    whole_proj = lax.all_gather(w_proj, "ctx", axis=1, tiled=True)
    normed_grad = lax.psum(partial_grad, "hd")
    weighted = normed_grad * gain_f32
    unit_rows = rows_f32 * inv_rms
    resid_grad = (
        cot.astype(jnp.float32)
        + inv_rms * (weighted - unit_rows * jnp.mean(weighted * unit_rows, axis=-1, keepdims=True))
    ).astype(jnp.bfloat16)
    out_grad = lax.dot_general(
        resid_grad, whole_proj, contract_last, preferred_element_type=jnp.float32
    ).astype(jnp.bfloat16)
    all_queries, all_grads = (
        lax.all_gather(queries, "ctx", axis=0, tiled=True),
        lax.all_gather(out_grad, "ctx", axis=0, tiled=True),
    )
    ctx_count = lax.axis_size("ctx")
    lat_dev = cot.shape[0]
    latents = lat_dev * ctx_count
    blocks = max(1, min(lat_dev, latents // 512))
    per_block = lat_dev // blocks
    block_rows = ctx_count * per_block
    features = queries.shape[1]
    local_heads = features // HDIM
    events_dev = keys.shape[0]
    event_index = lax.axis_index("ctx") * events_dev + jnp.arange(events_dev, dtype=jnp.int32)
    factor = 1.0 / math.sqrt(HDIM)
    head_keys = keys.reshape(events_dev, local_heads, HDIM)
    head_values = values.reshape(events_dev, local_heads, HDIM)

    def block_view(array, which):
        shaped = array.reshape((ctx_count, blocks, per_block) + array.shape[1:])
        picked = lax.dynamic_index_in_dim(shaped, which, 1, keepdims=False)
        return picked.reshape((block_rows,) + array.shape[1:])

    def block_terms(which):
        block_q = block_view(all_queries, which).reshape(block_rows, local_heads, HDIM)
        block_do = block_view(all_grads, which).reshape(block_rows, local_heads, HDIM)
        block_pos = block_view(latent_pos, which)
        block_start = block_view(seg_start, which)
        visible = (event_index[None, :] >= block_start[:, None]) & (
            event_index[None, :] <= block_pos[:, None]
        )
        scores = factor * jnp.einsum(
            "rhe,khe->hrk", block_q, head_keys, preferred_element_type=jnp.float32
        )
        prob_grad = jnp.einsum(
            "rhe,khe->hrk", block_do, head_values, preferred_element_type=jnp.float32
        )
        return (block_q, block_do, visible[None], scores, prob_grad)

    def first_pass(carry, which):
        block_q, block_do, visible, scores, prob_grad = block_terms(which)
        block_top = jnp.max(jnp.where(visible, scores, -1e30), axis=2)
        expo = jnp.where(visible, jnp.exp(scores - block_top[..., None]), 0.0)
        return (carry, (block_top, jnp.sum(expo, axis=2), jnp.sum(expo * prob_grad, axis=2)))

    unused, local_totals = lax.scan(first_pass, jnp.int32(0), jnp.arange(blocks, dtype=jnp.int32))
    tops, totals, weight_sums = joined(local_totals, "ctx", combine_totals)
    deltas = weight_sums / totals

    def second_pass(carry, which):
        key_acc, value_acc = carry
        block_q, block_do, visible, scores, prob_grad = block_terms(which)
        block_top = lax.dynamic_index_in_dim(tops, which, 0, keepdims=False)
        block_total = lax.dynamic_index_in_dim(totals, which, 0, keepdims=False)
        block_delta = lax.dynamic_index_in_dim(deltas, which, 0, keepdims=False)
        expo = jnp.where(visible, jnp.exp(scores - block_top[..., None]), 0.0)
        probs = expo / block_total[..., None]
        prob_round = probs.astype(jnp.bfloat16)
        score_grad = (factor * probs * (prob_grad - block_delta[..., None])).astype(jnp.bfloat16)
        value_acc = value_acc + jnp.einsum(
            "hrk,rhe->khe", prob_round, block_do, preferred_element_type=jnp.float32
        )
        key_acc = key_acc + jnp.einsum(
            "hrk,rhe->khe", score_grad, block_q, preferred_element_type=jnp.float32
        )
        query_part = jnp.einsum(
            "hrk,khe->rhe", score_grad, head_keys, preferred_element_type=jnp.float32
        )
        query_part = query_part.reshape(ctx_count, per_block, features)
        return ((key_acc, value_acc), query_part)

    start_acc = (
        jnp.zeros((events_dev, local_heads, HDIM), jnp.float32),
        jnp.zeros((events_dev, local_heads, HDIM), jnp.float32),
    )
    (key_acc, value_acc), query_parts = lax.scan(
        second_pass, start_acc, jnp.arange(blocks, dtype=jnp.int32)
    )
    query_parts = lax.psum_scatter(query_parts, "ctx", scatter_dimension=1, tiled=True)
    query_grad = query_parts.reshape(lat_dev, features).astype(jnp.bfloat16)
    key_grad = key_acc.reshape(events_dev, features).astype(jnp.bfloat16)
    value_grad = value_acc.reshape(events_dev, features).astype(jnp.bfloat16)
    return (query_grad, key_grad, value_grad)


def solution(mesh):
    in_specs = (
        P("ctx", None),
        P("ctx", None),
        P(),
        P(None, "hd"),
        P("hd", None),
        P("hd", "ctx"),
        P("ctx", "hd"),
        P("ctx", "hd"),
        P("ctx", "hd"),
        P(),
        P(),
    )
    out_specs = (P("ctx", "hd"), P("ctx", "hd"), P("ctx", "hd"))
    return jax.shard_map(
        per_device, mesh=mesh, in_specs=in_specs, out_specs=out_specs, check_vma=False
    )
```

profile of v0, /device:TPU:0, one launch (start us, length us, event | category | flops | bytes accessed | tf_op | source)
XLA Modules:
  0.0 109.4 jit_solution(16017298675824774815)
XLA Ops:
  0.7 0.8 convert_element_type.55
  1.5 0.8 fusion.22
  2.3 1.1 %fusion.38 = f32[4,1024]{1,0:T(4,128)S(1)} fusion(bf16[1024,1024]{1,0:T(8,128)(2,1)S(1)} %copy-done, bf16[4,1024]{1,0:T(4,128)(2,1)} %param.14, f32[1024]{0:T(1024)S(1)} %convert_element_type.55, f32[4]{0:T(128)S(1)} %add_rsqrt_fusion), kind=kOutput, calls=%fused_computation.59 | convolution fusion | flops 8404992 | bytes 2125840 | tf_op jit(solution)/shard_map/dot_general | solution.py:48
  3.5 2.9 %fusion.4 = f32[4,1024]{1,0:T(4,128)S(1)} fusion(bf16[1024,1024]{1,0:T(8,128)(2,1)S(1)} %copy-done, bf16[4,1024]{1,0:T(4,128)(2,1)S(1)} %copy-done.5, bf16[1024,1024]{1,0:T(8,128)(2,1)} %param.17, f32[4,1024]{1,0:T(4,128)S(1)} %fusion.38), kind=kOutput, calls=%fused_computation.14 | convolution fusion | flops 16855040 | bytes 4235264 | tf_op jit(solution)/shard_map/dot_general | solution.py:51
  6.4 20.5 %psum.7 = f32[4,1024]{1,0:T(4,128)S(1)} all-reduce(f32[4,1024]{1,0:T(4,128)S(1)} %fusion.4), channel_id=1, replica_groups=mesh['ctx'=8,'hd'=4] {'hd'}, use_global_device_ids=true, to_apply=%region_3.4 | all-reduce | flops 4096 | bytes 32768 | tf_op jit(solution)/shard_map/psum | solution.py:55
  26.9 0.2 fusion.17
  27.1 10.0 %all_gather.32 = bf16[256,1024]{1,0:T(8,128)(2,1)S(1)} all-gather(bf16[256,128]{1,0:T(8,128)(2,1)S(1)} %copy-done.4), channel_id=1, replica_groups=mesh['ctx'=8,'hd'=4] {'ctx'}, dimensions={1}, use_global_device_ids=true | all-gather | bytes 589824 | tf_op jit(solution)/shard_map/all_gather | solution.py:54
  37.1 0.2 fusion.5
  37.3 8.9 %all-gather.6 = bf16[8,4,256]{2,1,0:T(4,128)(2,1)S(1)} all-gather(bf16[1,4,256]{2,1,0:T(4,128)(2,1)S(1)} %fusion.5), channel_id=1, replica_groups=mesh['ctx'=8,'hd'=4] {'ctx'}, dimensions={0}, use_global_device_ids=true | all-gather | bytes 18432 | tf_op jit(solution)/shard_map/all_gather | solution.py:67
  46.6 7.9 %all-gather.3 = bf16[8,4,256]{2,1,0:T(4,128)(2,1)S(1)} all-gather(bf16[1,4,256]{2,1,0:T(4,128)(2,1)S(1)} %bitcast.83), channel_id=1, replica_groups=mesh['ctx'=8,'hd'=4] {'ctx'}, dimensions={0}, use_global_device_ids=true | all-gather | bytes 18432 | tf_op jit(solution)/shard_map/all_gather | solution.py:66
  54.6 0.2 select_reduce_fusion
  54.9 0.2 multiply_reduce_fusion
  55.2 8.9 %all-gather.7 = f32[8,4,32]{2,1,0:T(4,128)S(1)} all-gather(f32[1,4,32]{2,1,0:T(4,128)S(1)} %bitcast.82), channel_id=4, replica_groups=mesh['ctx'=8,'hd'=4] {'ctx'}, dimensions={0}, use_global_device_ids=true | all-gather | bytes 4608 | tf_op jit(solution)/shard_map/all_gather | solution.py:12
  64.0 7.9 %all-gather.5 = f32[8,4,32]{2,1,0:T(4,128)S(1)} all-gather(f32[1,4,32]{2,1,0:T(4,128)S(1)} %bitcast.81), channel_id=3, replica_groups=mesh['ctx'=8,'hd'=4] {'ctx'}, dimensions={0}, use_global_device_ids=true | all-gather | bytes 4608 | tf_op jit(solution)/shard_map/all_gather | solution.py:12
  72.0 8.9 %all-gather.4 = f32[8,4,32]{2,1,0:T(4,128)S(1)} all-gather(f32[1,4,32]{2,1,0:T(4,128)S(1)} %bitcast.80), channel_id=2, replica_groups=mesh['ctx'=8,'hd'=4] {'ctx'}, dimensions={0}, use_global_device_ids=true | all-gather | bytes 4608 | tf_op jit(solution)/shard_map/all_gather | solution.py:12
  80.8 0.5 while.2
  81.3 0.3 convolution_convert_fusion
  81.6 0.8 copy.57
  82.5 0.2 convolution_convert_fusion.1
  82.7 0.8 copy.56
  83.5 0.1 convolution_bitcast_fusion
  83.8 23.6 %all-reduce = bf16[1,8,4,256]{3,2,1,0:T(4,128)(2,1)S(1)} all-reduce(f32[1,8,4,256]{3,2,1,0:T(4,128)S(1)} %broadcast_in_dim.69), channel_id=5, replica_groups=mesh['ctx'=8,'hd'=4] {'ctx'}, use_global_device_ids=true, to_apply=%region_8.9.clone | all-reduce | flops 8192 | bytes 49152
  107.4 0.7 dynamic-slice
  108.1 1.3 %fusion.50 = bf16[4,256]{1,0:T(4,128)(2,1)} fusion(bf16[1,8,4,256]{3,2,1,0:T(4,128)(2,1)S(1)} %all-reduce, u32[]{:T(128)} %bitcast.30), kind=kLoop, calls=%fused_computation.71 | loop fusion | bytes 4100 | tf_op jit(solution)/shard_map/convert_element_type | solution.py:144
  (59 shorter events, 1.2 us)
Async XLA Ops:
  0.6 1.7 %copy-start = (bf16[1024,1024]{1,0:T(8,128)(2,1)S(1)}, bf16[1024,1024]{1,0:T(8,128)(2,1)}, u32[]{:S(2)}) copy-start(bf16[1024,1024]{1,0:T(8,128)(2,1)} %param.16) | copy-start | bytes 6291460
  0.6 2.8 %copy-start.5 = (bf16[4,1024]{1,0:T(4,128)(2,1)S(1)}, bf16[4,1024]{1,0:T(4,128)(2,1)}, u32[]{:S(2)}) copy-start(bf16[4,1024]{1,0:T(4,128)(2,1)} %param.13) | copy-start | bytes 24580
  3.4 23.5 %copy-start.3 = (bf16[4,1024]{1,0:T(4,128)(2,1)S(1)}, bf16[4,1024]{1,0:T(4,128)(2,1)}, u32[]{:S(2)}) copy-start(bf16[4,1024]{1,0:T(4,128)(2,1)} %param.14) | copy-start | bytes 24580
  3.4 23.6 %copy-start.4 = (bf16[256,128]{1,0:T(8,128)(2,1)S(1)}, bf16[256,128]{1,0:T(8,128)(2,1)}, u32[]{:S(2)}) copy-start(bf16[256,128]{1,0:T(8,128)(2,1)} %param.18) | copy-start | bytes 196612
  3.4 42.9 %copy-start.7 = (s32[32]{0:T(128)S(1)}, s32[32]{0:T(128)}, u32[]{:S(2)}) copy-start(s32[32]{0:T(128)} %param.22) | copy-start | bytes 388
  3.5 42.9 %copy-start.8 = (s32[32]{0:T(128)S(1)}, s32[32]{0:T(128)}, u32[]{:S(2)}) copy-start(s32[32]{0:T(128)} %param.23) | copy-start | bytes 388
  3.5 43.0 %copy-start.1 = (bf16[256,256]{1,0:T(8,128)(2,1)S(1)}, bf16[256,256]{1,0:T(8,128)(2,1)}, u32[]{:S(2)}) copy-start(bf16[256,256]{1,0:T(8,128)(2,1)} %param.20) | copy-start | bytes 393220
  3.5 43.1 %copy-start.6 = (bf16[4,256]{1,0:T(4,128)(2,1)S(1)}, bf16[4,256]{1,0:T(4,128)(2,1)}, u32[]{:S(2)}) copy-start(bf16[4,256]{1,0:T(4,128)(2,1)} %param.19) | copy-start | bytes 6148
  3.5 51.3 %copy-start.2 = (bf16[256,256]{1,0:T(8,128)(2,1)S(1)}, bf16[256,256]{1,0:T(8,128)(2,1)}, u32[]{:S(2)}) copy-start(bf16[256,256]{1,0:T(8,128)(2,1)} %param.21) | copy-start | bytes 393220
  46.2 61.2 %copy-start.9 = (u32[32]{0:T(128)S(1)}, u32[32]{0:T(128)}, u32[]{:S(2)}) copy-start(u32[32]{0:T(128)} %constant.106) | copy-start | bytes 388
where the time goes:
time: 110 us; the launch traced here: 109 us
  blocking collectives  96.6 us (88%)
  matrix products  5.33 us (5%)
  local copies, waits for them, and re-layouts  4.08 us (4%)
  other arithmetic  2.38 us (2%)
    all_gather x3, blocking collectives, joined(): pieces = jax.tree.map(lambda part: lax.all_gather(part, axis), value)  25.7 us
    unnamed x1, blocking collectives  23.6 us
    psum x1, blocking collectives, per_device(): normed_grad = lax.psum(partial_grad, 'hd')  20.5 us
    all_gather x1, blocking collectives, per_device(): whole_proj = lax.all_gather(w_proj, 'ctx', axis=1, tiled=True)  10 us
    all_gather x1, blocking collectives, per_device(): lax.all_gather(out_grad, 'ctx', axis=0, tiled=True)  8.9 us
    all_gather x1, blocking collectives, per_device(): lax.all_gather(queries, 'ctx', axis=0, tiled=True)  7.93 us
    dot_general x1, matrix products, per_device(): lax.dot_general(pre_grad, w_in, contract_last, preferred_element_type=jnp...  2.89 us
    unnamed x25, local copies, waits for them, and re-layouts  2.44 us

commit v1 on v0

--- a/solution.py
+++ b/solution.py
@@ -1,11 +1,15 @@
+import functools
 import math
 
 import jax
 import jax.numpy as jnp
 from jax import lax
+from jax.experimental import pallas as pl
+from jax.experimental.pallas import tpu as pltpu
 from jax.sharding import PartitionSpec as P
 
 HDIM = 64
+WINDOW = 256
 
 
 def joined(value, axis, join):
@@ -37,7 +41,7 @@
     )
 
 
-def per_device(
+def per_device_streamed(
     cot, resid, norm_gain, w_in, w_out, w_proj, queries, keys, values, latent_pos, seg_start
 ):
     contract_last = (((1,), (1,)), ((), ()))
@@ -147,6 +151,261 @@
     return (query_grad, key_grad, value_grad)
 
 
+NT = (((1,), (1,)), ((), ()))
+TN = (((0,), (0,)), ((), ()))
+Q_ROWS = 16
+
+
+def pack_kernel(k_ref, v_ref, w_ref, q_ref, out_ref):
+    events, half = k_ref.shape[0], w_ref.shape[0] // 2
+    out_ref[:events, :] = k_ref[...]
+    out_ref[events : 2 * events, :] = v_ref[...]
+    base = 2 * events
+    out_ref[base : base + half, : w_ref.shape[1]] = w_ref[:half, :]
+    out_ref[base : base + half, w_ref.shape[1] :] = w_ref[half:, :]
+    rows = q_ref[...].astype(jnp.float32)
+    spare = jnp.zeros((Q_ROWS - rows.shape[0], rows.shape[1]), jnp.float32)
+    out_ref[base + half :, :] = jnp.concatenate([rows, spare], axis=0).astype(jnp.bfloat16)
+
+
+def ordered(own, other):
+    own, other = own.astype(jnp.float32), other.astype(jnp.float32)
+    first = lax.axis_index("ctx") % 2 == 0
+    return jnp.where(
+        first, jnp.concatenate([own, other], axis=0), jnp.concatenate([other, own], axis=0)
+    )
+
+
+def rms_parts(rows):
+    inv_rms = lax.rsqrt(jnp.mean(rows * rows, axis=-1, keepdims=True) + 1e-05)
+    return inv_rms, rows * inv_rms
+
+
+def mlp_kernel(cot_ref, cot_other, resid_ref, resid_other, gain_ref, w_in_ref, w_out_ref, out_ref):
+    cot = ordered(cot_ref[...], cot_other[...]).astype(jnp.bfloat16)
+    rows = ordered(resid_ref[...], resid_other[...])
+    unit = rms_parts(rows)[1]
+    normed = (unit * gain_ref[...].astype(jnp.float32)).astype(jnp.bfloat16)
+    pre_act = jnp.dot(normed, w_in_ref[...], preferred_element_type=jnp.float32)
+    hidden_grad = lax.dot_general(cot, w_out_ref[...], NT, preferred_element_type=jnp.float32)
+    pre_grad = (hidden_grad * gelu_slope(pre_act)).astype(jnp.bfloat16)
+    out_ref[...] = lax.dot_general(pre_grad, w_in_ref[...], NT, preferred_element_type=jnp.float32)
+
+
+def resid_kernel(part_ref, arrived_ref, cot_ref, cot_other, resid_ref, resid_other, gain_ref, out_ref):
+    rows = ordered(resid_ref[...], resid_other[...])
+    inv_rms, unit = rms_parts(rows)
+    weighted = (part_ref[...] + arrived_ref[...]) * gain_ref[...].astype(jnp.float32)
+    cot = ordered(cot_ref[...], cot_other[...])
+    grad = cot + inv_rms * (weighted - unit * jnp.mean(weighted * unit, axis=-1, keepdims=True))
+    out_ref[...] = grad.astype(jnp.bfloat16)
+
+
+def attention_kernel(
+    row_offsets, pack_offsets, latents, lat_dev, events_dev, first_block, *refs
+):
+    n_rows, n_packs = len(row_offsets), len(pack_offsets)
+    pos_ref, start_ref = refs[:2]
+    row_refs = refs[2 : 2 + n_rows]
+    pack_refs = refs[2 + n_rows : 2 + n_rows + n_packs]
+    qg_ref, kg_ref, vg_ref, packs, rows_all, qg_all, own_probs, own_scores, sems = refs[
+        2 + n_rows + n_packs :
+    ]
+    me = lax.axis_index("ctx")
+    blocks = n_packs
+    features = packs.shape[2]
+    heads = features // HDIM
+    lanes = heads * latents
+    factor = 1.0 / math.sqrt(HDIM)
+    copies = [
+        pltpu.make_async_copy(ref, packs.at[me ^ offset], sems.at[slot])
+        for slot, (offset, ref) in enumerate(zip(pack_offsets, pack_refs))
+    ]
+    for copy in copies:
+        copy.start()
+    for offset, ref in zip(row_offsets, row_refs):
+        rows_all[(me // 2) ^ offset] = ref[...].astype(jnp.float32)
+    resid_grad = rows_all[...].reshape(latents, rows_all.shape[2]).astype(jnp.bfloat16)
+    for copy in copies:
+        copy.wait()
+
+    base = 2 * events_dev
+    half = packs.shape[1] - base - Q_ROWS
+    halves = [packs[block, base : base + half, :] for block in range(blocks)]
+    cols = features // 2
+    upper = jnp.concatenate([piece[:, :cols] for piece in halves], axis=1)
+    lower = jnp.concatenate([piece[:, cols:] for piece in halves], axis=1)
+    out_grad = jnp.concatenate(
+        [
+            lax.dot_general(resid_grad, piece, NT, preferred_element_type=jnp.float32)
+            for piece in (upper, lower)
+        ],
+        axis=1,
+    )
+    out_grad = out_grad.astype(jnp.bfloat16).astype(jnp.float32)
+    queries = jnp.concatenate(
+        [
+            packs[block, base + half :, :].astype(jnp.float32)[:lat_dev]
+            for block in range(blocks)
+        ],
+        axis=0,
+    )
+    lane_head = lax.broadcasted_iota(jnp.int32, (lanes, features), 0) // latents
+    own_head = lane_head == lax.broadcasted_iota(jnp.int32, (lanes, features), 1) // HDIM
+
+    def spread(array):
+        return jnp.where(own_head, jnp.concatenate([array] * heads, axis=0), 0.0)
+
+    wide_q, wide_g = spread(queries), spread(out_grad)
+    wide_qt, wide_gt = wide_q.T.astype(jnp.bfloat16), wide_g.T.astype(jnp.bfloat16)
+    wide_q, wide_g = wide_q.astype(jnp.bfloat16), wide_g.astype(jnp.bfloat16)
+
+    lane = lax.broadcasted_iota(jnp.int32, (1, lanes), 1) % latents
+    pos, start = jnp.zeros((1, lanes), jnp.int32), jnp.zeros((1, lanes), jnp.int32)
+    for latent in range(latents):
+        pos = jnp.where(lane == latent, pos_ref[latent], pos)
+        start = jnp.where(lane == latent, start_ref[latent], start)
+
+    used = range(first_block, blocks)
+    keys = jnp.concatenate([packs[block, :events_dev, :] for block in used], axis=0)
+    values = jnp.concatenate([packs[block, events_dev:base, :] for block in used], axis=0)
+    spot = first_block * events_dev + lax.broadcasted_iota(jnp.int32, (keys.shape[0], lanes), 0)
+    visible = (spot >= start) & (spot <= pos)
+    scores = factor * jnp.dot(keys, wide_qt, preferred_element_type=jnp.float32)
+    scores = jnp.where(visible, scores, -1e30)
+    top = jnp.max(scores, axis=0, keepdims=True)
+    expo = jnp.where(visible, jnp.exp(scores - top), 0.0)
+    probs = expo * (1.0 / jnp.sum(expo, axis=0, keepdims=True))
+    prob_grad = jnp.dot(values, wide_gt, preferred_element_type=jnp.float32)
+    delta = jnp.sum(probs * prob_grad, axis=0, keepdims=True)
+    score_grad = (factor * probs * (prob_grad - delta)).astype(jnp.bfloat16)
+    prob_round = probs.astype(jnp.bfloat16)
+
+    wide = lax.dot_general(score_grad, keys, TN, preferred_element_type=jnp.float32)
+    wide = jnp.where(own_head, wide, 0.0)
+    total = sum(wide[head * latents : (head + 1) * latents] for head in range(heads))
+    qg_all[...] = total.reshape(qg_all.shape)
+    pair = qg_all[me // 2]
+    mine = jnp.where(me % 2 == 0, pair[:lat_dev], pair[lat_dev:])
+    qg_ref[...] = mine.astype(jnp.bfloat16)
+
+    for slot in range(first_block):
+        own_probs[slot] = jnp.zeros((events_dev, lanes), jnp.bfloat16)
+        own_scores[slot] = jnp.zeros((events_dev, lanes), jnp.bfloat16)
+    for slot in used:
+        place = (slot - first_block) * events_dev
+        own_probs[slot] = prob_round[place : place + events_dev]
+        own_scores[slot] = score_grad[place : place + events_dev]
+    kg_ref[...] = jnp.dot(own_scores[me], wide_q, preferred_element_type=jnp.float32).astype(
+        jnp.bfloat16
+    )
+    vg_ref[...] = jnp.dot(own_probs[me], wide_g, preferred_element_type=jnp.float32).astype(
+        jnp.bfloat16
+    )
+
+
+def swap(array, bit):
+    count = lax.axis_size("ctx")
+    return lax.ppermute(array, "ctx", [(index, index ^ bit) for index in range(count)])
+
+
+def swap_hd(array, bit):
+    ctx, hd = lax.axis_size("ctx"), lax.axis_size("hd")
+    pairs = [
+        (c * hd + z, (c ^ 1) * hd + (z ^ bit)) for c in range(ctx) for z in range(hd)
+    ]
+    return lax.ppermute(array, ("ctx", "hd"), pairs)
+
+
+def gathered(array, bits):
+    pieces = [(0, array)]
+    for bit in bits:
+        pieces += [(offset ^ bit, swap(piece, bit)) for offset, piece in pieces]
+    return pieces
+
+
+def per_device_packed(
+    cot, resid, norm_gain, w_in, w_out, w_proj, queries, keys, values, latent_pos, seg_start
+):
+    ctx, hd = lax.axis_size("ctx"), lax.axis_size("hd")
+    lat_dev, width = cot.shape
+    latents = lat_dev * ctx
+    events_dev, features = keys.shape
+    vmem, anywhere = pl.BlockSpec(memory_space=pltpu.VMEM), pl.BlockSpec(memory_space=pl.ANY)
+    smem = pl.BlockSpec(memory_space=pltpu.SMEM)
+    gain = norm_gain.reshape(1, width)
+    cot_other, resid_other = swap(cot, 1), swap(resid, 1)
+
+    pack_rows = 2 * events_dev + w_proj.shape[0] // 2 + Q_ROWS
+    pack = pl.pallas_call(
+        pack_kernel,
+        out_shape=jax.ShapeDtypeStruct((pack_rows, features), jnp.bfloat16),
+        in_specs=[vmem] * 4,
+        out_specs=vmem,
+        name="pack",
+    )(keys, values, w_proj, queries)
+    chip_bits = [1 << shift for shift in range(1, ctx.bit_length() - 1)]
+    packs = gathered(pack, [bit | 1 for bit in chip_bits])
+    packs = packs + [(offset ^ 1, swap(piece, 1)) for offset, piece in packs]
+
+    part = pl.pallas_call(
+        mlp_kernel,
+        out_shape=jax.ShapeDtypeStruct((2 * lat_dev, width), jnp.float32),
+        in_specs=[vmem] * 7,
+        out_specs=vmem,
+        name="mlp",
+    )(cot, cot_other, resid, resid_other, gain, w_in, w_out)
+    hd_bits = [1 << shift for shift in range(hd.bit_length() - 1)]
+    for bit in hd_bits[:-1]:
+        part = part + swap_hd(part, bit)
+    arrived = swap_hd(part, hd_bits[-1])
+    rows = pl.pallas_call(
+        resid_kernel,
+        out_shape=jax.ShapeDtypeStruct((2 * lat_dev, width), jnp.bfloat16),
+        in_specs=[vmem] * 7,
+        out_specs=vmem,
+        name="resid",
+    )(part, arrived, cot, cot_other, resid, resid_other, gain)
+    row_pieces = gathered(rows, [bit | 1 for bit in chip_bits])
+
+    first_event = max(0, events_dev * ctx // 2 - WINDOW)
+    lanes = features // HDIM * latents
+    kernel = functools.partial(
+        attention_kernel,
+        [offset >> 1 for offset, _ in row_pieces],
+        [offset for offset, _ in packs],
+        latents,
+        lat_dev,
+        events_dev,
+        first_event // events_dev,
+    )
+    return pl.pallas_call(
+        kernel,
+        out_shape=(
+            jax.ShapeDtypeStruct((lat_dev, features), jnp.bfloat16),
+            jax.ShapeDtypeStruct((events_dev, features), jnp.bfloat16),
+            jax.ShapeDtypeStruct((events_dev, features), jnp.bfloat16),
+        ),
+        in_specs=[smem] * 2 + [vmem] * len(row_pieces) + [anywhere] * len(packs),
+        out_specs=(vmem,) * 3,
+        scratch_shapes=[
+            pltpu.VMEM((ctx, pack_rows, features), jnp.bfloat16),
+            pltpu.VMEM((ctx // 2, 2 * lat_dev, width), jnp.float32),
+            pltpu.VMEM((ctx // 2, 2 * lat_dev, features), jnp.float32),
+            pltpu.VMEM((ctx, events_dev, lanes), jnp.bfloat16),
+            pltpu.VMEM((ctx, events_dev, lanes), jnp.bfloat16),
+            pltpu.SemaphoreType.DMA((len(packs),)),
+        ],
+        compiler_params=pltpu.CompilerParams(vmem_limit_bytes=32 * 1024 * 1024),
+        name="attention",
+    )(
+        latent_pos,
+        seg_start,
+        *[piece for _, piece in row_pieces],
+        *[piece for _, piece in packs],
+    )
+
+
 def solution(mesh):
     in_specs = (
         P("ctx", None),
@@ -162,6 +421,17 @@
         P(),
     )
     out_specs = (P("ctx", "hd"), P("ctx", "hd"), P("ctx", "hd"))
+    ctx, hd = mesh.shape["ctx"], mesh.shape["hd"]
+
+    def per_device(*arrays):
+        lat_dev, features = arrays[6].shape
+        fits = ctx * arrays[7].size * arrays[7].dtype.itemsize <= 2 * 1024 * 1024
+        powers = ctx >= 4 and hd >= 2 and ctx & (ctx - 1) == 0 and hd & (hd - 1) == 0
+        aligned = 2 * lat_dev == 8 and features % HDIM == 0 and lat_dev <= Q_ROWS
+        if fits and powers and aligned:
+            return per_device_packed(*arrays)
+        return per_device_streamed(*arrays)
+
     return jax.shard_map(
         per_device, mesh=mesh, in_specs=in_specs, out_specs=out_specs, check_vma=False
     )

time: 110 us -> 57.9 us (0.53)
  blocking collectives: 96.6 us -> 0 us
  waiting for transfers between devices: 0 us -> 24 us
  starting transfers between devices: 0 us -> 17.3 us
  Pallas kernels: 0 us -> 11.5 us
  matrix products: 5.33 us -> 0 us
  other arithmetic: 2.38 us -> 0.76 us
    all_gather x6 -> x0, blocking collectives: 52.5 us -> none  [the longest x3 25.7 us: joined(): pieces = jax.tree.map(lambda part: lax.all_gather(part, axis), value)]
    ppermute x0 -> x14, waiting for transfers between devices: none -> 24 us  [the longest x12 20.4 us: swap(): lax.ppermute(array, 'ctx', [(index, index ^ bit) for index in range(count)])]
    unnamed x1 -> x0, blocking collectives: 23.6 us -> none
    psum x1 -> x0, blocking collectives: 20.5 us -> none  [per_device(): normed_grad = lax.psum(partial_grad, 'hd')]
    ppermute x0 -> x14, starting transfers between devices: none -> 17.3 us  [the longest x12 12.7 us: swap(): lax.ppermute(array, 'ctx', [(index, index ^ bit) for index in range(count)])]
    pallas_call x0 -> x4, Pallas kernels: none -> 11.5 us  [the longest x1 4.46 us: per_device_packed(): pl.pallas_call(mlp_kernel, out_shape=jax.ShapeDtypeStruct((2 * lat_dev, w...]
    dot_general x8 -> x0, matrix products: 5.33 us -> none  [the longest x1 2.89 us: per_device(): lax.dot_general(pre_grad, w_in, contract_last, preferred_element_type=jnp...]
    convert_element_type x1 -> x0, local copies, waits for them, and re-layouts: 1.27 us -> none  [per_device(): query_grad = query_parts.reshape(lat_dev, features).astype(jnp.bfloat16)]
  transfers between devices with their start and end apart: 0 -> 14, of which waited for: 0 -> 8; matrix products, arithmetic and copies ran while one was open for 0% -> 4% of each run, Pallas kernels for 0% -> 11%
where the time goes in v1:
time: 57.9 us; the launch traced here: 57.5 us
  waiting for transfers between devices  24 us (41%)
  starting transfers between devices  17.3 us (30%)
  Pallas kernels  11.5 us (20%)
  local copies, waits for them, and re-layouts  3.19 us (6%)
  other arithmetic  0.76 us (1%)
  between operations  0.71 us (1%)
    ppermute x12, waiting for transfers between devices, swap(): lax.ppermute(array, 'ctx', [(index, index ^ bit) for index in range(count)])  20.4 us
    ppermute x12, starting transfers between devices, swap(): lax.ppermute(array, 'ctx', [(index, index ^ bit) for index in range(count)])  12.7 us
    ppermute x2, starting transfers between devices, swap_hd(): return lax.ppermute(array, ('ctx', 'hd'), pairs)  4.64 us
    pallas_call x1, Pallas kernels, per_device_packed(): pl.pallas_call(mlp_kernel, out_shape=jax.ShapeDtypeStruct((2 * lat_dev, w...  4.46 us
    pallas_call x1, Pallas kernels, per_device_packed(): pl.pallas_call(kernel, out_shape=(jax.ShapeDtypeStruct((lat_dev, features...  3.74 us
    ppermute x2, waiting for transfers between devices, swap_hd(): return lax.ppermute(array, ('ctx', 'hd'), pairs)  3.52 us
    unnamed x16, local copies, waits for them, and re-layouts  1.93 us
    pallas_call x1, Pallas kernels, per_device_packed(): pl.pallas_call(pack_kernel, out_shape=jax.ShapeDtypeStruct((pack_rows, fe...  1.74 us
  transfers between devices with their start and end apart: 14, of which 8 were waited for; matrix products, arithmetic and copies ran while one was open for 4% of the time, Pallas kernels for 11%

profile of v1, /device:TPU:0, one launch (start us, length us, event | category | flops | bytes accessed | tf_op | source)
XLA Modules:
  0.0 57.5 jit_solution(5315901823517443499)
XLA Ops:
  0.6 1.7 %pack.1.refs_6_ = bf16[656,256]{1,0:T(8,128)(2,1)} custom-call(bf16[256,256]{1,0:T(8,128)(2,1)} %k_ref.1, bf16[256,256]{1,0:T(8,128)(2,1)} %v_ref.1, bf16[256,128]{1,0:T(8,128)(2,1)} %w_ref.1, bf16[4,256]{1,0:T(4,128)(2,1)} %q_ref.1), custom_call_target="tpu_custom_call" | custom-call | tf_op jit(solution)/shard_map/pack/pallas_call | solution.py:340
  2.4 2.4 %collective-permute-start.7 = (bf16[656,256]{1,0:T(8,128)(2,1)}, bf16[656,256]{1,0:T(8,128)(2,1)S(1)}, u32[]{:S(2)}, u32[]{:S(2)}) collective-permute-start(bf16[656,256]{1,0:T(8,128)(2,1)} %pack.1.refs_6_), channel_id=1, source_target_pairs={{0,12},{4,8},{8,4},{12,0},{16,28},{20,24},{24,20},{28,16},{1,13},{... | collective-permute-start | bytes 1007624 | tf_op jit(solution)/shard_map/ppermute | solution.py:309
  4.7 1.8 %collective-permute-start.8 = (bf16[656,256]{1,0:T(8,128)(2,1)}, bf16[656,256]{1,0:T(8,128)(2,1)S(1)}, u32[]{:S(2)}, u32[]{:S(2)}) collective-permute-start(bf16[656,256]{1,0:T(8,128)(2,1)} %pack.1.refs_6_), channel_id=1, source_target_pairs={{0,20},{4,16},{8,28},{12,24},{16,4},{20,0},{24,12},{28,8},{1,21},{... | collective-permute-start | bytes 1007624 | tf_op jit(solution)/shard_map/ppermute | solution.py:309
  6.5 6.8 %collective-permute-done.7.refs_7_ = bf16[656,256]{1,0:T(8,128)(2,1)S(1)} collective-permute-done((bf16[656,256]{1,0:T(8,128)(2,1)}, bf16[656,256]{1,0:T(8,128)(2,1)S(1)}, u32[]{:S(2)}, u32[]{:S(2)}) %collective-permute-start.7) | collective-permute-done | bytes 335904 | tf_op jit(solution)/shard_map/ppermute | solution.py:309
  13.3 2.1 %collective-permute-start.9 = (bf16[656,256]{1,0:T(8,128)(2,1)S(1)}, bf16[656,256]{1,0:T(8,128)(2,1)S(1)}, u32[]{:S(2)}, u32[]{:S(2)}) collective-permute-start(bf16[656,256]{1,0:T(8,128)(2,1)S(1)} %collective-permute-done.7.refs_7_), channel_id=1, source_target_pairs={{0,20},{4,16},{8,28},{12,24},{16,4},{20,0},{24,12},{28,8},{1,21},{... | collective-permute-start | bytes 1007624 | tf_op jit(solution)/shard_map/ppermute | solution.py:309
  16.3 7.1 %collective-permute-done.9.refs_9_ = bf16[656,256]{1,0:T(8,128)(2,1)S(1)} collective-permute-done((bf16[656,256]{1,0:T(8,128)(2,1)S(1)}, bf16[656,256]{1,0:T(8,128)(2,1)S(1)}, u32[]{:S(2)}, u32[]{:S(2)}) %collective-permute-start.9) | collective-permute-done | bytes 335904 | tf_op jit(solution)/shard_map/ppermute | solution.py:309
  23.9 1.4 %collective-permute-done.cot_other = bf16[4,1024]{1,0:T(4,128)(2,1)S(1)} collective-permute-done((bf16[4,1024]{1,0:T(4,128)(2,1)}, bf16[4,1024]{1,0:T(4,128)(2,1)S(1)}, u32[]{:S(2)}, u32[]{:S(2)}) %collective-permute-start) | collective-permute-done | bytes 8224 | tf_op jit(solution)/shard_map/ppermute | solution.py:309
  25.6 1.3 %reshape.9.gain_ref = bf16[1,1024]{1,0:T(2,128)(2,1)} reshape(bf16[1024]{0:T(1024)(128)(2,1)} %param.13) | data formatting | bytes 4096 | tf_op jit(solution)/shard_map/reshape | solution.py:336
  27.5 4.5 %mlp.1 = f32[8,1024]{1,0:T(8,128)} custom-call(bf16[4,1024]{1,0:T(4,128)(2,1)} %cot_ref.3, bf16[4,1024]{1,0:T(4,128)(2,1)} %copy-done.5, bf16[4,1024]{1,0:T(4,128)(2,1)} %resid_ref.3, bf16[4,1024]{1,0:T(4,128)(2,1)} %copy-done.6, bf16[1,1024]{1,0:T(2,128)(2,1)} %reshape.9.gain_ref, bf16[1024,1024]{1,0:T(8,128)(2,1)} %w_in_ref.1, bf16[1024,1024]{1,0:T(8,128)(2,1)} %w_out_ref.1), custom_call_target="tpu_custom_call" | custom-call | tf_op jit(solution)/shard_map/mlp/pallas_call | solution.py:351
  31.9 2.0 %collective-permute-start.2 = (f32[8,1024]{1,0:T(8,128)}, f32[8,1024]{1,0:T(8,128)S(1)}, u32[]{:S(2)}, u32[]{:S(2)}) collective-permute-start(f32[8,1024]{1,0:T(8,128)} %mlp.1), channel_id=1, source_target_pairs={{0,5},{1,4},{2,7},{3,6},{4,1},{5,0},{6,3},{7,2},{8,13},{9,12},{10,... | collective-permute-start | bytes 98312 | tf_op jit(solution)/shard_map/ppermute | solution.py:317
  33.9 1.9 %collective-permute-done.2 = f32[8,1024]{1,0:T(8,128)S(1)} collective-permute-done((f32[8,1024]{1,0:T(8,128)}, f32[8,1024]{1,0:T(8,128)S(1)}, u32[]{:S(2)}, u32[]{:S(2)}) %collective-permute-start.2) | collective-permute-done | bytes 32800 | tf_op jit(solution)/shard_map/ppermute | solution.py:317
  35.8 0.8 %add.3.part_ref = f32[8,1024]{1,0:T(8,128)S(1)} add(f32[8,1024]{1,0:T(8,128)} %mlp.1, f32[8,1024]{1,0:T(8,128)S(1)} %collective-permute-done.2) | non-fusion elementwise | flops 8192 | bytes 98304 | tf_op jit(solution)/shard_map/add | solution.py:360
  36.6 2.6 %collective-permute-start.3 = (f32[8,1024]{1,0:T(8,128)S(1)}, f32[8,1024]{1,0:T(8,128)S(1)}, u32[]{:S(2)}, u32[]{:S(2)}) collective-permute-start(f32[8,1024]{1,0:T(8,128)S(1)} %add.3.part_ref), channel_id=1, source_target_pairs={{0,6},{1,7},{2,4},{3,5},{4,2},{5,3},{6,0},{7,1},{8,14},{9,15},{10,... | collective-permute-start | bytes 98312 | tf_op jit(solution)/shard_map/ppermute | solution.py:317
  39.2 1.6 %collective-permute-done.3.arrived_ref = f32[8,1024]{1,0:T(8,128)S(1)} collective-permute-done((f32[8,1024]{1,0:T(8,128)S(1)}, f32[8,1024]{1,0:T(8,128)S(1)}, u32[]{:S(2)}, u32[]{:S(2)}) %collective-permute-start.3) | collective-permute-done | bytes 32800 | tf_op jit(solution)/shard_map/ppermute | solution.py:317
  40.8 0.6 %copy-done.7 = f32[8,1024]{1,0:T(8,128)} copy-done((f32[8,1024]{1,0:T(8,128)}, f32[8,1024]{1,0:T(8,128)S(1)}, u32[]{:S(2)}) %copy-start.7) | copy-done | bytes 32792
  41.5 1.6 %resid.1.refs_2_ = bf16[8,1024]{1,0:T(8,128)(2,1)} custom-call(f32[8,1024]{1,0:T(8,128)} %copy-done.4, f32[8,1024]{1,0:T(8,128)} %copy-done.7, bf16[4,1024]{1,0:T(4,128)(2,1)} %cot_ref.3, bf16[4,1024]{1,0:T(4,128)(2,1)} %copy-done.5, bf16[4,1024]{1,0:T(4,128)(2,1)} %resid_ref.3, bf16[4,1024]{1,0:T(4,128)(2,1)} %copy-done.6, bf16[1,1024]{1,0:T(2,128)(2,1)} %reshape.9.gain_ref), custom_call_target="tpu_custom_call" | custom-call | tf_op jit(solution)/shard_map/resid/pallas_call | solution.py:362
  43.1 1.6 %collective-permute-start.5 = (bf16[8,1024]{1,0:T(8,128)(2,1)}, bf16[8,1024]{1,0:T(8,128)(2,1)S(1)}, u32[]{:S(2)}, u32[]{:S(2)}) collective-permute-start(bf16[8,1024]{1,0:T(8,128)(2,1)} %resid.1.refs_2_), channel_id=1, source_target_pairs={{0,20},{4,16},{8,28},{12,24},{16,4},{20,0},{24,12},{28,8},{1,21},{... | collective-permute-start | bytes 49160 | tf_op jit(solution)/shard_map/ppermute | solution.py:309
  44.6 1.8 %collective-permute-done.5.refs_4_ = bf16[8,1024]{1,0:T(8,128)(2,1)S(1)} collective-permute-done((bf16[8,1024]{1,0:T(8,128)(2,1)}, bf16[8,1024]{1,0:T(8,128)(2,1)S(1)}, u32[]{:S(2)}, u32[]{:S(2)}) %collective-permute-start.5) | collective-permute-done | bytes 16416 | tf_op jit(solution)/shard_map/ppermute | solution.py:309
  46.4 1.6 %collective-permute-start.4 = (bf16[8,1024]{1,0:T(8,128)(2,1)}, bf16[8,1024]{1,0:T(8,128)(2,1)S(1)}, u32[]{:S(2)}, u32[]{:S(2)}) collective-permute-start(bf16[8,1024]{1,0:T(8,128)(2,1)} %resid.1.refs_2_), channel_id=1, source_target_pairs={{0,12},{4,8},{8,4},{12,0},{16,28},{20,24},{24,20},{28,16},{1,13},{... | collective-permute-start | bytes 49160 | tf_op jit(solution)/shard_map/ppermute | solution.py:309
  48.0 1.8 %collective-permute-done.4.refs_3_ = bf16[8,1024]{1,0:T(8,128)(2,1)S(1)} collective-permute-done((bf16[8,1024]{1,0:T(8,128)(2,1)}, bf16[8,1024]{1,0:T(8,128)(2,1)S(1)}, u32[]{:S(2)}, u32[]{:S(2)}) %collective-permute-start.4) | collective-permute-done | bytes 16416 | tf_op jit(solution)/shard_map/ppermute | solution.py:309
  49.8 1.6 %collective-permute-start.6 = (bf16[8,1024]{1,0:T(8,128)(2,1)S(1)}, bf16[8,1024]{1,0:T(8,128)(2,1)S(1)}, u32[]{:S(2)}, u32[]{:S(2)}) collective-permute-start(bf16[8,1024]{1,0:T(8,128)(2,1)S(1)} %collective-permute-done.4.refs_3_), channel_id=1, source_target_pairs={{0,20},{4,16},{8,28},{12,24},{16,4},{20,0},{24,12},{28,8},{1,21},{... | collective-permute-start | bytes 49160 | tf_op jit(solution)/shard_map/ppermute | solution.py:309
  51.4 1.6 %collective-permute-done.6.refs_5_ = bf16[8,1024]{1,0:T(8,128)(2,1)S(1)} collective-permute-done((bf16[8,1024]{1,0:T(8,128)(2,1)S(1)}, bf16[8,1024]{1,0:T(8,128)(2,1)S(1)}, u32[]{:S(2)}, u32[]{:S(2)}) %collective-permute-start.6) | collective-permute-done | bytes 16416 | tf_op jit(solution)/shard_map/ppermute | solution.py:309
  53.1 0.7 %copy-done.1 = bf16[8,1024]{1,0:T(8,128)(2,1)S(1)} copy-done((bf16[8,1024]{1,0:T(8,128)(2,1)S(1)}, bf16[8,1024]{1,0:T(8,128)(2,1)}, u32[]{:S(2)}) %copy-start.1) | copy-done | bytes 16408
  53.8 3.7 %attention.1 = (bf16[4,256]{1,0:T(4,128)(2,1)}, bf16[256,256]{1,0:T(8,128)(2,1)}, bf16[256,256]{1,0:T(8,128)(2,1)}) custom-call(s32[32]{0:T(128)S(1)} %copy-done.2, s32[32]{0:T(128)S(1)} %copy-done.3, bf16[8,1024]{1,0:T(8,128)(2,1)S(1)} %copy-done.1, bf16[8,1024]{1,0:T(8,128)(2,1)S(1)} %collective-permute-done.4.refs_3_, ...), custom_call_target="tpu_custom_call" | custom-call | tf_op jit(solution)/shard_map/attention/pallas_call | solution.py:382
  (26 shorter events, 2.3 us)
Async XLA Ops:
  2.4 11.0 %collective-permute-start.7 = (bf16[656,256]{1,0:T(8,128)(2,1)}, bf16[656,256]{1,0:T(8,128)(2,1)S(1)}, u32[]{:S(2)}, u32[]{:S(2)}) collective-permute-start(bf16[656,256]{1,0:T(8,128)(2,1)} %pack.1.refs_6_), channel_id=1, source_target_pairs={{0,12},{4,8},{8,4},{12,0},{16,28},{20,24},{24,20},{28,16},{1,13},{... | collective-permute-start | bytes 1007624 | tf_op jit(solution)/shard_map/ppermute | solution.py:309
  4.7 11.2 %collective-permute-start.8 = (bf16[656,256]{1,0:T(8,128)(2,1)}, bf16[656,256]{1,0:T(8,128)(2,1)S(1)}, u32[]{:S(2)}, u32[]{:S(2)}) collective-permute-start(bf16[656,256]{1,0:T(8,128)(2,1)} %pack.1.refs_6_), channel_id=1, source_target_pairs={{0,20},{4,16},{8,28},{12,24},{16,4},{20,0},{24,12},{28,8},{1,21},{... | collective-permute-start | bytes 1007624 | tf_op jit(solution)/shard_map/ppermute | solution.py:309
  13.3 10.1 %collective-permute-start.9 = (bf16[656,256]{1,0:T(8,128)(2,1)S(1)}, bf16[656,256]{1,0:T(8,128)(2,1)S(1)}, u32[]{:S(2)}, u32[]{:S(2)}) collective-permute-start(bf16[656,256]{1,0:T(8,128)(2,1)S(1)} %collective-permute-done.7.refs_7_), channel_id=1, source_target_pairs={{0,20},{4,16},{8,28},{12,24},{16,4},{20,0},{24,12},{28,8},{1,21},{... | collective-permute-start | bytes 1007624 | tf_op jit(solution)/shard_map/ppermute | solution.py:309
  15.5 37.5 %collective-permute-start.10 = (bf16[656,256]{1,0:T(8,128)(2,1)}, bf16[656,256]{1,0:T(8,128)(2,1)S(1)}, u32[]{:S(2)}, u32[]{:S(2)}) collective-permute-start(bf16[656,256]{1,0:T(8,128)(2,1)} %pack.1.refs_6_), channel_id=1, source_target_pairs={{0,4},{4,0},{8,12},{12,8},{16,20},{20,16},{24,28},{28,24},{1,5},{5... | collective-permute-start | bytes 1007624 | tf_op jit(solution)/shard_map/ppermute | solution.py:309
  15.8 37.2 %collective-permute-start.11 = (bf16[656,256]{1,0:T(8,128)(2,1)S(1)}, bf16[656,256]{1,0:T(8,128)(2,1)S(1)}, u32[]{:S(2)}, u32[]{:S(2)}) collective-permute-start(bf16[656,256]{1,0:T(8,128)(2,1)S(1)} %collective-permute-done.7.refs_7_), channel_id=1, source_target_pairs={{0,4},{4,0},{8,12},{12,8},{16,20},{20,16},{24,28},{28,24},{1,5},{5... | collective-permute-start | bytes 1007624 | tf_op jit(solution)/shard_map/ppermute | solution.py:309
  16.0 37.0 %collective-permute-start.12 = (bf16[656,256]{1,0:T(8,128)(2,1)S(1)}, bf16[656,256]{1,0:T(8,128)(2,1)S(1)}, u32[]{:S(2)}, u32[]{:S(2)}) collective-permute-start(bf16[656,256]{1,0:T(8,128)(2,1)S(1)} %collective-permute-done.8.refs_8_), channel_id=1, source_target_pairs={{0,4},{4,0},{8,12},{12,8},{16,20},{20,16},{24,28},{28,24},{1,5},{5... | collective-permute-start | bytes 1007624 | tf_op jit(solution)/shard_map/ppermute | solution.py:309
  23.4 29.6 %collective-permute-start.13 = (bf16[656,256]{1,0:T(8,128)(2,1)S(1)}, bf16[656,256]{1,0:T(8,128)(2,1)S(1)}, u32[]{:S(2)}, u32[]{:S(2)}) collective-permute-start(bf16[656,256]{1,0:T(8,128)(2,1)S(1)} %collective-permute-done.9.refs_9_), channel_id=1, source_target_pairs={{0,4},{4,0},{8,12},{12,8},{16,20},{20,16},{24,28},{28,24},{1,5},{5... | collective-permute-start | bytes 1007624 | tf_op jit(solution)/shard_map/ppermute | solution.py:309
  23.7 1.6 %collective-permute-start = (bf16[4,1024]{1,0:T(4,128)(2,1)}, bf16[4,1024]{1,0:T(4,128)(2,1)S(1)}, u32[]{:S(2)}, u32[]{:S(2)}) collective-permute-start(bf16[4,1024]{1,0:T(4,128)(2,1)} %cot_ref.3), channel_id=1, source_target_pairs={{0,4},{4,0},{8,12},{12,8},{16,20},{20,16},{24,28},{28,24},{1,5},{5... | collective-permute-start | bytes 24584 | tf_op jit(solution)/shard_map/ppermute | solution.py:309
  25.3 1.6 %copy-start.5 = (bf16[4,1024]{1,0:T(4,128)(2,1)}, bf16[4,1024]{1,0:T(4,128)(2,1)S(1)}, u32[]{:S(2)}) copy-start(bf16[4,1024]{1,0:T(4,128)(2,1)S(1)} %collective-permute-done.cot_other) | copy-start | bytes 24580
  25.3 1.6 %collective-permute-start.1 = (bf16[4,1024]{1,0:T(4,128)(2,1)}, bf16[4,1024]{1,0:T(4,128)(2,1)S(1)}, u32[]{:S(2)}, u32[]{:S(2)}) collective-permute-start(bf16[4,1024]{1,0:T(4,128)(2,1)} %resid_ref.3), channel_id=1, source_target_pairs={{0,4},{4,0},{8,12},{12,8},{16,20},{20,16},{24,28},{28,24},{1,5},{5... | collective-permute-start | bytes 24584 | tf_op jit(solution)/shard_map/ppermute | solution.py:309
  26.8 26.2 %copy-start = (bf16[656,256]{1,0:T(8,128)(2,1)S(1)}, bf16[656,256]{1,0:T(8,128)(2,1)}, u32[]{:S(2)}) copy-start(bf16[656,256]{1,0:T(8,128)(2,1)} %pack.1.refs_6_) | copy-start | bytes 1007620
  26.8 26.2 %copy-start.2 = (s32[32]{0:T(128)S(1)}, s32[32]{0:T(128)}, u32[]{:S(2)}) copy-start(s32[32]{0:T(128)} %refs_0_.1) | copy-start | bytes 388
  26.8 26.2 %copy-start.3 = (s32[32]{0:T(128)S(1)}, s32[32]{0:T(128)}, u32[]{:S(2)}) copy-start(s32[32]{0:T(128)} %refs_1_.1) | copy-start | bytes 388
  26.9 0.6 %copy-start.6 = (bf16[4,1024]{1,0:T(4,128)(2,1)}, bf16[4,1024]{1,0:T(4,128)(2,1)S(1)}, u32[]{:S(2)}) copy-start(bf16[4,1024]{1,0:T(4,128)(2,1)S(1)} %collective-permute-done.1.resid_other) | copy-start | bytes 24580
  31.9 3.9 %collective-permute-start.2 = (f32[8,1024]{1,0:T(8,128)}, f32[8,1024]{1,0:T(8,128)S(1)}, u32[]{:S(2)}, u32[]{:S(2)}) collective-permute-start(f32[8,1024]{1,0:T(8,128)} %mlp.1), channel_id=1, source_target_pairs={{0,5},{1,4},{2,7},{3,6},{4,1},{5,0},{6,3},{7,2},{8,13},{9,12},{10,... | collective-permute-start | bytes 98312 | tf_op jit(solution)/shard_map/ppermute | solution.py:317
  36.6 4.3 %copy-start.4 = (f32[8,1024]{1,0:T(8,128)}, f32[8,1024]{1,0:T(8,128)S(1)}, u32[]{:S(2)}) copy-start(f32[8,1024]{1,0:T(8,128)S(1)} %add.3.part_ref) | copy-start | bytes 98308
  36.6 4.3 %collective-permute-start.3 = (f32[8,1024]{1,0:T(8,128)S(1)}, f32[8,1024]{1,0:T(8,128)S(1)}, u32[]{:S(2)}, u32[]{:S(2)}) collective-permute-start(f32[8,1024]{1,0:T(8,128)S(1)} %add.3.part_ref), channel_id=1, source_target_pairs={{0,6},{1,7},{2,4},{3,5},{4,2},{5,3},{6,0},{7,1},{8,14},{9,15},{10,... | collective-permute-start | bytes 98312 | tf_op jit(solution)/shard_map/ppermute | solution.py:317
  40.8 0.6 %copy-start.7 = (f32[8,1024]{1,0:T(8,128)}, f32[8,1024]{1,0:T(8,128)S(1)}, u32[]{:S(2)}) copy-start(f32[8,1024]{1,0:T(8,128)S(1)} %collective-permute-done.3.arrived_ref) | copy-start | bytes 98308
  43.1 3.4 %collective-permute-start.5 = (bf16[8,1024]{1,0:T(8,128)(2,1)}, bf16[8,1024]{1,0:T(8,128)(2,1)S(1)}, u32[]{:S(2)}, u32[]{:S(2)}) collective-permute-start(bf16[8,1024]{1,0:T(8,128)(2,1)} %resid.1.refs_2_), channel_id=1, source_target_pairs={{0,20},{4,16},{8,28},{12,24},{16,4},{20,0},{24,12},{28,8},{1,21},{... | collective-permute-start | bytes 49160 | tf_op jit(solution)/shard_map/ppermute | solution.py:309
  46.4 3.4 %collective-permute-start.4 = (bf16[8,1024]{1,0:T(8,128)(2,1)}, bf16[8,1024]{1,0:T(8,128)(2,1)S(1)}, u32[]{:S(2)}, u32[]{:S(2)}) collective-permute-start(bf16[8,1024]{1,0:T(8,128)(2,1)} %resid.1.refs_2_), channel_id=1, source_target_pairs={{0,12},{4,8},{8,4},{12,0},{16,28},{20,24},{24,20},{28,16},{1,13},{... | collective-permute-start | bytes 49160 | tf_op jit(solution)/shard_map/ppermute | solution.py:309
  49.8 3.2 %collective-permute-start.6 = (bf16[8,1024]{1,0:T(8,128)(2,1)S(1)}, bf16[8,1024]{1,0:T(8,128)(2,1)S(1)}, u32[]{:S(2)}, u32[]{:S(2)}) collective-permute-start(bf16[8,1024]{1,0:T(8,128)(2,1)S(1)} %collective-permute-done.4.refs_3_), channel_id=1, source_target_pairs={{0,20},{4,16},{8,28},{12,24},{16,4},{20,0},{24,12},{28,8},{1,21},{... | collective-permute-start | bytes 49160 | tf_op jit(solution)/shard_map/ppermute | solution.py:309
  53.0 0.7 %copy-start.1 = (bf16[8,1024]{1,0:T(8,128)(2,1)S(1)}, bf16[8,1024]{1,0:T(8,128)(2,1)}, u32[]{:S(2)}) copy-start(bf16[8,1024]{1,0:T(8,128)(2,1)} %resid.1.refs_2_) | copy-start | bytes 49156

commit v2 on v0

--- a/solution.py
+++ b/solution.py
@@ -1,11 +1,15 @@
+import functools
 import math
 
 import jax
 import jax.numpy as jnp
 from jax import lax
+from jax.experimental import pallas as pl
+from jax.experimental.pallas import tpu as pltpu
 from jax.sharding import PartitionSpec as P
 
 HDIM = 64
+WINDOW = 256
 
 
 def joined(value, axis, join):
@@ -37,7 +41,7 @@
     )
 
 
-def per_device(
+def per_device_streamed(
     cot, resid, norm_gain, w_in, w_out, w_proj, queries, keys, values, latent_pos, seg_start
 ):
     contract_last = (((1,), (1,)), ((), ()))
@@ -147,6 +151,377 @@
     return (query_grad, key_grad, value_grad)
 
 
+NT = (((1,), (1,)), ((), ()))
+TN = (((0,), (0,)), ((), ()))
+Q_ROWS = 16
+MLP_PARTS = 4
+MLP_AHEAD = 2
+
+
+def load_kernel(
+    k_ref,
+    v_ref,
+    w_ref,
+    q_ref,
+    cot_ref,
+    resid_ref,
+    gain_ref,
+    pack_ref,
+    rows_ref,
+    q_own,
+    cot_own,
+    resid_own,
+    gain_own,
+    sems,
+):
+    events, half, cols = k_ref.shape[0], w_ref.shape[0] // 2, w_ref.shape[1]
+    base = 2 * events
+    moves = [
+        (q_ref, q_own),
+        (cot_ref, cot_own),
+        (resid_ref, resid_own),
+        (gain_ref, gain_own),
+        (k_ref, pack_ref.at[pl.ds(0, events)]),
+        (v_ref, pack_ref.at[pl.ds(events, events)]),
+        (w_ref.at[pl.ds(0, half)], pack_ref.at[pl.ds(base, half), pl.ds(0, cols)]),
+        (w_ref.at[pl.ds(half, half)], pack_ref.at[pl.ds(base, half), pl.ds(cols, cols)]),
+    ]
+    copies = [
+        pltpu.make_async_copy(source, target, sems.at[slot])
+        for slot, (source, target) in enumerate(moves)
+    ]
+    for copy in copies:
+        copy.start()
+    for copy in copies[:4]:
+        copy.wait()
+    rows = q_own[...].astype(jnp.float32)
+    spare = jnp.zeros((Q_ROWS - rows.shape[0], rows.shape[1]), jnp.float32)
+    pack_ref[base + half :, :] = jnp.concatenate([rows, spare], axis=0).astype(jnp.bfloat16)
+    gain = gain_own[...].astype(jnp.float32).reshape(1, gain_own.shape[0])
+    lat_dev = cot_own.shape[0]
+    held = [cot_own[...].astype(jnp.float32), resid_own[...].astype(jnp.float32)]
+    held += [jnp.broadcast_to(gain, (rows_ref.shape[0] - 2 * lat_dev, gain.shape[1]))]
+    rows_ref[...] = jnp.concatenate(held, axis=0).astype(jnp.bfloat16)
+    for copy in copies[4:]:
+        copy.wait()
+
+
+def chip_rows(own_ref, other_ref):
+    own, other = own_ref[...].astype(jnp.float32), other_ref[...].astype(jnp.float32)
+    first = lax.axis_index("ctx") % 2 == 0
+    low, high = jnp.where(first, own, other), jnp.where(first, other, own)
+    half = own.shape[0] // 4
+    cot = jnp.concatenate([low[:half], high[:half]], axis=0)
+    rows = jnp.concatenate([low[half : 2 * half], high[half : 2 * half]], axis=0)
+    return cot, rows, own[2 * half : 2 * half + 1]
+
+
+def rms_parts(rows):
+    inv_rms = lax.rsqrt(jnp.mean(rows * rows, axis=-1, keepdims=True) + 1e-05)
+    return inv_rms, rows * inv_rms
+
+
+def mlp_kernel(own_ref, other_ref, w_in_ref, w_out_ref, out_ref, w_in, w_out, sems):
+    parts, size = w_in.shape[0], w_in.shape[2]
+    copies = []
+    for part in range(parts):
+        span = pl.ds(part * size, size)
+        copies.append(
+            (
+                pltpu.make_async_copy(w_in_ref.at[:, span], w_in.at[part], sems.at[0, part]),
+                pltpu.make_async_copy(w_out_ref.at[span], w_out.at[part], sems.at[1, part]),
+            )
+        )
+
+    def begin(part):
+        if part < parts:
+            for copy in copies[part]:
+                copy.start()
+
+    for part in range(MLP_AHEAD):
+        begin(part)
+    cot, rows, gain = chip_rows(own_ref, other_ref)
+    cot = cot.astype(jnp.bfloat16)
+    normed = (rms_parts(rows)[1] * gain).astype(jnp.bfloat16)
+    total = jnp.zeros(out_ref.shape, jnp.float32)
+    for part in range(parts):
+        for copy in copies[part]:
+            copy.wait()
+        begin(part + MLP_AHEAD)
+        up = w_in[part]
+        pre_act = jnp.dot(normed, up, preferred_element_type=jnp.float32)
+        hidden_grad = lax.dot_general(cot, w_out[part], NT, preferred_element_type=jnp.float32)
+        pre_grad = (hidden_grad * gelu_slope(pre_act)).astype(jnp.bfloat16)
+        total += lax.dot_general(pre_grad, up, NT, preferred_element_type=jnp.float32)
+    out_ref[...] = total
+
+
+def resid_kernel(part_ref, arrived_ref, own_ref, other_ref, out_ref):
+    cot, rows, gain = chip_rows(own_ref, other_ref)
+    inv_rms, unit = rms_parts(rows)
+    weighted = (part_ref[...] + arrived_ref[...]) * gain
+    grad = cot + inv_rms * (weighted - unit * jnp.mean(weighted * unit, axis=-1, keepdims=True))
+    out_ref[...] = grad.astype(jnp.bfloat16)
+
+
+def wide_rows(array, latents):
+    features = array.shape[1]
+    heads = features // HDIM
+    shape = (heads * latents, features)
+    row_head = lax.broadcasted_iota(jnp.int32, shape, 0) // latents
+    own_head = row_head == lax.broadcasted_iota(jnp.int32, shape, 1) // HDIM
+    return jnp.where(own_head, jnp.concatenate([array] * heads, axis=0), 0.0), own_head
+
+
+def probs_kernel(offsets, latents, lat_dev, events_dev, first_block, *refs):
+    pos_ref, start_ref = refs[:2]
+    pack_refs = refs[2:-6]
+    probs_ref, keys_ref, values_ref, proj_ref, wide_ref, q_all = refs[-6:]
+    me = lax.axis_index("ctx")
+    even = me % 2 == 0
+    base = 2 * events_dev
+    pack_rows = base + proj_ref.shape[1] + Q_ROWS
+    places = []
+    for ref, pair in zip(pack_refs, offsets):
+        for slot, offset in enumerate(pair):
+            places.append((ref, slot * pack_rows, offset))
+    queries = {}
+    for ref, row, offset in places:
+        block = me ^ jnp.where(even, *offset)
+        proj_ref[block] = ref[row + base : row + base + proj_ref.shape[1], :]
+        queries[offset] = ref[row + pack_rows - Q_ROWS : row + pack_rows, :].astype(jnp.float32)
+
+        @pl.when(block >= first_block)
+        def _(ref=ref, row=row, block=block):
+            keys_ref[block - first_block] = ref[row : row + events_dev, :]
+            values_ref[block - first_block] = ref[row + events_dev : row + base, :]
+
+    for offset, own in queries.items():
+        if offset[0] % 2 == 0:
+            other = queries[(offset[0] ^ 1, offset[1] ^ 1)]
+            low, high = jnp.where(even, own, other), jnp.where(even, other, own)
+            chip = (me ^ jnp.where(even, *offset)) // 2
+            q_all[chip] = jnp.concatenate([low[:lat_dev], high[:lat_dev]], axis=0)
+    wide_q = wide_rows(q_all[...].reshape(latents, q_all.shape[2]), latents)[0]
+    wide_ref[...] = wide_q.astype(jnp.bfloat16)
+    wide_qt = wide_q.T.astype(jnp.bfloat16)
+    lanes = wide_qt.shape[1]
+
+    lane = lax.broadcasted_iota(jnp.int32, (1, lanes), 1) % latents
+    pos, start = jnp.zeros((1, lanes), jnp.int32), jnp.zeros((1, lanes), jnp.int32)
+    for latent in range(latents):
+        pos = jnp.where(lane == latent, pos_ref[latent], pos)
+        start = jnp.where(lane == latent, start_ref[latent], start)
+    used, features = keys_ref.shape[0], keys_ref.shape[2]
+    keys = keys_ref[...].reshape(used * events_dev, features)
+    spot = first_block * events_dev + lax.broadcasted_iota(jnp.int32, (keys.shape[0], lanes), 0)
+    visible = (spot >= start) & (spot <= pos)
+    scores = (1.0 / math.sqrt(HDIM)) * jnp.dot(keys, wide_qt, preferred_element_type=jnp.float32)
+    scores = jnp.where(visible, scores, -1e30)
+    top = jnp.max(scores, axis=0, keepdims=True)
+    expo = jnp.where(visible, jnp.exp(scores - top), 0.0)
+    probs = expo * (1.0 / jnp.sum(expo, axis=0, keepdims=True))
+    probs_ref[:first_block] = jnp.zeros((first_block, events_dev, lanes), jnp.float32)
+    probs_ref[first_block:] = probs.reshape(used, events_dev, lanes)
+
+
+def grads_kernel(
+    row_offsets,
+    latents,
+    first_block,
+    probs_ref,
+    keys_ref,
+    values_ref,
+    proj_ref,
+    wide_ref,
+    *refs,
+):
+    row_refs = refs[: len(row_offsets)]
+    qg_ref, kg_ref, vg_ref, rows_all, qg_all, scores_all = refs[len(row_offsets) :]
+    me = lax.axis_index("ctx")
+    lat_dev = qg_ref.shape[0]
+    blocks, events_dev, lanes = probs_ref.shape
+    used, features = keys_ref.shape[0], keys_ref.shape[2]
+    factor = 1.0 / math.sqrt(HDIM)
+    for offset, ref in zip(row_offsets, row_refs):
+        rows_all[(me // 2) ^ offset] = ref[...].astype(jnp.float32)
+    resid_grad = rows_all[...].reshape(latents, rows_all.shape[2]).astype(jnp.bfloat16)
+    cols = features // 2
+    upper = jnp.concatenate([proj_ref[block, :, :cols] for block in range(blocks)], axis=1)
+    lower = jnp.concatenate([proj_ref[block, :, cols:] for block in range(blocks)], axis=1)
+    out_grad = [
+        lax.dot_general(resid_grad, piece, NT, preferred_element_type=jnp.float32)
+        for piece in (upper, lower)
+    ]
+    out_grad = jnp.concatenate(out_grad, axis=1).astype(jnp.bfloat16).astype(jnp.float32)
+    wide_g, own_head = wide_rows(out_grad, latents)
+    wide_gt, wide_g = wide_g.T.astype(jnp.bfloat16), wide_g.astype(jnp.bfloat16)
+    keys = keys_ref[...].reshape(used * events_dev, features)
+    values = values_ref[...].reshape(used * events_dev, features)
+    probs = probs_ref[first_block:].reshape(used * events_dev, lanes)
+    prob_grad = jnp.dot(values, wide_gt, preferred_element_type=jnp.float32)
+    delta = jnp.sum(probs * prob_grad, axis=0, keepdims=True)
+    score_grad = (factor * probs * (prob_grad - delta)).astype(jnp.bfloat16)
+    scores_all[:first_block] = jnp.zeros((first_block, events_dev, lanes), jnp.bfloat16)
+    scores_all[first_block:] = score_grad.reshape(used, events_dev, lanes)
+
+    wide = lax.dot_general(score_grad, keys, TN, preferred_element_type=jnp.float32)
+    wide = jnp.where(own_head, wide, 0.0)
+    total = sum(wide[head * latents : (head + 1) * latents] for head in range(lanes // latents))
+    qg_all[...] = total.reshape(qg_all.shape)
+    pair = qg_all[me // 2]
+    mine = jnp.where(me % 2 == 0, pair[:lat_dev], pair[lat_dev:])
+    qg_ref[...] = mine.astype(jnp.bfloat16)
+    prob_round = probs_ref[me].astype(jnp.bfloat16)
+    vg_ref[...] = jnp.dot(prob_round, wide_g, preferred_element_type=jnp.float32).astype(
+        jnp.bfloat16
+    )
+    kg_ref[...] = jnp.dot(scores_all[me], wide_ref[...], preferred_element_type=jnp.float32).astype(
+        jnp.bfloat16
+    )
+
+
+def swap(array, bit, odd_bit=None):
+    bits = (bit, bit if odd_bit is None else odd_bit)
+    count = lax.axis_size("ctx")
+    return lax.ppermute(array, "ctx", [(index, index ^ bits[index % 2]) for index in range(count)])
+
+
+def swap_hd(array, bit):
+    ctx, hd = lax.axis_size("ctx"), lax.axis_size("hd")
+    pairs = [
+        (c * hd + z, (c ^ 1) * hd + (z ^ bit)) for c in range(ctx) for z in range(hd)
+    ]
+    return lax.ppermute(array, ("ctx", "hd"), pairs)
+
+
+def after(array, *others):
+    return lax.optimization_barrier((array, *others))[0]
+
+
+def in_hbm(array):
+    return pltpu.with_memory_space_constraint(array, pltpu.HBM)
+
+
+def params(mebibytes):
+    return pltpu.CompilerParams(vmem_limit_bytes=mebibytes * 1024 * 1024)
+
+
+def per_device_packed(
+    cot, resid, norm_gain, w_in, w_out, w_proj, queries, keys, values, latent_pos, seg_start
+):
+    ctx, hd = lax.axis_size("ctx"), lax.axis_size("hd")
+    lat_dev, width = cot.shape
+    latents = lat_dev * ctx
+    events_dev, features = keys.shape
+    hidden = w_in.shape[1]
+    vmem = pl.BlockSpec(memory_space=pltpu.VMEM)
+    smem = pl.BlockSpec(memory_space=pltpu.SMEM)
+    hbm = pl.BlockSpec(memory_space=pltpu.HBM)
+    pack_rows = 2 * events_dev + w_proj.shape[0] // 2 + Q_ROWS
+    pack, own_rows = pl.pallas_call(
+        load_kernel,
+        out_shape=(
+            jax.ShapeDtypeStruct((pack_rows, features), jnp.bfloat16),
+            jax.ShapeDtypeStruct((4 * lat_dev, width), jnp.bfloat16),
+        ),
+        in_specs=[hbm] * 7,
+        out_specs=(vmem,) * 2,
+        scratch_shapes=[
+            pltpu.VMEM((lat_dev, features), jnp.bfloat16),
+            pltpu.VMEM((lat_dev, width), jnp.bfloat16),
+            pltpu.VMEM((lat_dev, width), jnp.bfloat16),
+            pltpu.VMEM((width,), jnp.bfloat16),
+            pltpu.SemaphoreType.DMA((8,)),
+        ],
+        compiler_params=params(8),
+        name="load",
+    )(*[in_hbm(array) for array in (keys, values, w_proj, queries, cot, resid, norm_gain)])
+    other_rows = swap(own_rows, 1)
+
+    chip_bits = [1 << shift for shift in range(1, ctx.bit_length() - 1)]
+    hd_bits = [1 << shift for shift in range(hd.bit_length() - 1)]
+    steps = (tuple(chip_bits), tuple(reversed(chip_bits)))
+    first_piece = swap(pack, *steps[0])
+    part = pl.pallas_call(
+        mlp_kernel,
+        out_shape=jax.ShapeDtypeStruct((2 * lat_dev, width), jnp.float32),
+        in_specs=[vmem] * 2 + [hbm] * 2,
+        out_specs=vmem,
+        scratch_shapes=[
+            pltpu.VMEM((MLP_PARTS, width, hidden // MLP_PARTS), jnp.bfloat16),
+            pltpu.VMEM((MLP_PARTS, hidden // MLP_PARTS, width), jnp.bfloat16),
+            pltpu.SemaphoreType.DMA((2, MLP_PARTS)),
+        ],
+        compiler_params=params(16),
+        cost_estimate=pl.CostEstimate(
+            flops=12 * lat_dev * w_in.size, bytes_accessed=4 * w_in.size, transcendentals=0
+        ),
+        name="mlp",
+    )(own_rows, other_rows, in_hbm(w_in), in_hbm(w_out))
+    first_pair = jnp.concatenate([pack, after(first_piece, part)], axis=0)
+    second_pair = swap(first_pair, *steps[1])
+    for bit in hd_bits[:-1]:
+        part = part + swap_hd(part, bit)
+    first_other = swap(after(first_pair, part), 1)
+    arrived = swap_hd(part, hd_bits[-1])
+    rows = pl.pallas_call(
+        resid_kernel,
+        out_shape=jax.ShapeDtypeStruct((2 * lat_dev, width), jnp.bfloat16),
+        in_specs=[vmem] * 4,
+        out_specs=vmem,
+        compiler_params=params(8),
+        name="resid",
+    )(part, arrived, own_rows, other_rows)
+    row_x, row_y = (swap(rows, bit | 1) for bit in chip_bits)
+    row_xy = swap(after(row_x, second_pair), chip_bits[1] | 1)
+    second_other = swap(after(second_pair, row_x), 1)
+
+    corner = tuple(step ^ other for step, other in zip(*steps))
+    turn = lambda pair: (pair[1] ^ 1, pair[0] ^ 1)
+    near, far = [(0, 0), steps[0]], [steps[1], corner]
+    offsets = [near, [turn(pair) for pair in near], far, [turn(pair) for pair in far]]
+    first_block = max(0, events_dev * ctx // 2 - WINDOW) // events_dev
+    lanes = features // HDIM * latents
+    probs, used_keys, used_values, proj, wide_q = pl.pallas_call(
+        functools.partial(probs_kernel, offsets, latents, lat_dev, events_dev, first_block),
+        out_shape=(
+            jax.ShapeDtypeStruct((ctx, events_dev, lanes), jnp.float32),
+            jax.ShapeDtypeStruct((ctx - first_block, events_dev, features), jnp.bfloat16),
+            jax.ShapeDtypeStruct((ctx - first_block, events_dev, features), jnp.bfloat16),
+            jax.ShapeDtypeStruct((ctx, w_proj.shape[0] // 2, features), jnp.bfloat16),
+            jax.ShapeDtypeStruct((lanes, features), jnp.bfloat16),
+        ),
+        in_specs=[smem] * 2 + [vmem] * 4,
+        out_specs=(vmem,) * 5,
+        scratch_shapes=[pltpu.VMEM((ctx // 2, 2 * lat_dev, features), jnp.float32)],
+        compiler_params=params(24),
+        cost_estimate=pl.CostEstimate(
+            flops=2 * ctx * keys.size * lanes, bytes_accessed=8 * keys.size, transcendentals=0
+        ),
+        name="probs",
+    )(latent_pos, seg_start, first_pair, first_other, second_pair, second_other)
+    return pl.pallas_call(
+        functools.partial(
+            grads_kernel, [0, *[bit // 2 for bit in chip_bits], sum(chip_bits) // 2], latents, first_block
+        ),
+        out_shape=(
+            jax.ShapeDtypeStruct((lat_dev, features), jnp.bfloat16),
+            jax.ShapeDtypeStruct((events_dev, features), jnp.bfloat16),
+            jax.ShapeDtypeStruct((events_dev, features), jnp.bfloat16),
+        ),
+        in_specs=[vmem] * 9,
+        out_specs=(vmem,) * 3,
+        scratch_shapes=[
+            pltpu.VMEM((ctx // 2, 2 * lat_dev, width), jnp.float32),
+            pltpu.VMEM((ctx // 2, 2 * lat_dev, features), jnp.float32),
+            pltpu.VMEM((ctx, events_dev, lanes), jnp.bfloat16),
+        ],
+        compiler_params=params(24),
+        name="grads",
+    )(probs, used_keys, used_values, proj, wide_q, rows, row_x, row_y, row_xy)
+
+
 def solution(mesh):
     in_specs = (
         P("ctx", None),
@@ -162,6 +537,17 @@
         P(),
     )
     out_specs = (P("ctx", "hd"), P("ctx", "hd"), P("ctx", "hd"))
+    ctx, hd = mesh.shape["ctx"], mesh.shape["hd"]
+
+    def per_device(*arrays):
+        lat_dev, features = arrays[6].shape
+        fits = ctx * arrays[7].size * arrays[7].dtype.itemsize <= 2 * 1024 * 1024
+        powers = ctx == 8 and hd >= 2 and ctx & (ctx - 1) == 0 and hd & (hd - 1) == 0
+        aligned = 2 * lat_dev == 8 and features % HDIM == 0 and lat_dev <= Q_ROWS
+        if fits and powers and aligned:
+            return per_device_packed(*arrays)
+        return per_device_streamed(*arrays)
+
     return jax.shard_map(
         per_device, mesh=mesh, in_specs=in_specs, out_specs=out_specs, check_vma=False
     )

time: 110 us -> 29.1 us (0.26)
  blocking collectives: 96.6 us -> 0 us
  starting transfers between devices: 0 us -> 11.1 us
  Pallas kernels: 0 us -> 9.08 us
  waiting for transfers between devices: 0 us -> 7.97 us
  matrix products: 5.33 us -> 0 us
  local copies, waits for them, and re-layouts: 4.08 us -> 0.06 us
  other arithmetic: 2.38 us -> 0.01 us
    all_gather x6 -> x0, blocking collectives: 52.5 us -> none  [the longest x3 25.7 us: joined(): pieces = jax.tree.map(lambda part: lax.all_gather(part, axis), value)]
    unnamed x1 -> x0, blocking collectives: 23.6 us -> none
    psum x1 -> x0, blocking collectives: 20.5 us -> none  [per_device(): normed_grad = lax.psum(partial_grad, 'hd')]
    ppermute x0 -> x10, starting transfers between devices: none -> 11.1 us  [the longest x8 8.39 us: swap(): lax.ppermute(array, 'ctx', [(index, index ^ bits[index % 2]) for index in...]
    pallas_call x0 -> x5, Pallas kernels: none -> 9.08 us  [the longest x1 4.25 us: per_device_packed(): pl.pallas_call(mlp_kernel, out_shape=jax.ShapeDtypeStruct((2 * lat_dev, w...]
    ppermute x0 -> x10, waiting for transfers between devices: none -> 7.97 us  [the longest x2 5.09 us: swap_hd(): return lax.ppermute(array, ('ctx', 'hd'), pairs)]
    dot_general x8 -> x0, matrix products: 5.33 us -> none  [the longest x1 2.89 us: per_device(): lax.dot_general(pre_grad, w_in, contract_last, preferred_element_type=jnp...]
    unnamed x25 -> x5, local copies, waits for them, and re-layouts: 2.44 us -> 0.04 us
  transfers between devices with their start and end apart: 0 -> 10, of which waited for: 0 -> 5; matrix products, arithmetic and copies ran while one was open for 0% -> 0% of each run, Pallas kernels for 0% -> 20%
where the time goes in v2:
time: 29.1 us; the launch traced here: 28.9 us
  starting transfers between devices  11.1 us (38%)
  Pallas kernels  9.08 us (31%)
  waiting for transfers between devices  7.97 us (27%)
  between operations  0.71 us (2%)
    ppermute x8, starting transfers between devices, swap(): lax.ppermute(array, 'ctx', [(index, index ^ bits[index % 2]) for index in...  8.39 us
    ppermute x2, waiting for transfers between devices, swap_hd(): return lax.ppermute(array, ('ctx', 'hd'), pairs)  5.09 us
    pallas_call x1, Pallas kernels, per_device_packed(): pl.pallas_call(mlp_kernel, out_shape=jax.ShapeDtypeStruct((2 * lat_dev, w...  4.25 us
    ppermute x8, waiting for transfers between devices, swap(): lax.ppermute(array, 'ctx', [(index, index ^ bits[index % 2]) for index in...  2.88 us
    ppermute x2, starting transfers between devices, swap_hd(): return lax.ppermute(array, ('ctx', 'hd'), pairs)  2.71 us
    pallas_call x1, Pallas kernels, per_device_packed(): pl.pallas_call(functools.partial(grads_kernel, [0, *[bit // 2 for bit in...  2.13 us
    pallas_call x1, Pallas kernels, per_device_packed(): pl.pallas_call(functools.partial(probs_kernel, offsets, latents, lat_dev,...  1.4 us
    pallas_call x1, Pallas kernels, per_device_packed(): pl.pallas_call(load_kernel, out_shape=(jax.ShapeDtypeStruct((pack_rows, f...  1.11 us
  transfers between devices with their start and end apart: 10, of which 5 were waited for; matrix products, arithmetic and copies ran while one was open for 0% of the time, Pallas kernels for 20%

profile of v2, /device:TPU:0, one launch (start us, length us, event | category | flops | bytes accessed | tf_op | source)
XLA Modules:
  0.0 28.9 jit_solution(9276328239396766473)
XLA Ops:
  0.6 1.1 %load.1 = (bf16[656,256]{1,0:T(8,128)(2,1)S(1)}, bf16[16,1024]{1,0:T(8,128)(2,1)S(1)}) custom-call(bf16[256,256]{1,0:T(8,128)(2,1)} %k_ref.1, bf16[256,256]{1,0:T(8,128)(2,1)} %v_ref.1, bf16[256,128]{1,0:T(8,128)(2,1)} %w_ref.1, bf16[4,256]{1,0:T(4,128)(2,1)} %q_ref.1, bf16[4,1024]{1,0:T(4,128)(2,1)} %cot_ref.1, bf16[4,1024]{1,0:T(4,128)(2,1)} %resid_ref.1, ...), custom_call_target="tpu_custom_call" | custom-call | tf_op jit(solution)/shard_map/load/pallas_call | solution.py:422
  1.7 3.0 %collective-permute-start = (bf16[656,256]{1,0:T(8,128)(2,1)S(1)}, bf16[656,256]{1,0:T(8,128)(2,1)S(1)}, u32[]{:S(2)}, u32[]{:S(2)}) collective-permute-start(bf16[656,256]{1,0:T(8,128)(2,1)S(1)} %get-tuple-element.14), channel_id=1, source_target_pairs={{0,8},{4,20},{8,0},{12,28},{16,24},{20,4},{24,16},{28,12},{1,9},{5... | collective-permute-start | bytes 1007624 | tf_op jit(solution)/shard_map/ppermute | solution.py:387
  4.8 0.0 collective-permute-start.1
  4.8 0.0 copy-start
  4.8 0.0 copy-start.1
  4.8 1.2 %collective-permute-done.1.other_ref = bf16[16,1024]{1,0:T(8,128)(2,1)S(1)} collective-permute-done((bf16[16,1024]{1,0:T(8,128)(2,1)S(1)}, bf16[16,1024]{1,0:T(8,128)(2,1)S(1)}, u32[]{:S(2)}, u32[]{:S(2)}) %collective-permute-start.1) | collective-permute-done | bytes 32800 | tf_op jit(solution)/shard_map/ppermute | solution.py:387
  6.0 4.2 %mlp.1 = f32[8,1024]{1,0:T(8,128)S(1)} custom-call(bf16[16,1024]{1,0:T(8,128)(2,1)S(1)} %get-tuple-element.15.own_ref, bf16[16,1024]{1,0:T(8,128)(2,1)S(1)} %collective-permute-done.1.other_ref, bf16[1024,1024]{1,0:T(8,128)(2,1)} %w_in_ref.1, bf16[1024,1024]{1,0:T(8,128)(2,1)} %w_out_ref.1), custom_call_target="tpu_custom_call" | custom-call | flops 50331648 | bytes 4194304 | tf_op jit(solution)/shard_map/mlp/pallas_call | solution.py:446
  10.2 0.0 collective-permute-done
  10.3 1.8 %collective-permute-start.4 = (bf16[1312,256]{1,0:T(8,128)(2,1)S(1)}, bf16[1312,256]{1,0:T(8,128)(2,1)S(1)}, u32[]{:S(2)}, u32[]{:S(2)}) collective-permute-start(bf16[1312,256]{1,0:T(8,128)(2,1)S(1)} %constant_dynamic-update-slice_fusion.refs_2_), channel_id=1, source_target_pairs={{0,16},{4,12},{8,24},{12,4},{16,0},{20,28},{24,8},{28,20},{1,17},{... | collective-permute-start | bytes 2015240 | tf_op jit(solution)/shard_map/ppermute | solution.py:387
  12.0 0.3 collective-permute-start.2
  12.3 3.3 %collective-permute-done.2 = f32[8,1024]{1,0:T(8,128)S(1)} collective-permute-done((f32[8,1024]{1,0:T(8,128)S(1)}, f32[8,1024]{1,0:T(8,128)S(1)}, u32[]{:S(2)}, u32[]{:S(2)}) %collective-permute-start.2) | collective-permute-done | bytes 32800 | tf_op jit(solution)/shard_map/ppermute | solution.py:395
  15.6 2.4 %collective-permute-start.5 = (f32[8,1024]{1,0:T(8,128)S(1)}, f32[8,1024]{1,0:T(8,128)S(1)}, u32[]{:S(2)}, u32[]{:S(2)}) collective-permute-start(f32[8,1024]{1,0:T(8,128)S(1)} %add.3.part_ref), channel_id=1, source_target_pairs={{0,6},{1,7},{2,4},{3,5},{4,2},{5,3},{6,0},{7,1},{8,14},{9,15},{10,... | collective-permute-start | bytes 98312 | tf_op jit(solution)/shard_map/ppermute | solution.py:395
  18.0 1.8 %collective-permute-done.5.arrived_ref = f32[8,1024]{1,0:T(8,128)S(1)} collective-permute-done((f32[8,1024]{1,0:T(8,128)S(1)}, f32[8,1024]{1,0:T(8,128)S(1)}, u32[]{:S(2)}, u32[]{:S(2)}) %collective-permute-start.5) | collective-permute-done | bytes 32800 | tf_op jit(solution)/shard_map/ppermute | solution.py:395
  19.8 0.2 resid.1.refs_0_
  20.0 1.3 %collective-permute-start.6 = (bf16[8,1024]{1,0:T(8,128)(2,1)S(1)}, bf16[8,1024]{1,0:T(8,128)(2,1)S(1)}, u32[]{:S(2)}, u32[]{:S(2)}) collective-permute-start(bf16[8,1024]{1,0:T(8,128)(2,1)S(1)} %resid.1.refs_0_), channel_id=1, source_target_pairs={{0,12},{4,8},{8,4},{12,0},{16,28},{20,24},{24,20},{28,16},{1,13},{... | collective-permute-start | bytes 49160 | tf_op jit(solution)/shard_map/ppermute | solution.py:387
  21.4 0.3 collective-permute-start.3
  21.6 1.6 %collective-permute-done.6.refs_1_ = bf16[8,1024]{1,0:T(8,128)(2,1)S(1)} collective-permute-done((bf16[8,1024]{1,0:T(8,128)(2,1)S(1)}, bf16[8,1024]{1,0:T(8,128)(2,1)S(1)}, u32[]{:S(2)}, u32[]{:S(2)}) %collective-permute-start.6) | collective-permute-done | bytes 16416 | tf_op jit(solution)/shard_map/ppermute | solution.py:387
  23.2 0.2 collective-permute-start.7
  23.4 0.2 collective-permute-start.8
  23.6 1.6 %collective-permute-start.9 = (bf16[8,1024]{1,0:T(8,128)(2,1)S(1)}, bf16[8,1024]{1,0:T(8,128)(2,1)S(1)}, u32[]{:S(2)}, u32[]{:S(2)}) collective-permute-start(bf16[8,1024]{1,0:T(8,128)(2,1)S(1)} %collective-permute-done.6.refs_1_), channel_id=1, source_target_pairs={{0,20},{4,16},{8,28},{12,24},{16,4},{20,0},{24,12},{28,8},{1,21},{... | collective-permute-start | bytes 49160 | tf_op jit(solution)/shard_map/ppermute | solution.py:387
  25.2 0.1 collective-permute-done.7.refs_5_
  25.3 1.4 %probs.1 = (f32[8,256,128]{2,1,0:T(8,128)S(1)}, bf16[5,256,256]{2,1,0:T(8,128)(2,1)S(1)}, bf16[5,256,256]{2,1,0:T(8,128)(2,1)S(1)}, bf16[8,128,256]{2,1,0:T(8,128)(2,1)S(1)}, bf16[128,256]{1,0:T(8,128)(2,1)S(1)}) custom-call(s32[32]{0:T(128)S(1)} %copy-done, s32[32]{0:T(128)S(1)} %copy-done.1, ...), custom_call_target="tpu_custom_call" | custom-call | flops 134217728 | bytes 524288 | tf_op jit(solution)/shard_map/probs/pallas_call | solution.py:486
  26.8 0.0 collective-permute-done.9.refs_3_
  26.8 2.1 %grads.1 = (bf16[4,256]{1,0:T(4,128)(2,1)}, bf16[256,256]{1,0:T(8,128)(2,1)}, bf16[256,256]{1,0:T(8,128)(2,1)}) custom-call(f32[8,256,128]{2,1,0:T(8,128)S(1)} %get-tuple-element.19.probs_ref, bf16[5,256,256]{2,1,0:T(8,128)(2,1)S(1)} %get-tuple-element.20.keys_ref, bf16[5,256,256]{2,1,0:T(8,128)(2,1)S(1)} %get-tuple-element.21.values_ref, ...), custom_call_target="tpu_custom_call" | custom-call | tf_op jit(solution)/shard_map/grads/pallas_call | solution.py:504
  (8 shorter events, 0.1 us)
Async XLA Ops:
  1.7 8.5 %collective-permute-start = (bf16[656,256]{1,0:T(8,128)(2,1)S(1)}, bf16[656,256]{1,0:T(8,128)(2,1)S(1)}, u32[]{:S(2)}, u32[]{:S(2)}) collective-permute-start(bf16[656,256]{1,0:T(8,128)(2,1)S(1)} %get-tuple-element.14), channel_id=1, source_target_pairs={{0,8},{4,20},{8,0},{12,28},{16,24},{20,4},{24,16},{28,12},{1,9},{5... | collective-permute-start | bytes 1007624 | tf_op jit(solution)/shard_map/ppermute | solution.py:387
  4.8 1.2 %collective-permute-start.1 = (bf16[16,1024]{1,0:T(8,128)(2,1)S(1)}, bf16[16,1024]{1,0:T(8,128)(2,1)S(1)}, u32[]{:S(2)}, u32[]{:S(2)}) collective-permute-start(bf16[16,1024]{1,0:T(8,128)(2,1)S(1)} %get-tuple-element.15.own_ref), channel_id=1, source_target_pairs={{0,4},{4,0},{8,12},{12,8},{16,20},{20,16},{24,28},{28,24},{1,5},{5... | collective-permute-start | bytes 98312 | tf_op jit(solution)/shard_map/ppermute | solution.py:387
  4.8 20.5 %copy-start = (s32[32]{0:T(128)S(1)}, s32[32]{0:T(128)}, u32[]{:S(2)}) copy-start(s32[32]{0:T(128)} %refs_0_.1) | copy-start | bytes 388
  4.8 20.5 %copy-start.1 = (s32[32]{0:T(128)S(1)}, s32[32]{0:T(128)}, u32[]{:S(2)}) copy-start(s32[32]{0:T(128)} %refs_1_.1) | copy-start | bytes 388
  10.3 12.9 %collective-permute-start.4 = (bf16[1312,256]{1,0:T(8,128)(2,1)S(1)}, bf16[1312,256]{1,0:T(8,128)(2,1)S(1)}, u32[]{:S(2)}, u32[]{:S(2)}) collective-permute-start(bf16[1312,256]{1,0:T(8,128)(2,1)S(1)} %constant_dynamic-update-slice_fusion.refs_2_), channel_id=1, source_target_pairs={{0,16},{4,12},{8,24},{12,4},{16,0},{20,28},{24,8},{28,20},{1,17},{... | collective-permute-start | bytes 2015240 | tf_op jit(solution)/shard_map/ppermute | solution.py:387
  12.0 3.6 %collective-permute-start.2 = (f32[8,1024]{1,0:T(8,128)S(1)}, f32[8,1024]{1,0:T(8,128)S(1)}, u32[]{:S(2)}, u32[]{:S(2)}) collective-permute-start(f32[8,1024]{1,0:T(8,128)S(1)} %mlp.1), channel_id=1, source_target_pairs={{0,5},{1,4},{2,7},{3,6},{4,1},{5,0},{6,3},{7,2},{8,13},{9,12},{10,... | collective-permute-start | bytes 98312 | tf_op jit(solution)/shard_map/ppermute | solution.py:395
  15.6 4.2 %collective-permute-start.5 = (f32[8,1024]{1,0:T(8,128)S(1)}, f32[8,1024]{1,0:T(8,128)S(1)}, u32[]{:S(2)}, u32[]{:S(2)}) collective-permute-start(f32[8,1024]{1,0:T(8,128)S(1)} %add.3.part_ref), channel_id=1, source_target_pairs={{0,6},{1,7},{2,4},{3,5},{4,2},{5,3},{6,0},{7,1},{8,14},{9,15},{10,... | collective-permute-start | bytes 98312 | tf_op jit(solution)/shard_map/ppermute | solution.py:395
  20.0 3.2 %collective-permute-start.6 = (bf16[8,1024]{1,0:T(8,128)(2,1)S(1)}, bf16[8,1024]{1,0:T(8,128)(2,1)S(1)}, u32[]{:S(2)}, u32[]{:S(2)}) collective-permute-start(bf16[8,1024]{1,0:T(8,128)(2,1)S(1)} %resid.1.refs_0_), channel_id=1, source_target_pairs={{0,12},{4,8},{8,4},{12,0},{16,28},{20,24},{24,20},{28,16},{1,13},{... | collective-permute-start | bytes 49160 | tf_op jit(solution)/shard_map/ppermute | solution.py:387
  21.4 3.8 %collective-permute-start.3 = (bf16[1312,256]{1,0:T(8,128)(2,1)S(1)}, bf16[1312,256]{1,0:T(8,128)(2,1)S(1)}, u32[]{:S(2)}, u32[]{:S(2)}) collective-permute-start(bf16[1312,256]{1,0:T(8,128)(2,1)S(1)} %constant_dynamic-update-slice_fusion.refs_2_), channel_id=1, source_target_pairs={{0,4},{4,0},{8,12},{12,8},{16,20},{20,16},{24,28},{28,24},{1,5},{5... | collective-permute-start | bytes 2015240 | tf_op jit(solution)/shard_map/ppermute | solution.py:387
  23.2 2.1 %collective-permute-start.7 = (bf16[1312,256]{1,0:T(8,128)(2,1)S(1)}, bf16[1312,256]{1,0:T(8,128)(2,1)S(1)}, u32[]{:S(2)}, u32[]{:S(2)}) collective-permute-start(bf16[1312,256]{1,0:T(8,128)(2,1)S(1)} %collective-permute-done.4.refs_4_), channel_id=1, source_target_pairs={{0,4},{4,0},{8,12},{12,8},{16,20},{20,16},{24,28},{28,24},{1,5},{5... | collective-permute-start | bytes 2015240 | tf_op jit(solution)/shard_map/ppermute | solution.py:387
  23.4 3.3 %collective-permute-start.8 = (bf16[8,1024]{1,0:T(8,128)(2,1)S(1)}, bf16[8,1024]{1,0:T(8,128)(2,1)S(1)}, u32[]{:S(2)}, u32[]{:S(2)}) collective-permute-start(bf16[8,1024]{1,0:T(8,128)(2,1)S(1)} %resid.1.refs_0_), channel_id=1, source_target_pairs={{0,20},{4,16},{8,28},{12,24},{16,4},{20,0},{24,12},{28,8},{1,21},{... | collective-permute-start | bytes 49160 | tf_op jit(solution)/shard_map/ppermute | solution.py:387
  23.6 3.2 %collective-permute-start.9 = (bf16[8,1024]{1,0:T(8,128)(2,1)S(1)}, bf16[8,1024]{1,0:T(8,128)(2,1)S(1)}, u32[]{:S(2)}, u32[]{:S(2)}) collective-permute-start(bf16[8,1024]{1,0:T(8,128)(2,1)S(1)} %collective-permute-done.6.refs_1_), channel_id=1, source_target_pairs={{0,20},{4,16},{8,28},{12,24},{16,4},{20,0},{24,12},{28,8},{1,21},{... | collective-permute-start | bytes 49160 | tf_op jit(solution)/shard_map/ppermute | solution.py:387

commit v3 on v2

--- a/solution.py
+++ b/solution.py
@@ -154,8 +154,8 @@
 NT = (((1,), (1,)), ((), ()))
 TN = (((0,), (0,)), ((), ()))
 Q_ROWS = 16
-MLP_PARTS = 4
-MLP_AHEAD = 2
+LATE_ROWS = 96
+MLP_PARTS = 2
 
 
 def load_kernel(
@@ -221,37 +221,26 @@
     return inv_rms, rows * inv_rms
 
 
-def mlp_kernel(own_ref, other_ref, w_in_ref, w_out_ref, out_ref, w_in, w_out, sems):
+def mlp_kernel(own_ref, other_ref, w_in_ref, w_out_ref, out_ref, w_in, sems):
     parts, size = w_in.shape[0], w_in.shape[2]
     copies = []
     for part in range(parts):
         span = pl.ds(part * size, size)
-        copies.append(
-            (
-                pltpu.make_async_copy(w_in_ref.at[:, span], w_in.at[part], sems.at[0, part]),
-                pltpu.make_async_copy(w_out_ref.at[span], w_out.at[part], sems.at[1, part]),
-            )
-        )
-
-    def begin(part):
-        if part < parts:
-            for copy in copies[part]:
-                copy.start()
-
-    for part in range(MLP_AHEAD):
-        begin(part)
+        copies.append(pltpu.make_async_copy(w_in_ref.at[:, span], w_in.at[part], sems.at[part]))
+    for copy in copies:
+        copy.start()
     cot, rows, gain = chip_rows(own_ref, other_ref)
-    cot = cot.astype(jnp.bfloat16)
     normed = (rms_parts(rows)[1] * gain).astype(jnp.bfloat16)
+    hidden_grad = lax.dot_general(
+        cot.astype(jnp.bfloat16), w_out_ref[...], NT, preferred_element_type=jnp.float32
+    )
     total = jnp.zeros(out_ref.shape, jnp.float32)
-    for part in range(parts):
-        for copy in copies[part]:
-            copy.wait()
-        begin(part + MLP_AHEAD)
+    for part, copy in enumerate(copies):
+        copy.wait()
         up = w_in[part]
         pre_act = jnp.dot(normed, up, preferred_element_type=jnp.float32)
-        hidden_grad = lax.dot_general(cot, w_out[part], NT, preferred_element_type=jnp.float32)
-        pre_grad = (hidden_grad * gelu_slope(pre_act)).astype(jnp.bfloat16)
+        span = slice(part * size, (part + 1) * size)
+        pre_grad = (hidden_grad[:, span] * gelu_slope(pre_act)).astype(jnp.bfloat16)
         total += lax.dot_general(pre_grad, up, NT, preferred_element_type=jnp.float32)
     out_ref[...] = total
 
@@ -271,6 +260,10 @@
     row_head = lax.broadcasted_iota(jnp.int32, shape, 0) // latents
     own_head = row_head == lax.broadcasted_iota(jnp.int32, shape, 1) // HDIM
     return jnp.where(own_head, jnp.concatenate([array] * heads, axis=0), 0.0), own_head
+
+
+def straight(index):
+    return (index ^ (index >> 1) ^ (index >> 2)) % 2 == 0
 
 
 def probs_kernel(offsets, latents, lat_dev, events_dev, first_block, *refs):
@@ -287,7 +280,7 @@
             places.append((ref, slot * pack_rows, offset))
     queries = {}
     for ref, row, offset in places:
-        block = me ^ jnp.where(even, *offset)
+        block = me ^ jnp.where(straight(me), *offset)
         proj_ref[block] = ref[row + base : row + base + proj_ref.shape[1], :]
         queries[offset] = ref[row + pack_rows - Q_ROWS : row + pack_rows, :].astype(jnp.float32)
 
@@ -300,7 +293,7 @@
         if offset[0] % 2 == 0:
             other = queries[(offset[0] ^ 1, offset[1] ^ 1)]
             low, high = jnp.where(even, own, other), jnp.where(even, other, own)
-            chip = (me ^ jnp.where(even, *offset)) // 2
+            chip = (me ^ jnp.where(straight(me), *offset)) // 2
             q_all[chip] = jnp.concatenate([low[:lat_dev], high[:lat_dev]], axis=0)
     wide_q = wide_rows(q_all[...].reshape(latents, q_all.shape[2]), latents)[0]
     wide_ref[...] = wide_q.astype(jnp.bfloat16)
@@ -327,6 +320,7 @@
 
 def grads_kernel(
     row_offsets,
+    pair_offset,
     latents,
     first_block,
     probs_ref,
@@ -344,7 +338,9 @@
     used, features = keys_ref.shape[0], keys_ref.shape[2]
     factor = 1.0 / math.sqrt(HDIM)
     for offset, ref in zip(row_offsets, row_refs):
-        rows_all[(me // 2) ^ offset] = ref[...].astype(jnp.float32)
+        pair = ref[...].astype(jnp.float32)
+        rows_all[(me // 2) ^ offset] = pair[: 2 * lat_dev]
+        rows_all[(me // 2) ^ offset ^ pair_offset] = pair[2 * lat_dev :]
     resid_grad = rows_all[...].reshape(latents, rows_all.shape[2]).astype(jnp.bfloat16)
     cols = features // 2
     upper = jnp.concatenate([proj_ref[block, :, :cols] for block in range(blocks)], axis=1)
@@ -381,10 +377,10 @@
     )
 
 
-def swap(array, bit, odd_bit=None):
-    bits = (bit, bit if odd_bit is None else odd_bit)
-    count = lax.axis_size("ctx")
-    return lax.ppermute(array, "ctx", [(index, index ^ bits[index % 2]) for index in range(count)])
+def swap(array, bit, other_bit=None):
+    bits = (bit, bit if other_bit is None else other_bit)
+    pairs = [(c, c ^ bits[c.bit_count() % 2]) for c in range(lax.axis_size("ctx"))]
+    return lax.ppermute(array, "ctx", pairs)
 
 
 def swap_hd(array, bit):
@@ -438,33 +434,37 @@
         name="load",
     )(*[in_hbm(array) for array in (keys, values, w_proj, queries, cot, resid, norm_gain)])
     other_rows = swap(own_rows, 1)
+    near_out = swap(w_out, 1)
 
     chip_bits = [1 << shift for shift in range(1, ctx.bit_length() - 1)]
     hd_bits = [1 << shift for shift in range(hd.bit_length() - 1)]
-    steps = (tuple(chip_bits), tuple(reversed(chip_bits)))
+    steps = (tuple(bit | 1 for bit in chip_bits), tuple(bit | 1 for bit in reversed(chip_bits)))
     first_piece = swap(pack, *steps[0])
     part = pl.pallas_call(
         mlp_kernel,
         out_shape=jax.ShapeDtypeStruct((2 * lat_dev, width), jnp.float32),
-        in_specs=[vmem] * 2 + [hbm] * 2,
+        in_specs=[vmem] * 2 + [hbm, vmem],
         out_specs=vmem,
         scratch_shapes=[
             pltpu.VMEM((MLP_PARTS, width, hidden // MLP_PARTS), jnp.bfloat16),
-            pltpu.VMEM((MLP_PARTS, hidden // MLP_PARTS, width), jnp.bfloat16),
-            pltpu.SemaphoreType.DMA((2, MLP_PARTS)),
+            pltpu.SemaphoreType.DMA((MLP_PARTS,)),
         ],
         compiler_params=params(16),
         cost_estimate=pl.CostEstimate(
             flops=12 * lat_dev * w_in.size, bytes_accessed=4 * w_in.size, transcendentals=0
         ),
         name="mlp",
-    )(own_rows, other_rows, in_hbm(w_in), in_hbm(w_out))
+    )(own_rows, other_rows, in_hbm(w_in), near_out)
     first_pair = jnp.concatenate([pack, after(first_piece, part)], axis=0)
     second_pair = swap(first_pair, *steps[1])
     for bit in hd_bits[:-1]:
         part = part + swap_hd(part, bit)
-    first_other = swap(after(first_pair, part), 1)
+    early_rows = first_pair.shape[0] - LATE_ROWS
+    early_other = swap(after(first_pair, part)[:early_rows], 1)
+    late_other = swap(after(first_pair, part)[early_rows:], 1)
+    first_other = jnp.concatenate([early_other, late_other], axis=0)
     arrived = swap_hd(part, hd_bits[-1])
+    arrived = after(arrived, early_other)
     rows = pl.pallas_call(
         resid_kernel,
         out_shape=jax.ShapeDtypeStruct((2 * lat_dev, width), jnp.bfloat16),
@@ -473,8 +473,10 @@
         compiler_params=params(8),
         name="resid",
     )(part, arrived, own_rows, other_rows)
-    row_x, row_y = (swap(rows, bit | 1) for bit in chip_bits)
-    row_xy = swap(after(row_x, second_pair), chip_bits[1] | 1)
+    rows = after(rows, late_other)
+    row_x = swap(rows, chip_bits[0] | 1)
+    row_pair = jnp.concatenate([rows, row_x], axis=0)
+    row_far = swap(row_pair, chip_bits[1] | 1)
     second_other = swap(after(second_pair, row_x), 1)
 
     corner = tuple(step ^ other for step, other in zip(*steps))
@@ -503,14 +505,14 @@
     )(latent_pos, seg_start, first_pair, first_other, second_pair, second_other)
     return pl.pallas_call(
         functools.partial(
-            grads_kernel, [0, *[bit // 2 for bit in chip_bits], sum(chip_bits) // 2], latents, first_block
+            grads_kernel, [0, chip_bits[1] // 2], chip_bits[0] // 2, latents, first_block
         ),
         out_shape=(
             jax.ShapeDtypeStruct((lat_dev, features), jnp.bfloat16),
             jax.ShapeDtypeStruct((events_dev, features), jnp.bfloat16),
             jax.ShapeDtypeStruct((events_dev, features), jnp.bfloat16),
         ),
-        in_specs=[vmem] * 9,
+        in_specs=[vmem] * 7,
         out_specs=(vmem,) * 3,
         scratch_shapes=[
             pltpu.VMEM((ctx // 2, 2 * lat_dev, width), jnp.float32),
@@ -519,7 +521,7 @@
         ],
         compiler_params=params(24),
         name="grads",
-    )(probs, used_keys, used_values, proj, wide_q, rows, row_x, row_y, row_xy)
+    )(probs, used_keys, used_values, proj, wide_q, row_pair, row_far)
 
 
 def solution(mesh):

time: 29.1 us -> 27.6 us (0.948)
  waiting for transfers between devices: 7.97 us -> 5.52 us
  starting transfers between devices: 11.1 us -> 13.3 us
  Pallas kernels: 9.08 us -> 7.79 us
    ppermute x2, waiting for transfers between devices: 5.09 us -> 1.65 us  [swap_hd(): return lax.ppermute(array, ('ctx', 'hd'), pairs)]
    ppermute x2, starting transfers between devices: 2.71 us -> 4.5 us  [swap_hd(): return lax.ppermute(array, ('ctx', 'hd'), pairs)]
    pallas_call x1, Pallas kernels: 4.25 us -> 2.96 us  [per_device_packed(): pl.pallas_call(mlp_kernel, out_shape=jax.ShapeDtypeStruct((2 * lat_dev, w...]
    ppermute x8 -> x9, waiting for transfers between devices: 2.88 us -> 3.87 us  [swap(): return lax.ppermute(array, 'ctx', pairs)]
    ppermute x8 -> x9, starting transfers between devices: 8.39 us -> 8.8 us  [swap(): return lax.ppermute(array, 'ctx', pairs)]
  transfers between devices with their start and end apart: 10 -> 11, of which waited for: 5 -> 6; matrix products, arithmetic and copies ran while one was open for 0% -> 1% of each run, Pallas kernels for 20% -> 21%
where the time goes in v3:
time: 27.6 us; the launch traced here: 27.5 us
  starting transfers between devices  13.3 us (48%)
  Pallas kernels  7.79 us (28%)
  waiting for transfers between devices  5.52 us (20%)
  between operations  0.71 us (3%)
    ppermute x9, starting transfers between devices, swap(): return lax.ppermute(array, 'ctx', pairs)  8.8 us
    ppermute x2, starting transfers between devices, swap_hd(): return lax.ppermute(array, ('ctx', 'hd'), pairs)  4.5 us
    ppermute x9, waiting for transfers between devices, swap(): return lax.ppermute(array, 'ctx', pairs)  3.87 us
    pallas_call x1, Pallas kernels, per_device_packed(): pl.pallas_call(mlp_kernel, out_shape=jax.ShapeDtypeStruct((2 * lat_dev, w...  2.96 us
    pallas_call x1, Pallas kernels, per_device_packed(): pl.pallas_call(functools.partial(grads_kernel, [0, chip_bits[1] // 2], ch...  2.13 us
    ppermute x2, waiting for transfers between devices, swap_hd(): return lax.ppermute(array, ('ctx', 'hd'), pairs)  1.65 us
    pallas_call x1, Pallas kernels, per_device_packed(): pl.pallas_call(functools.partial(probs_kernel, offsets, latents, lat_dev,...  1.41 us
    pallas_call x1, Pallas kernels, per_device_packed(): pl.pallas_call(load_kernel, out_shape=(jax.ShapeDtypeStruct((pack_rows, f...  1.1 us
  transfers between devices with their start and end apart: 11, of which 6 were waited for; matrix products, arithmetic and copies ran while one was open for 1% of the time, Pallas kernels for 21%

profile of v3, /device:TPU:0, one launch (start us, length us, event | category | flops | bytes accessed | tf_op | source)
XLA Modules:
  0.0 27.5 jit_solution(15356548079353079147)
XLA Ops:
  0.6 0.5 %collective-permute-start.2 = (bf16[1024,1024]{1,0:T(8,128)(2,1)}, bf16[1024,1024]{1,0:T(8,128)(2,1)S(1)}, u32[]{:S(2)}, u32[]{:S(2)}) collective-permute-start(bf16[1024,1024]{1,0:T(8,128)(2,1)} %param.15), channel_id=1, source_target_pairs={{0,4},{4,0},{8,12},{12,8},{16,20},{20,16},{24,28},{28,24},{1,5},{5... | collective-permute-start | bytes 6291464 | tf_op jit(solution)/shard_map/ppermute | solution.py:383
  1.2 1.1 %load.1 = (bf16[656,256]{1,0:T(8,128)(2,1)S(1)}, bf16[16,1024]{1,0:T(8,128)(2,1)S(1)}) custom-call(bf16[256,256]{1,0:T(8,128)(2,1)} %k_ref.1, bf16[256,256]{1,0:T(8,128)(2,1)} %v_ref.1, bf16[256,128]{1,0:T(8,128)(2,1)} %w_ref.1, bf16[4,256]{1,0:T(4,128)(2,1)} %q_ref.1, bf16[4,1024]{1,0:T(4,128)(2,1)} %cot_ref.1, bf16[4,1024]{1,0:T(4,128)(2,1)} %resid_ref.1, ...), custom_call_target="tpu_custom_call" | custom-call | tf_op jit(solution)/shard_map/load/pallas_call | solution.py:418
  2.3 2.7 %collective-permute-start = (bf16[656,256]{1,0:T(8,128)(2,1)S(1)}, bf16[656,256]{1,0:T(8,128)(2,1)S(1)}, u32[]{:S(2)}, u32[]{:S(2)}) collective-permute-start(bf16[656,256]{1,0:T(8,128)(2,1)S(1)} %get-tuple-element.15), channel_id=1, source_target_pairs={{0,12},{4,16},{8,28},{12,0},{16,4},{20,24},{24,20},{28,8},{1,13},{... | collective-permute-start | bytes 1007624 | tf_op jit(solution)/shard_map/ppermute | solution.py:383
  4.9 0.0 collective-permute-start.1
  5.0 1.1 %collective-permute-done.1.other_ref = bf16[16,1024]{1,0:T(8,128)(2,1)S(1)} collective-permute-done((bf16[16,1024]{1,0:T(8,128)(2,1)S(1)}, bf16[16,1024]{1,0:T(8,128)(2,1)S(1)}, u32[]{:S(2)}, u32[]{:S(2)}) %collective-permute-start.1) | collective-permute-done | bytes 32800 | tf_op jit(solution)/shard_map/ppermute | solution.py:383
  6.1 3.0 %mlp.1 = f32[8,1024]{1,0:T(8,128)S(1)} custom-call(bf16[16,1024]{1,0:T(8,128)(2,1)S(1)} %get-tuple-element.16.own_ref, bf16[16,1024]{1,0:T(8,128)(2,1)S(1)} %collective-permute-done.1.other_ref, bf16[1024,1024]{1,0:T(8,128)(2,1)} %w_in_ref.1, bf16[1024,1024]{1,0:T(8,128)(2,1)S(1)} %collective-permute-done.2.w_out_ref), custom_call_target="tpu_custom_call" | custom-call | flops 50331648 | bytes 4194304 | tf_op jit(solution)/shard_map/mlp/pallas_call | solution.py:443
  9.1 0.0 copy-start
  9.1 1.8 %collective-permute-start.3 = (f32[8,1024]{1,0:T(8,128)S(1)}, f32[8,1024]{1,0:T(8,128)S(1)}, u32[]{:S(2)}, u32[]{:S(2)}) collective-permute-start(f32[8,1024]{1,0:T(8,128)S(1)} %mlp.1), channel_id=1, source_target_pairs={{0,5},{1,4},{2,7},{3,6},{4,1},{5,0},{6,3},{7,2},{8,13},{9,12},{10,... | collective-permute-start | bytes 98312 | tf_op jit(solution)/shard_map/ppermute | solution.py:391
  10.9 1.6 %collective-permute-start.6 = (bf16[1312,256]{1,0:T(8,128)(2,1)S(1)}, bf16[1312,256]{1,0:T(8,128)(2,1)S(1)}, u32[]{:S(2)}, u32[]{:S(2)}) collective-permute-start(bf16[1312,256]{1,0:T(8,128)(2,1)S(1)} %constant_dynamic-update-slice_fusion.refs_2_), channel_id=1, source_target_pairs={{0,20},{4,8},{8,4},{12,24},{16,28},{20,0},{24,12},{28,16},{1,21},{... | collective-permute-start | bytes 2015240 | tf_op jit(solution)/shard_map/ppermute | solution.py:383
  12.5 0.1 collective-permute-done.3
  12.6 0.4 %collective-permute-start.4 = (bf16[1216,256]{1,0:T(8,128)(2,1)S(1)}, bf16[1216,256]{1,0:T(8,128)(2,1)S(1)}, u32[]{:S(2)}, u32[]{:S(2)}) collective-permute-start(bf16[1216,256]{1,0:T(8,128)(2,1)S(1)} %slice.6), channel_id=1, source_target_pairs={{0,4},{4,0},{8,12},{12,8},{16,20},{20,16},{24,28},{28,24},{1,5},{5... | collective-permute-start | bytes 1867784 | tf_op jit(solution)/shard_map/ppermute | solution.py:383
  13.0 0.2 collective-permute-start.5
  13.2 2.7 %collective-permute-start.7 = (f32[8,1024]{1,0:T(8,128)S(1)}, f32[8,1024]{1,0:T(8,128)S(1)}, u32[]{:S(2)}, u32[]{:S(2)}) collective-permute-start(f32[8,1024]{1,0:T(8,128)S(1)} %add.3.part_ref), channel_id=1, source_target_pairs={{0,6},{1,7},{2,4},{3,5},{4,2},{5,3},{6,0},{7,1},{8,14},{9,15},{10,... | collective-permute-start | bytes 98312 | tf_op jit(solution)/shard_map/ppermute | solution.py:391
  15.9 1.6 %collective-permute-done.7.arrived_ref = f32[8,1024]{1,0:T(8,128)S(1)} collective-permute-done((f32[8,1024]{1,0:T(8,128)S(1)}, f32[8,1024]{1,0:T(8,128)S(1)}, u32[]{:S(2)}, u32[]{:S(2)}) %collective-permute-start.7) | collective-permute-done | bytes 32800 | tf_op jit(solution)/shard_map/ppermute | solution.py:391
  17.5 0.2 resid.1
  17.7 1.6 %collective-permute-start.8 = (bf16[8,1024]{1,0:T(8,128)(2,1)S(1)}, bf16[8,1024]{1,0:T(8,128)(2,1)S(1)}, u32[]{:S(2)}, u32[]{:S(2)}) collective-permute-start(bf16[8,1024]{1,0:T(8,128)(2,1)S(1)} %resid.1), channel_id=1, source_target_pairs={{0,12},{4,8},{8,4},{12,0},{16,28},{20,24},{24,20},{28,16},{1,13},{... | collective-permute-start | bytes 49160 | tf_op jit(solution)/shard_map/ppermute | solution.py:383
  19.4 1.8 %collective-permute-done.6.refs_4_ = bf16[1312,256]{1,0:T(8,128)(2,1)S(1)} collective-permute-done((bf16[1312,256]{1,0:T(8,128)(2,1)S(1)}, bf16[1312,256]{1,0:T(8,128)(2,1)S(1)}, u32[]{:S(2)}, u32[]{:S(2)}) %collective-permute-start.6) | collective-permute-done | bytes 671776 | tf_op jit(solution)/shard_map/ppermute | solution.py:383
  21.2 0.0 collective-permute-done.8
  21.2 0.7 %collective-permute-start.9 = (bf16[1312,256]{1,0:T(8,128)(2,1)S(1)}, bf16[1312,256]{1,0:T(8,128)(2,1)S(1)}, u32[]{:S(2)}, u32[]{:S(2)}) collective-permute-start(bf16[1312,256]{1,0:T(8,128)(2,1)S(1)} %collective-permute-done.6.refs_4_), channel_id=1, source_target_pairs={{0,4},{4,0},{8,12},{12,8},{16,20},{20,16},{24,28},{28,24},{1,5},{5... | collective-permute-start | bytes 2015240 | tf_op jit(solution)/shard_map/ppermute | solution.py:383
  21.9 1.1 %collective-permute-start.10 = (bf16[16,1024]{1,0:T(8,128)(2,1)S(1)}, bf16[16,1024]{1,0:T(8,128)(2,1)S(1)}, u32[]{:S(2)}, u32[]{:S(2)}) collective-permute-start(bf16[16,1024]{1,0:T(8,128)(2,1)S(1)} %constant_dynamic-update-slice_fusion.2.refs_0_), channel_id=1, source_target_pairs={{0,20},{4,16},{8,28},{12,24},{16,4},{20,0},{24,12},{28,8},{1,21},{... | collective-permute-start | bytes 98312 | tf_op jit(solution)/shard_map/ppermute | solution.py:383
  23.0 0.6 %collective-permute-done.9.refs_5_ = bf16[1312,256]{1,0:T(8,128)(2,1)S(1)} collective-permute-done((bf16[1312,256]{1,0:T(8,128)(2,1)S(1)}, bf16[1312,256]{1,0:T(8,128)(2,1)S(1)}, u32[]{:S(2)}, u32[]{:S(2)}) %collective-permute-start.9) | collective-permute-done | bytes 671776 | tf_op jit(solution)/shard_map/ppermute | solution.py:383
  23.7 1.4 %probs.1 = (f32[8,256,128]{2,1,0:T(8,128)S(1)}, bf16[5,256,256]{2,1,0:T(8,128)(2,1)S(1)}, bf16[5,256,256]{2,1,0:T(8,128)(2,1)S(1)}, bf16[8,128,256]{2,1,0:T(8,128)(2,1)S(1)}, bf16[128,256]{1,0:T(8,128)(2,1)S(1)}) custom-call(s32[32]{0:T(128)S(1)} %copy-done, s32[32]{0:T(128)S(1)} %copy-done.1, ...), custom_call_target="tpu_custom_call" | custom-call | flops 134217728 | bytes 524288 | tf_op jit(solution)/shard_map/probs/pallas_call | solution.py:488
  25.1 0.3 %collective-permute-done.10.refs_1_ = bf16[16,1024]{1,0:T(8,128)(2,1)S(1)} collective-permute-done((bf16[16,1024]{1,0:T(8,128)(2,1)S(1)}, bf16[16,1024]{1,0:T(8,128)(2,1)S(1)}, u32[]{:S(2)}, u32[]{:S(2)}) %collective-permute-start.10) | collective-permute-done | bytes 32800 | tf_op jit(solution)/shard_map/ppermute | solution.py:383
  25.3 2.1 %grads.1 = (bf16[4,256]{1,0:T(4,128)(2,1)}, bf16[256,256]{1,0:T(8,128)(2,1)}, bf16[256,256]{1,0:T(8,128)(2,1)}) custom-call(f32[8,256,128]{2,1,0:T(8,128)S(1)} %get-tuple-element.22.probs_ref, bf16[5,256,256]{2,1,0:T(8,128)(2,1)S(1)} %get-tuple-element.23.keys_ref, bf16[5,256,256]{2,1,0:T(8,128)(2,1)S(1)} %get-tuple-element.24.values_ref, ...), custom_call_target="tpu_custom_call" | custom-call | tf_op jit(solution)/shard_map/grads/pallas_call | solution.py:506
  (15 shorter events, 0.2 us)
Async XLA Ops:
  0.6 5.5 %collective-permute-start.2 = (bf16[1024,1024]{1,0:T(8,128)(2,1)}, bf16[1024,1024]{1,0:T(8,128)(2,1)S(1)}, u32[]{:S(2)}, u32[]{:S(2)}) collective-permute-start(bf16[1024,1024]{1,0:T(8,128)(2,1)} %param.15), channel_id=1, source_target_pairs={{0,4},{4,0},{8,12},{12,8},{16,20},{20,16},{24,28},{28,24},{1,5},{5... | collective-permute-start | bytes 6291464 | tf_op jit(solution)/shard_map/ppermute | solution.py:383
  2.3 8.6 %collective-permute-start = (bf16[656,256]{1,0:T(8,128)(2,1)S(1)}, bf16[656,256]{1,0:T(8,128)(2,1)S(1)}, u32[]{:S(2)}, u32[]{:S(2)}) collective-permute-start(bf16[656,256]{1,0:T(8,128)(2,1)S(1)} %get-tuple-element.15), channel_id=1, source_target_pairs={{0,12},{4,16},{8,28},{12,0},{16,4},{20,24},{24,20},{28,8},{1,13},{... | collective-permute-start | bytes 1007624 | tf_op jit(solution)/shard_map/ppermute | solution.py:383
  4.9 1.2 %collective-permute-start.1 = (bf16[16,1024]{1,0:T(8,128)(2,1)S(1)}, bf16[16,1024]{1,0:T(8,128)(2,1)S(1)}, u32[]{:S(2)}, u32[]{:S(2)}) collective-permute-start(bf16[16,1024]{1,0:T(8,128)(2,1)S(1)} %get-tuple-element.16.own_ref), channel_id=1, source_target_pairs={{0,4},{4,0},{8,12},{12,8},{16,20},{20,16},{24,28},{28,24},{1,5},{5... | collective-permute-start | bytes 98312 | tf_op jit(solution)/shard_map/ppermute | solution.py:383
  9.1 14.5 %copy-start = (s32[32]{0:T(128)S(1)}, s32[32]{0:T(128)}, u32[]{:S(2)}) copy-start(s32[32]{0:T(128)} %refs_0_.1) | copy-start | bytes 388
  9.1 14.5 %copy-start.1 = (s32[32]{0:T(128)S(1)}, s32[32]{0:T(128)}, u32[]{:S(2)}) copy-start(s32[32]{0:T(128)} %refs_1_.1) | copy-start | bytes 388
  9.1 3.4 %collective-permute-start.3 = (f32[8,1024]{1,0:T(8,128)S(1)}, f32[8,1024]{1,0:T(8,128)S(1)}, u32[]{:S(2)}, u32[]{:S(2)}) collective-permute-start(f32[8,1024]{1,0:T(8,128)S(1)} %mlp.1), channel_id=1, source_target_pairs={{0,5},{1,4},{2,7},{3,6},{4,1},{5,0},{6,3},{7,2},{8,13},{9,12},{10,... | collective-permute-start | bytes 98312 | tf_op jit(solution)/shard_map/ppermute | solution.py:391
  10.9 10.3 %collective-permute-start.6 = (bf16[1312,256]{1,0:T(8,128)(2,1)S(1)}, bf16[1312,256]{1,0:T(8,128)(2,1)S(1)}, u32[]{:S(2)}, u32[]{:S(2)}) collective-permute-start(bf16[1312,256]{1,0:T(8,128)(2,1)S(1)} %constant_dynamic-update-slice_fusion.refs_2_), channel_id=1, source_target_pairs={{0,20},{4,8},{8,4},{12,24},{16,28},{20,0},{24,12},{28,16},{1,21},{... | collective-permute-start | bytes 2015240 | tf_op jit(solution)/shard_map/ppermute | solution.py:383
  12.6 4.9 %collective-permute-start.4 = (bf16[1216,256]{1,0:T(8,128)(2,1)S(1)}, bf16[1216,256]{1,0:T(8,128)(2,1)S(1)}, u32[]{:S(2)}, u32[]{:S(2)}) collective-permute-start(bf16[1216,256]{1,0:T(8,128)(2,1)S(1)} %slice.6), channel_id=1, source_target_pairs={{0,4},{4,0},{8,12},{12,8},{16,20},{20,16},{24,28},{28,24},{1,5},{5... | collective-permute-start | bytes 1867784 | tf_op jit(solution)/shard_map/ppermute | solution.py:383
  13.0 4.7 %collective-permute-start.5 = (bf16[96,256]{1,0:T(8,128)(2,1)S(1)}, bf16[96,256]{1,0:T(8,128)(2,1)S(1)}, u32[]{:S(2)}, u32[]{:S(2)}) collective-permute-start(bf16[96,256]{1,0:T(8,128)(2,1)S(1)} %slice.7), channel_id=1, source_target_pairs={{0,4},{4,0},{8,12},{12,8},{16,20},{20,16},{24,28},{28,24},{1,5},{5... | collective-permute-start | bytes 147464 | tf_op jit(solution)/shard_map/ppermute | solution.py:383
  13.2 4.3 %collective-permute-start.7 = (f32[8,1024]{1,0:T(8,128)S(1)}, f32[8,1024]{1,0:T(8,128)S(1)}, u32[]{:S(2)}, u32[]{:S(2)}) collective-permute-start(f32[8,1024]{1,0:T(8,128)S(1)} %add.3.part_ref), channel_id=1, source_target_pairs={{0,6},{1,7},{2,4},{3,5},{4,2},{5,3},{6,0},{7,1},{8,14},{9,15},{10,... | collective-permute-start | bytes 98312 | tf_op jit(solution)/shard_map/ppermute | solution.py:391
  17.7 3.5 %collective-permute-start.8 = (bf16[8,1024]{1,0:T(8,128)(2,1)S(1)}, bf16[8,1024]{1,0:T(8,128)(2,1)S(1)}, u32[]{:S(2)}, u32[]{:S(2)}) collective-permute-start(bf16[8,1024]{1,0:T(8,128)(2,1)S(1)} %resid.1), channel_id=1, source_target_pairs={{0,12},{4,8},{8,4},{12,0},{16,28},{20,24},{24,20},{28,16},{1,13},{... | collective-permute-start | bytes 49160 | tf_op jit(solution)/shard_map/ppermute | solution.py:383
  21.2 2.5 %collective-permute-start.9 = (bf16[1312,256]{1,0:T(8,128)(2,1)S(1)}, bf16[1312,256]{1,0:T(8,128)(2,1)S(1)}, u32[]{:S(2)}, u32[]{:S(2)}) collective-permute-start(bf16[1312,256]{1,0:T(8,128)(2,1)S(1)} %collective-permute-done.6.refs_4_), channel_id=1, source_target_pairs={{0,4},{4,0},{8,12},{12,8},{16,20},{20,16},{24,28},{28,24},{1,5},{5... | collective-permute-start | bytes 2015240 | tf_op jit(solution)/shard_map/ppermute | solution.py:383
  21.9 3.4 %collective-permute-start.10 = (bf16[16,1024]{1,0:T(8,128)(2,1)S(1)}, bf16[16,1024]{1,0:T(8,128)(2,1)S(1)}, u32[]{:S(2)}, u32[]{:S(2)}) collective-permute-start(bf16[16,1024]{1,0:T(8,128)(2,1)S(1)} %constant_dynamic-update-slice_fusion.2.refs_0_), channel_id=1, source_target_pairs={{0,20},{4,16},{8,28},{12,24},{16,4},{20,0},{24,12},{28,8},{1,21},{... | collective-permute-start | bytes 98312 | tf_op jit(solution)/shard_map/ppermute | solution.py:383

commit v4 on v3

--- a/solution.py
+++ b/solution.py
@@ -166,12 +166,17 @@
     cot_ref,
     resid_ref,
     gain_ref,
+    pos_ref,
+    start_ref,
     pack_ref,
     rows_ref,
+    marks_ref,
     q_own,
     cot_own,
     resid_own,
     gain_own,
+    pos_own,
+    start_own,
     sems,
 ):
     events, half, cols = k_ref.shape[0], w_ref.shape[0] // 2, w_ref.shape[1]
@@ -181,6 +186,8 @@
         (cot_ref, cot_own),
         (resid_ref, resid_own),
         (gain_ref, gain_own),
+        (pos_ref, pos_own),
+        (start_ref, start_own),
         (k_ref, pack_ref.at[pl.ds(0, events)]),
         (v_ref, pack_ref.at[pl.ds(events, events)]),
         (w_ref.at[pl.ds(0, half)], pack_ref.at[pl.ds(base, half), pl.ds(0, cols)]),
@@ -192,7 +199,7 @@
     ]
     for copy in copies:
         copy.start()
-    for copy in copies[:4]:
+    for copy in copies[:6]:
         copy.wait()
     rows = q_own[...].astype(jnp.float32)
     spare = jnp.zeros((Q_ROWS - rows.shape[0], rows.shape[1]), jnp.float32)
@@ -202,7 +209,15 @@
     held = [cot_own[...].astype(jnp.float32), resid_own[...].astype(jnp.float32)]
     held += [jnp.broadcast_to(gain, (rows_ref.shape[0] - 2 * lat_dev, gain.shape[1]))]
     rows_ref[...] = jnp.concatenate(held, axis=0).astype(jnp.bfloat16)
-    for copy in copies[4:]:
+    latents = pos_ref.shape[0]
+    lane = lax.broadcasted_iota(jnp.int32, marks_ref.shape, 1) % latents
+    first = lax.broadcasted_iota(jnp.int32, marks_ref.shape, 0) == 0
+    marks = jnp.zeros(marks_ref.shape, jnp.int32)
+    for latent in range(latents):
+        pair = jnp.where(first, pos_own[latent], start_own[latent])
+        marks = jnp.where(lane == latent, pair, marks)
+    marks_ref[...] = marks
+    for copy in copies[6:]:
         copy.wait()
 
 
@@ -267,8 +282,8 @@
 
 
 def probs_kernel(offsets, latents, lat_dev, events_dev, first_block, *refs):
-    pos_ref, start_ref = refs[:2]
-    pack_refs = refs[2:-6]
+    marks_ref = refs[0]
+    pack_refs = refs[1:-6]
     probs_ref, keys_ref, values_ref, proj_ref, wide_ref, q_all = refs[-6:]
     me = lax.axis_index("ctx")
     even = me % 2 == 0
@@ -296,26 +311,29 @@
             chip = (me ^ jnp.where(straight(me), *offset)) // 2
             q_all[chip] = jnp.concatenate([low[:lat_dev], high[:lat_dev]], axis=0)
     wide_q = wide_rows(q_all[...].reshape(latents, q_all.shape[2]), latents)[0]
+    wide_q = wide_q * (1.0 / math.sqrt(HDIM))
     wide_ref[...] = wide_q.astype(jnp.bfloat16)
     wide_qt = wide_q.T.astype(jnp.bfloat16)
     lanes = wide_qt.shape[1]
 
-    lane = lax.broadcasted_iota(jnp.int32, (1, lanes), 1) % latents
-    pos, start = jnp.zeros((1, lanes), jnp.int32), jnp.zeros((1, lanes), jnp.int32)
-    for latent in range(latents):
-        pos = jnp.where(lane == latent, pos_ref[latent], pos)
-        start = jnp.where(lane == latent, start_ref[latent], start)
+    pos, start = marks_ref[0:1, :], marks_ref[1:2, :]
     used, features = keys_ref.shape[0], keys_ref.shape[2]
-    keys = keys_ref[...].reshape(used * events_dev, features)
-    spot = first_block * events_dev + lax.broadcasted_iota(jnp.int32, (keys.shape[0], lanes), 0)
-    visible = (spot >= start) & (spot <= pos)
-    scores = (1.0 / math.sqrt(HDIM)) * jnp.dot(keys, wide_qt, preferred_element_type=jnp.float32)
-    scores = jnp.where(visible, scores, -1e30)
-    top = jnp.max(scores, axis=0, keepdims=True)
-    expo = jnp.where(visible, jnp.exp(scores - top), 0.0)
-    probs = expo * (1.0 / jnp.sum(expo, axis=0, keepdims=True))
+    top = jnp.full((1, lanes), -1e30, jnp.float32)
+    for slot in range(used):
+        scores = jnp.dot(keys_ref[slot], wide_qt, preferred_element_type=jnp.float32)
+        spot = (first_block + slot) * events_dev + lax.broadcasted_iota(jnp.int32, scores.shape, 0)
+        scores = jnp.where((spot >= start) & (spot <= pos), scores, -1e30)
+        probs_ref[first_block + slot] = scores
+        top = jnp.maximum(top, jnp.max(scores, axis=0, keepdims=True))
+    total = jnp.zeros((1, lanes), jnp.float32)
+    for slot in range(used):
+        expo = jnp.exp(probs_ref[first_block + slot] - top)
+        probs_ref[first_block + slot] = expo
+        total += jnp.sum(expo, axis=0, keepdims=True)
+    share = 1.0 / total
+    for slot in range(used):
+        probs_ref[first_block + slot] = probs_ref[first_block + slot] * share
     probs_ref[:first_block] = jnp.zeros((first_block, events_dev, lanes), jnp.float32)
-    probs_ref[first_block:] = probs.reshape(used, events_dev, lanes)
 
 
 def grads_kernel(
@@ -331,7 +349,7 @@
     *refs,
 ):
     row_refs = refs[: len(row_offsets)]
-    qg_ref, kg_ref, vg_ref, rows_all, qg_all, scores_all = refs[len(row_offsets) :]
+    qg_ref, kg_ref, vg_ref, rows_all, qg_all, grad_all, scores_all = refs[len(row_offsets) :]
     me = lax.axis_index("ctx")
     lat_dev = qg_ref.shape[0]
     blocks, events_dev, lanes = probs_ref.shape
@@ -352,22 +370,27 @@
     out_grad = jnp.concatenate(out_grad, axis=1).astype(jnp.bfloat16).astype(jnp.float32)
     wide_g, own_head = wide_rows(out_grad, latents)
     wide_gt, wide_g = wide_g.T.astype(jnp.bfloat16), wide_g.astype(jnp.bfloat16)
-    keys = keys_ref[...].reshape(used * events_dev, features)
-    values = values_ref[...].reshape(used * events_dev, features)
-    probs = probs_ref[first_block:].reshape(used * events_dev, lanes)
-    prob_grad = jnp.dot(values, wide_gt, preferred_element_type=jnp.float32)
-    delta = jnp.sum(probs * prob_grad, axis=0, keepdims=True)
-    score_grad = (factor * probs * (prob_grad - delta)).astype(jnp.bfloat16)
-    scores_all[:first_block] = jnp.zeros((first_block, events_dev, lanes), jnp.bfloat16)
-    scores_all[first_block:] = score_grad.reshape(used, events_dev, lanes)
-
-    wide = lax.dot_general(score_grad, keys, TN, preferred_element_type=jnp.float32)
+    delta = jnp.zeros((1, lanes), jnp.float32)
+    for slot in range(used):
+        prob_grad = jnp.dot(values_ref[slot], wide_gt, preferred_element_type=jnp.float32)
+        grad_all[slot] = prob_grad
+        delta += jnp.sum(probs_ref[first_block + slot] * prob_grad, axis=0, keepdims=True)
+    wide = jnp.zeros((lanes, features), jnp.float32)
+    for slot in range(used):
+        score_grad = probs_ref[first_block + slot] * (grad_all[slot] - delta)
+        score_grad = score_grad.astype(jnp.bfloat16)
+        scores_all[first_block + slot] = score_grad
+        wide += lax.dot_general(
+            score_grad, keys_ref[slot], TN, preferred_element_type=jnp.float32
+        )
+    for slot in range(first_block):
+        scores_all[slot] = jnp.zeros((events_dev, lanes), jnp.bfloat16)
     wide = jnp.where(own_head, wide, 0.0)
     total = sum(wide[head * latents : (head + 1) * latents] for head in range(lanes // latents))
     qg_all[...] = total.reshape(qg_all.shape)
     pair = qg_all[me // 2]
     mine = jnp.where(me % 2 == 0, pair[:lat_dev], pair[lat_dev:])
-    qg_ref[...] = mine.astype(jnp.bfloat16)
+    qg_ref[...] = (factor * mine).astype(jnp.bfloat16)
     prob_round = probs_ref[me].astype(jnp.bfloat16)
     vg_ref[...] = jnp.dot(prob_round, wide_g, preferred_element_type=jnp.float32).astype(
         jnp.bfloat16
@@ -412,27 +435,37 @@
     events_dev, features = keys.shape
     hidden = w_in.shape[1]
     vmem = pl.BlockSpec(memory_space=pltpu.VMEM)
-    smem = pl.BlockSpec(memory_space=pltpu.SMEM)
     hbm = pl.BlockSpec(memory_space=pltpu.HBM)
     pack_rows = 2 * events_dev + w_proj.shape[0] // 2 + Q_ROWS
-    pack, own_rows = pl.pallas_call(
+    lanes = features // HDIM * latents
+    pack, own_rows, marks = pl.pallas_call(
         load_kernel,
         out_shape=(
             jax.ShapeDtypeStruct((pack_rows, features), jnp.bfloat16),
             jax.ShapeDtypeStruct((4 * lat_dev, width), jnp.bfloat16),
+            jax.ShapeDtypeStruct((8, lanes), jnp.int32),
         ),
-        in_specs=[hbm] * 7,
-        out_specs=(vmem,) * 2,
+        in_specs=[hbm] * 9,
+        out_specs=(vmem,) * 3,
         scratch_shapes=[
             pltpu.VMEM((lat_dev, features), jnp.bfloat16),
             pltpu.VMEM((lat_dev, width), jnp.bfloat16),
             pltpu.VMEM((lat_dev, width), jnp.bfloat16),
             pltpu.VMEM((width,), jnp.bfloat16),
-            pltpu.SemaphoreType.DMA((8,)),
+            pltpu.SMEM((latents,), jnp.int32),
+            pltpu.SMEM((latents,), jnp.int32),
+            pltpu.SemaphoreType.DMA((10,)),
         ],
         compiler_params=params(8),
         name="load",
-    )(*[in_hbm(array) for array in (keys, values, w_proj, queries, cot, resid, norm_gain)])
+    )(
+        *[
+            in_hbm(array)
+            for array in (
+                keys, values, w_proj, queries, cot, resid, norm_gain, latent_pos, seg_start
+            )
+        ]
+    )
     other_rows = swap(own_rows, 1)
     near_out = swap(w_out, 1)
 
@@ -494,7 +527,7 @@
             jax.ShapeDtypeStruct((ctx, w_proj.shape[0] // 2, features), jnp.bfloat16),
             jax.ShapeDtypeStruct((lanes, features), jnp.bfloat16),
         ),
-        in_specs=[smem] * 2 + [vmem] * 4,
+        in_specs=[vmem] * 5,
         out_specs=(vmem,) * 5,
         scratch_shapes=[pltpu.VMEM((ctx // 2, 2 * lat_dev, features), jnp.float32)],
         compiler_params=params(24),
@@ -502,7 +535,7 @@
             flops=2 * ctx * keys.size * lanes, bytes_accessed=8 * keys.size, transcendentals=0
         ),
         name="probs",
-    )(latent_pos, seg_start, first_pair, first_other, second_pair, second_other)
+    )(marks, first_pair, first_other, second_pair, second_other)
     return pl.pallas_call(
         functools.partial(
             grads_kernel, [0, chip_bits[1] // 2], chip_bits[0] // 2, latents, first_block
@@ -517,6 +550,7 @@
         scratch_shapes=[
             pltpu.VMEM((ctx // 2, 2 * lat_dev, width), jnp.float32),
             pltpu.VMEM((ctx // 2, 2 * lat_dev, features), jnp.float32),
+            pltpu.VMEM((ctx - first_block, events_dev, lanes), jnp.float32),
             pltpu.VMEM((ctx, events_dev, lanes), jnp.bfloat16),
         ],
         compiler_params=params(24),

time: 27.6 us -> 27.3 us (0.989)
  Pallas kernels: 7.79 us -> 6.86 us
  waiting for transfers between devices: 5.52 us -> 6.15 us
    ppermute x9, waiting for transfers between devices: 3.87 us -> 4.48 us  [swap(): return lax.ppermute(array, 'ctx', pairs)]
    pallas_call x1, Pallas kernels: 1.41 us -> 0.81 us  [per_device_packed(): pl.pallas_call(functools.partial(probs_kernel, offsets, latents, lat_dev,...]
    pallas_call x1, Pallas kernels: 2.13 us -> 1.78 us  [per_device_packed(): pl.pallas_call(functools.partial(grads_kernel, [0, chip_bits[1] // 2], ch...]
  transfers between devices with their start and end apart: 11 -> 11, of which waited for: 6 -> 6; matrix products, arithmetic and copies ran while one was open for 1% -> 1% of each run, Pallas kernels for 21% -> 19%
where the time goes in v4:
time: 27.3 us; the launch traced here: 27.1 us
  starting transfers between devices  13.3 us (49%)
  Pallas kernels  6.86 us (25%)
  waiting for transfers between devices  6.15 us (23%)
  between operations  0.69 us (3%)
    ppermute x9, starting transfers between devices, swap(): return lax.ppermute(array, 'ctx', pairs)  8.8 us
    ppermute x9, waiting for transfers between devices, swap(): return lax.ppermute(array, 'ctx', pairs)  4.48 us
    ppermute x2, starting transfers between devices, swap_hd(): return lax.ppermute(array, ('ctx', 'hd'), pairs)  4.46 us
    pallas_call x1, Pallas kernels, per_device_packed(): pl.pallas_call(mlp_kernel, out_shape=jax.ShapeDtypeStruct((2 * lat_dev, w...  2.96 us
    pallas_call x1, Pallas kernels, per_device_packed(): pl.pallas_call(functools.partial(grads_kernel, [0, chip_bits[1] // 2], ch...  1.78 us
    ppermute x2, waiting for transfers between devices, swap_hd(): return lax.ppermute(array, ('ctx', 'hd'), pairs)  1.67 us
    pallas_call x1, Pallas kernels, per_device_packed(): pl.pallas_call(load_kernel, out_shape=(jax.ShapeDtypeStruct((pack_rows, f...  1.12 us
    pallas_call x1, Pallas kernels, per_device_packed(): pl.pallas_call(functools.partial(probs_kernel, offsets, latents, lat_dev,...  0.81 us
  transfers between devices with their start and end apart: 11, of which 6 were waited for; matrix products, arithmetic and copies ran while one was open for 1% of the time, Pallas kernels for 19%

profile of v4, /device:TPU:0, one launch (start us, length us, event | category | flops | bytes accessed | tf_op | source)
XLA Modules:
  0.0 27.1 jit_solution(15660663262789187007)
XLA Ops:
  0.6 0.5 %collective-permute-start.2 = (bf16[1024,1024]{1,0:T(8,128)(2,1)}, bf16[1024,1024]{1,0:T(8,128)(2,1)S(1)}, u32[]{:S(2)}, u32[]{:S(2)}) collective-permute-start(bf16[1024,1024]{1,0:T(8,128)(2,1)} %param.15), channel_id=1, source_target_pairs={{0,4},{4,0},{8,12},{12,8},{16,20},{20,16},{24,28},{28,24},{1,5},{5... | collective-permute-start | bytes 6291464 | tf_op jit(solution)/shard_map/ppermute | solution.py:406
  1.2 1.1 %load.1 = (bf16[656,256]{1,0:T(8,128)(2,1)S(1)}, bf16[16,1024]{1,0:T(8,128)(2,1)S(1)}, s32[8,128]{1,0:T(8,128)S(1)}) custom-call(bf16[256,256]{1,0:T(8,128)(2,1)} %k_ref.1, bf16[256,256]{1,0:T(8,128)(2,1)} %v_ref.1, bf16[256,128]{1,0:T(8,128)(2,1)} %w_ref.1, bf16[4,256]{1,0:T(4,128)(2,1)} %q_ref.1, bf16[4,1024]{1,0:T(4,128)(2,1)} %cot_ref.1, ...), custom_call_target="tpu_custom_call" | custom-call | tf_op jit(solution)/shard_map/load/pallas_call | solution.py:441
  2.3 2.7 %collective-permute-start = (bf16[656,256]{1,0:T(8,128)(2,1)S(1)}, bf16[656,256]{1,0:T(8,128)(2,1)S(1)}, u32[]{:S(2)}, u32[]{:S(2)}) collective-permute-start(bf16[656,256]{1,0:T(8,128)(2,1)S(1)} %get-tuple-element.17), channel_id=1, source_target_pairs={{0,12},{4,16},{8,28},{12,0},{16,4},{20,24},{24,20},{28,8},{1,13},{... | collective-permute-start | bytes 1007624 | tf_op jit(solution)/shard_map/ppermute | solution.py:406
  4.9 0.0 collective-permute-start.1
  5.0 1.1 %collective-permute-done.1.other_ref = bf16[16,1024]{1,0:T(8,128)(2,1)S(1)} collective-permute-done((bf16[16,1024]{1,0:T(8,128)(2,1)S(1)}, bf16[16,1024]{1,0:T(8,128)(2,1)S(1)}, u32[]{:S(2)}, u32[]{:S(2)}) %collective-permute-start.1) | collective-permute-done | bytes 32800 | tf_op jit(solution)/shard_map/ppermute | solution.py:406
  6.2 3.0 %mlp.1 = f32[8,1024]{1,0:T(8,128)S(1)} custom-call(bf16[16,1024]{1,0:T(8,128)(2,1)S(1)} %get-tuple-element.18.own_ref, bf16[16,1024]{1,0:T(8,128)(2,1)S(1)} %collective-permute-done.1.other_ref, bf16[1024,1024]{1,0:T(8,128)(2,1)} %w_in_ref.1, bf16[1024,1024]{1,0:T(8,128)(2,1)S(1)} %collective-permute-done.2.w_out_ref), custom_call_target="tpu_custom_call" | custom-call | flops 50331648 | bytes 4194304 | tf_op jit(solution)/shard_map/mlp/pallas_call | solution.py:476
  9.1 1.7 %collective-permute-start.3 = (f32[8,1024]{1,0:T(8,128)S(1)}, f32[8,1024]{1,0:T(8,128)S(1)}, u32[]{:S(2)}, u32[]{:S(2)}) collective-permute-start(f32[8,1024]{1,0:T(8,128)S(1)} %mlp.1), channel_id=1, source_target_pairs={{0,5},{1,4},{2,7},{3,6},{4,1},{5,0},{6,3},{7,2},{8,13},{9,12},{10,... | collective-permute-start | bytes 98312 | tf_op jit(solution)/shard_map/ppermute | solution.py:414
  10.9 1.6 %collective-permute-start.6 = (bf16[1312,256]{1,0:T(8,128)(2,1)S(1)}, bf16[1312,256]{1,0:T(8,128)(2,1)S(1)}, u32[]{:S(2)}, u32[]{:S(2)}) collective-permute-start(bf16[1312,256]{1,0:T(8,128)(2,1)S(1)} %constant_dynamic-update-slice_fusion.refs_1_), channel_id=1, source_target_pairs={{0,20},{4,8},{8,4},{12,24},{16,28},{20,0},{24,12},{28,16},{1,21},{... | collective-permute-start | bytes 2015240 | tf_op jit(solution)/shard_map/ppermute | solution.py:406
  12.5 0.1 collective-permute-done.3
  12.6 0.4 %collective-permute-start.4 = (bf16[1216,256]{1,0:T(8,128)(2,1)S(1)}, bf16[1216,256]{1,0:T(8,128)(2,1)S(1)}, u32[]{:S(2)}, u32[]{:S(2)}) collective-permute-start(bf16[1216,256]{1,0:T(8,128)(2,1)S(1)} %slice.6), channel_id=1, source_target_pairs={{0,4},{4,0},{8,12},{12,8},{16,20},{20,16},{24,28},{28,24},{1,5},{5... | collective-permute-start | bytes 1867784 | tf_op jit(solution)/shard_map/ppermute | solution.py:406
  13.0 0.2 collective-permute-start.5
  13.2 2.7 %collective-permute-start.7 = (f32[8,1024]{1,0:T(8,128)S(1)}, f32[8,1024]{1,0:T(8,128)S(1)}, u32[]{:S(2)}, u32[]{:S(2)}) collective-permute-start(f32[8,1024]{1,0:T(8,128)S(1)} %add.3.part_ref), channel_id=1, source_target_pairs={{0,6},{1,7},{2,4},{3,5},{4,2},{5,3},{6,0},{7,1},{8,14},{9,15},{10,... | collective-permute-start | bytes 98312 | tf_op jit(solution)/shard_map/ppermute | solution.py:414
  15.9 1.6 %collective-permute-done.7.arrived_ref = f32[8,1024]{1,0:T(8,128)S(1)} collective-permute-done((f32[8,1024]{1,0:T(8,128)S(1)}, f32[8,1024]{1,0:T(8,128)S(1)}, u32[]{:S(2)}, u32[]{:S(2)}) %collective-permute-start.7) | collective-permute-done | bytes 32800 | tf_op jit(solution)/shard_map/ppermute | solution.py:414
  17.5 0.2 resid.1
  17.7 0.0 collective-permute-done.5
  17.7 1.6 %collective-permute-start.8 = (bf16[8,1024]{1,0:T(8,128)(2,1)S(1)}, bf16[8,1024]{1,0:T(8,128)(2,1)S(1)}, u32[]{:S(2)}, u32[]{:S(2)}) collective-permute-start(bf16[8,1024]{1,0:T(8,128)(2,1)S(1)} %resid.1), channel_id=1, source_target_pairs={{0,12},{4,8},{8,4},{12,0},{16,28},{20,24},{24,20},{28,16},{1,13},{... | collective-permute-start | bytes 49160 | tf_op jit(solution)/shard_map/ppermute | solution.py:406
  19.3 1.8 %collective-permute-done.6.refs_3_ = bf16[1312,256]{1,0:T(8,128)(2,1)S(1)} collective-permute-done((bf16[1312,256]{1,0:T(8,128)(2,1)S(1)}, bf16[1312,256]{1,0:T(8,128)(2,1)S(1)}, u32[]{:S(2)}, u32[]{:S(2)}) %collective-permute-start.6) | collective-permute-done | bytes 671776 | tf_op jit(solution)/shard_map/ppermute | solution.py:406
  21.1 0.0 collective-permute-done.8
  21.2 0.7 %collective-permute-start.9 = (bf16[1312,256]{1,0:T(8,128)(2,1)S(1)}, bf16[1312,256]{1,0:T(8,128)(2,1)S(1)}, u32[]{:S(2)}, u32[]{:S(2)}) collective-permute-start(bf16[1312,256]{1,0:T(8,128)(2,1)S(1)} %collective-permute-done.6.refs_3_), channel_id=1, source_target_pairs={{0,4},{4,0},{8,12},{12,8},{16,20},{20,16},{24,28},{28,24},{1,5},{5... | collective-permute-start | bytes 2015240 | tf_op jit(solution)/shard_map/ppermute | solution.py:406
  21.9 1.1 %collective-permute-start.10 = (bf16[16,1024]{1,0:T(8,128)(2,1)S(1)}, bf16[16,1024]{1,0:T(8,128)(2,1)S(1)}, u32[]{:S(2)}, u32[]{:S(2)}) collective-permute-start(bf16[16,1024]{1,0:T(8,128)(2,1)S(1)} %constant_dynamic-update-slice_fusion.2.refs_0_), channel_id=1, source_target_pairs={{0,20},{4,16},{8,28},{12,24},{16,4},{20,0},{24,12},{28,8},{1,21},{... | collective-permute-start | bytes 98312 | tf_op jit(solution)/shard_map/ppermute | solution.py:406
  23.0 0.6 %collective-permute-done.9.refs_4_ = bf16[1312,256]{1,0:T(8,128)(2,1)S(1)} collective-permute-done((bf16[1312,256]{1,0:T(8,128)(2,1)S(1)}, bf16[1312,256]{1,0:T(8,128)(2,1)S(1)}, u32[]{:S(2)}, u32[]{:S(2)}) %collective-permute-start.9) | collective-permute-done | bytes 671776 | tf_op jit(solution)/shard_map/ppermute | solution.py:406
  23.6 0.8 %probs.1 = (f32[8,256,128]{2,1,0:T(8,128)S(1)}, bf16[5,256,256]{2,1,0:T(8,128)(2,1)S(1)}, bf16[5,256,256]{2,1,0:T(8,128)(2,1)S(1)}, bf16[8,128,256]{2,1,0:T(8,128)(2,1)S(1)}, bf16[128,256]{1,0:T(8,128)(2,1)S(1)}) custom-call(s32[8,128]{1,0:T(8,128)S(1)} %get-tuple-element.16.refs_0_, bf16[1312,256]{1,0:T(8,128)(2,1)S(1)} %constant_dynamic-update-slice_fusion.refs_1_, ...), custom_call_target="tpu_custom_call" | custom-call | flops 134217728 | bytes 524288 | tf_op jit(solution)/shard_map/probs/pallas_call | solution.py:521
  24.4 0.9 %collective-permute-done.10.refs_1_ = bf16[16,1024]{1,0:T(8,128)(2,1)S(1)} collective-permute-done((bf16[16,1024]{1,0:T(8,128)(2,1)S(1)}, bf16[16,1024]{1,0:T(8,128)(2,1)S(1)}, u32[]{:S(2)}, u32[]{:S(2)}) %collective-permute-start.10) | collective-permute-done | bytes 32800 | tf_op jit(solution)/shard_map/ppermute | solution.py:406
  25.3 1.8 %grads.1 = (bf16[4,256]{1,0:T(4,128)(2,1)}, bf16[256,256]{1,0:T(8,128)(2,1)}, bf16[256,256]{1,0:T(8,128)(2,1)}) custom-call(f32[8,256,128]{2,1,0:T(8,128)S(1)} %get-tuple-element.24.probs_ref, bf16[5,256,256]{2,1,0:T(8,128)(2,1)S(1)} %get-tuple-element.25.keys_ref, bf16[5,256,256]{2,1,0:T(8,128)(2,1)S(1)} %get-tuple-element.26.values_ref, ...), custom_call_target="tpu_custom_call" | custom-call | tf_op jit(solution)/shard_map/grads/pallas_call | solution.py:539
  (11 shorter events, 0.2 us)
Async XLA Ops:
  0.6 5.5 %collective-permute-start.2 = (bf16[1024,1024]{1,0:T(8,128)(2,1)}, bf16[1024,1024]{1,0:T(8,128)(2,1)S(1)}, u32[]{:S(2)}, u32[]{:S(2)}) collective-permute-start(bf16[1024,1024]{1,0:T(8,128)(2,1)} %param.15), channel_id=1, source_target_pairs={{0,4},{4,0},{8,12},{12,8},{16,20},{20,16},{24,28},{28,24},{1,5},{5... | collective-permute-start | bytes 6291464 | tf_op jit(solution)/shard_map/ppermute | solution.py:406
  2.3 8.6 %collective-permute-start = (bf16[656,256]{1,0:T(8,128)(2,1)S(1)}, bf16[656,256]{1,0:T(8,128)(2,1)S(1)}, u32[]{:S(2)}, u32[]{:S(2)}) collective-permute-start(bf16[656,256]{1,0:T(8,128)(2,1)S(1)} %get-tuple-element.17), channel_id=1, source_target_pairs={{0,12},{4,16},{8,28},{12,0},{16,4},{20,24},{24,20},{28,8},{1,13},{... | collective-permute-start | bytes 1007624 | tf_op jit(solution)/shard_map/ppermute | solution.py:406
  4.9 1.2 %collective-permute-start.1 = (bf16[16,1024]{1,0:T(8,128)(2,1)S(1)}, bf16[16,1024]{1,0:T(8,128)(2,1)S(1)}, u32[]{:S(2)}, u32[]{:S(2)}) collective-permute-start(bf16[16,1024]{1,0:T(8,128)(2,1)S(1)} %get-tuple-element.18.own_ref), channel_id=1, source_target_pairs={{0,4},{4,0},{8,12},{12,8},{16,20},{20,16},{24,28},{28,24},{1,5},{5... | collective-permute-start | bytes 98312 | tf_op jit(solution)/shard_map/ppermute | solution.py:406
  9.1 3.4 %collective-permute-start.3 = (f32[8,1024]{1,0:T(8,128)S(1)}, f32[8,1024]{1,0:T(8,128)S(1)}, u32[]{:S(2)}, u32[]{:S(2)}) collective-permute-start(f32[8,1024]{1,0:T(8,128)S(1)} %mlp.1), channel_id=1, source_target_pairs={{0,5},{1,4},{2,7},{3,6},{4,1},{5,0},{6,3},{7,2},{8,13},{9,12},{10,... | collective-permute-start | bytes 98312 | tf_op jit(solution)/shard_map/ppermute | solution.py:414
  10.9 10.3 %collective-permute-start.6 = (bf16[1312,256]{1,0:T(8,128)(2,1)S(1)}, bf16[1312,256]{1,0:T(8,128)(2,1)S(1)}, u32[]{:S(2)}, u32[]{:S(2)}) collective-permute-start(bf16[1312,256]{1,0:T(8,128)(2,1)S(1)} %constant_dynamic-update-slice_fusion.refs_1_), channel_id=1, source_target_pairs={{0,20},{4,8},{8,4},{12,24},{16,28},{20,0},{24,12},{28,16},{1,21},{... | collective-permute-start | bytes 2015240 | tf_op jit(solution)/shard_map/ppermute | solution.py:406
  12.6 4.9 %collective-permute-start.4 = (bf16[1216,256]{1,0:T(8,128)(2,1)S(1)}, bf16[1216,256]{1,0:T(8,128)(2,1)S(1)}, u32[]{:S(2)}, u32[]{:S(2)}) collective-permute-start(bf16[1216,256]{1,0:T(8,128)(2,1)S(1)} %slice.6), channel_id=1, source_target_pairs={{0,4},{4,0},{8,12},{12,8},{16,20},{20,16},{24,28},{28,24},{1,5},{5... | collective-permute-start | bytes 1867784 | tf_op jit(solution)/shard_map/ppermute | solution.py:406
  13.0 4.7 %collective-permute-start.5 = (bf16[96,256]{1,0:T(8,128)(2,1)S(1)}, bf16[96,256]{1,0:T(8,128)(2,1)S(1)}, u32[]{:S(2)}, u32[]{:S(2)}) collective-permute-start(bf16[96,256]{1,0:T(8,128)(2,1)S(1)} %slice.7), channel_id=1, source_target_pairs={{0,4},{4,0},{8,12},{12,8},{16,20},{20,16},{24,28},{28,24},{1,5},{5... | collective-permute-start | bytes 147464 | tf_op jit(solution)/shard_map/ppermute | solution.py:406
  13.2 4.3 %collective-permute-start.7 = (f32[8,1024]{1,0:T(8,128)S(1)}, f32[8,1024]{1,0:T(8,128)S(1)}, u32[]{:S(2)}, u32[]{:S(2)}) collective-permute-start(f32[8,1024]{1,0:T(8,128)S(1)} %add.3.part_ref), channel_id=1, source_target_pairs={{0,6},{1,7},{2,4},{3,5},{4,2},{5,3},{6,0},{7,1},{8,14},{9,15},{10,... | collective-permute-start | bytes 98312 | tf_op jit(solution)/shard_map/ppermute | solution.py:414
  17.7 3.5 %collective-permute-start.8 = (bf16[8,1024]{1,0:T(8,128)(2,1)S(1)}, bf16[8,1024]{1,0:T(8,128)(2,1)S(1)}, u32[]{:S(2)}, u32[]{:S(2)}) collective-permute-start(bf16[8,1024]{1,0:T(8,128)(2,1)S(1)} %resid.1), channel_id=1, source_target_pairs={{0,12},{4,8},{8,4},{12,0},{16,28},{20,24},{24,20},{28,16},{1,13},{... | collective-permute-start | bytes 49160 | tf_op jit(solution)/shard_map/ppermute | solution.py:406
  21.2 2.5 %collective-permute-start.9 = (bf16[1312,256]{1,0:T(8,128)(2,1)S(1)}, bf16[1312,256]{1,0:T(8,128)(2,1)S(1)}, u32[]{:S(2)}, u32[]{:S(2)}) collective-permute-start(bf16[1312,256]{1,0:T(8,128)(2,1)S(1)} %collective-permute-done.6.refs_3_), channel_id=1, source_target_pairs={{0,4},{4,0},{8,12},{12,8},{16,20},{20,16},{24,28},{28,24},{1,5},{5... | collective-permute-start | bytes 2015240 | tf_op jit(solution)/shard_map/ppermute | solution.py:406
  21.9 3.4 %collective-permute-start.10 = (bf16[16,1024]{1,0:T(8,128)(2,1)S(1)}, bf16[16,1024]{1,0:T(8,128)(2,1)S(1)}, u32[]{:S(2)}, u32[]{:S(2)}) collective-permute-start(bf16[16,1024]{1,0:T(8,128)(2,1)S(1)} %constant_dynamic-update-slice_fusion.2.refs_0_), channel_id=1, source_target_pairs={{0,20},{4,16},{8,28},{12,24},{16,4},{20,0},{24,12},{28,8},{1,21},{... | collective-permute-start | bytes 98312 | tf_op jit(solution)/shard_map/ppermute | solution.py:406

commit v5 on v4

--- a/solution.py
+++ b/solution.py
@@ -357,8 +357,9 @@
     factor = 1.0 / math.sqrt(HDIM)
     for offset, ref in zip(row_offsets, row_refs):
         pair = ref[...].astype(jnp.float32)
-        rows_all[(me // 2) ^ offset] = pair[: 2 * lat_dev]
-        rows_all[(me // 2) ^ offset ^ pair_offset] = pair[2 * lat_dev :]
+        chip = (me // 2) ^ jnp.where(straight(me), *offset)
+        rows_all[chip] = pair[: 2 * lat_dev]
+        rows_all[chip ^ jnp.where(straight(me), *pair_offset)] = pair[2 * lat_dev :]
     resid_grad = rows_all[...].reshape(latents, rows_all.shape[2]).astype(jnp.bfloat16)
     cols = features // 2
     upper = jnp.concatenate([proj_ref[block, :, :cols] for block in range(blocks)], axis=1)
@@ -507,9 +508,9 @@
         name="resid",
     )(part, arrived, own_rows, other_rows)
     rows = after(rows, late_other)
-    row_x = swap(rows, chip_bits[0] | 1)
+    row_x = swap(rows, *steps[0])
     row_pair = jnp.concatenate([rows, row_x], axis=0)
-    row_far = swap(row_pair, chip_bits[1] | 1)
+    row_far = swap(row_pair, *steps[1])
     second_other = swap(after(second_pair, row_x), 1)
 
     corner = tuple(step ^ other for step, other in zip(*steps))
@@ -518,6 +519,8 @@
     offsets = [near, [turn(pair) for pair in near], far, [turn(pair) for pair in far]]
     first_block = max(0, events_dev * ctx // 2 - WINDOW) // events_dev
     lanes = features // HDIM * latents
+    pair_offset = tuple(bit // 2 for bit in steps[0])
+    row_offsets = [(0, 0), tuple(bit // 2 for bit in steps[1])]
     probs, used_keys, used_values, proj, wide_q = pl.pallas_call(
         functools.partial(probs_kernel, offsets, latents, lat_dev, events_dev, first_block),
         out_shape=(
@@ -538,7 +541,7 @@
     )(marks, first_pair, first_other, second_pair, second_other)
     return pl.pallas_call(
         functools.partial(
-            grads_kernel, [0, chip_bits[1] // 2], chip_bits[0] // 2, latents, first_block
+            grads_kernel, row_offsets, pair_offset, latents, first_block
         ),
         out_shape=(
             jax.ShapeDtypeStruct((lat_dev, features), jnp.bfloat16),

time: 27.3 us -> 27 us (0.989)
  waiting for transfers between devices: 6.15 us -> 5.71 us
    ppermute x9, waiting for transfers between devices: 4.48 us -> 4.04 us  [swap(): return lax.ppermute(array, 'ctx', pairs)]
where the time goes in v5:
time: 27 us; the launch traced here: 26.8 us
  starting transfers between devices  13.4 us (50%)
  Pallas kernels  6.85 us (25%)
  waiting for transfers between devices  5.71 us (21%)
  between operations  0.69 us (3%)
    ppermute x9, starting transfers between devices, swap(): return lax.ppermute(array, 'ctx', pairs)  8.98 us
    ppermute x2, starting transfers between devices, swap_hd(): return lax.ppermute(array, ('ctx', 'hd'), pairs)  4.46 us
    ppermute x9, waiting for transfers between devices, swap(): return lax.ppermute(array, 'ctx', pairs)  4.04 us
    pallas_call x1, Pallas kernels, per_device_packed(): pl.pallas_call(mlp_kernel, out_shape=jax.ShapeDtypeStruct((2 * lat_dev, w...  2.96 us
    pallas_call x1, Pallas kernels, per_device_packed(): pl.pallas_call(functools.partial(grads_kernel, row_offsets, pair_offset,...  1.78 us
    ppermute x2, waiting for transfers between devices, swap_hd(): return lax.ppermute(array, ('ctx', 'hd'), pairs)  1.67 us
    pallas_call x1, Pallas kernels, per_device_packed(): pl.pallas_call(load_kernel, out_shape=(jax.ShapeDtypeStruct((pack_rows, f...  1.12 us
    pallas_call x1, Pallas kernels, per_device_packed(): pl.pallas_call(functools.partial(probs_kernel, offsets, latents, lat_dev,...  0.8 us
  transfers between devices with their start and end apart: 11, of which 6 were waited for; matrix products, arithmetic and copies ran while one was open for 1% of the time, Pallas kernels for 19%

profile of v5, /device:TPU:0, one launch (start us, length us, event | category | flops | bytes accessed | tf_op | source)
XLA Modules:
  0.0 26.8 jit_solution(15396822022238666715)
XLA Ops:
  0.6 0.5 %collective-permute-start.2 = (bf16[1024,1024]{1,0:T(8,128)(2,1)}, bf16[1024,1024]{1,0:T(8,128)(2,1)S(1)}, u32[]{:S(2)}, u32[]{:S(2)}) collective-permute-start(bf16[1024,1024]{1,0:T(8,128)(2,1)} %param.15), channel_id=1, source_target_pairs={{0,4},{4,0},{8,12},{12,8},{16,20},{20,16},{24,28},{28,24},{1,5},{5... | collective-permute-start | bytes 6291464 | tf_op jit(solution)/shard_map/ppermute | solution.py:407
  1.2 1.1 %load.1 = (bf16[656,256]{1,0:T(8,128)(2,1)S(1)}, bf16[16,1024]{1,0:T(8,128)(2,1)S(1)}, s32[8,128]{1,0:T(8,128)S(1)}) custom-call(bf16[256,256]{1,0:T(8,128)(2,1)} %k_ref.1, bf16[256,256]{1,0:T(8,128)(2,1)} %v_ref.1, bf16[256,128]{1,0:T(8,128)(2,1)} %w_ref.1, bf16[4,256]{1,0:T(4,128)(2,1)} %q_ref.1, bf16[4,1024]{1,0:T(4,128)(2,1)} %cot_ref.1, ...), custom_call_target="tpu_custom_call" | custom-call | tf_op jit(solution)/shard_map/load/pallas_call | solution.py:442
  2.3 2.7 %collective-permute-start = (bf16[656,256]{1,0:T(8,128)(2,1)S(1)}, bf16[656,256]{1,0:T(8,128)(2,1)S(1)}, u32[]{:S(2)}, u32[]{:S(2)}) collective-permute-start(bf16[656,256]{1,0:T(8,128)(2,1)S(1)} %get-tuple-element.17), channel_id=1, source_target_pairs={{0,12},{4,16},{8,28},{12,0},{16,4},{20,24},{24,20},{28,8},{1,13},{... | collective-permute-start | bytes 1007624 | tf_op jit(solution)/shard_map/ppermute | solution.py:407
  4.9 0.0 collective-permute-start.1
  5.0 1.1 %collective-permute-done.1.other_ref = bf16[16,1024]{1,0:T(8,128)(2,1)S(1)} collective-permute-done((bf16[16,1024]{1,0:T(8,128)(2,1)S(1)}, bf16[16,1024]{1,0:T(8,128)(2,1)S(1)}, u32[]{:S(2)}, u32[]{:S(2)}) %collective-permute-start.1) | collective-permute-done | bytes 32800 | tf_op jit(solution)/shard_map/ppermute | solution.py:407
  6.2 3.0 %mlp.1 = f32[8,1024]{1,0:T(8,128)S(1)} custom-call(bf16[16,1024]{1,0:T(8,128)(2,1)S(1)} %get-tuple-element.18.own_ref, bf16[16,1024]{1,0:T(8,128)(2,1)S(1)} %collective-permute-done.1.other_ref, bf16[1024,1024]{1,0:T(8,128)(2,1)} %w_in_ref.1, bf16[1024,1024]{1,0:T(8,128)(2,1)S(1)} %collective-permute-done.2.w_out_ref), custom_call_target="tpu_custom_call" | custom-call | flops 50331648 | bytes 4194304 | tf_op jit(solution)/shard_map/mlp/pallas_call | solution.py:477
  9.1 1.7 %collective-permute-start.3 = (f32[8,1024]{1,0:T(8,128)S(1)}, f32[8,1024]{1,0:T(8,128)S(1)}, u32[]{:S(2)}, u32[]{:S(2)}) collective-permute-start(f32[8,1024]{1,0:T(8,128)S(1)} %mlp.1), channel_id=1, source_target_pairs={{0,5},{1,4},{2,7},{3,6},{4,1},{5,0},{6,3},{7,2},{8,13},{9,12},{10,... | collective-permute-start | bytes 98312 | tf_op jit(solution)/shard_map/ppermute | solution.py:415
  10.9 1.6 %collective-permute-start.6 = (bf16[1312,256]{1,0:T(8,128)(2,1)S(1)}, bf16[1312,256]{1,0:T(8,128)(2,1)S(1)}, u32[]{:S(2)}, u32[]{:S(2)}) collective-permute-start(bf16[1312,256]{1,0:T(8,128)(2,1)S(1)} %constant_dynamic-update-slice_fusion.refs_1_), channel_id=1, source_target_pairs={{0,20},{4,8},{8,4},{12,24},{16,28},{20,0},{24,12},{28,16},{1,21},{... | collective-permute-start | bytes 2015240 | tf_op jit(solution)/shard_map/ppermute | solution.py:407
  12.5 0.1 collective-permute-done.3
  12.6 0.4 %collective-permute-start.4 = (bf16[1216,256]{1,0:T(8,128)(2,1)S(1)}, bf16[1216,256]{1,0:T(8,128)(2,1)S(1)}, u32[]{:S(2)}, u32[]{:S(2)}) collective-permute-start(bf16[1216,256]{1,0:T(8,128)(2,1)S(1)} %slice.6), channel_id=1, source_target_pairs={{0,4},{4,0},{8,12},{12,8},{16,20},{20,16},{24,28},{28,24},{1,5},{5... | collective-permute-start | bytes 1867784 | tf_op jit(solution)/shard_map/ppermute | solution.py:407
  13.0 0.2 collective-permute-start.5
  13.2 2.7 %collective-permute-start.7 = (f32[8,1024]{1,0:T(8,128)S(1)}, f32[8,1024]{1,0:T(8,128)S(1)}, u32[]{:S(2)}, u32[]{:S(2)}) collective-permute-start(f32[8,1024]{1,0:T(8,128)S(1)} %add.3.part_ref), channel_id=1, source_target_pairs={{0,6},{1,7},{2,4},{3,5},{4,2},{5,3},{6,0},{7,1},{8,14},{9,15},{10,... | collective-permute-start | bytes 98312 | tf_op jit(solution)/shard_map/ppermute | solution.py:415
  15.9 1.6 %collective-permute-done.7.arrived_ref = f32[8,1024]{1,0:T(8,128)S(1)} collective-permute-done((f32[8,1024]{1,0:T(8,128)S(1)}, f32[8,1024]{1,0:T(8,128)S(1)}, u32[]{:S(2)}, u32[]{:S(2)}) %collective-permute-start.7) | collective-permute-done | bytes 32800 | tf_op jit(solution)/shard_map/ppermute | solution.py:415
  17.5 0.2 resid.1
  17.7 0.0 collective-permute-done.5
  17.7 1.6 %collective-permute-start.8 = (bf16[8,1024]{1,0:T(8,128)(2,1)S(1)}, bf16[8,1024]{1,0:T(8,128)(2,1)S(1)}, u32[]{:S(2)}, u32[]{:S(2)}) collective-permute-start(bf16[8,1024]{1,0:T(8,128)(2,1)S(1)} %resid.1), channel_id=1, source_target_pairs={{0,12},{4,16},{8,28},{12,0},{16,4},{20,24},{24,20},{28,8},{1,13},{... | collective-permute-start | bytes 49160 | tf_op jit(solution)/shard_map/ppermute | solution.py:407
  19.3 1.8 %collective-permute-done.6.refs_3_ = bf16[1312,256]{1,0:T(8,128)(2,1)S(1)} collective-permute-done((bf16[1312,256]{1,0:T(8,128)(2,1)S(1)}, bf16[1312,256]{1,0:T(8,128)(2,1)S(1)}, u32[]{:S(2)}, u32[]{:S(2)}) %collective-permute-start.6) | collective-permute-done | bytes 671776 | tf_op jit(solution)/shard_map/ppermute | solution.py:407
  21.1 0.0 collective-permute-done.8
  21.2 0.5 %collective-permute-start.9 = (bf16[1312,256]{1,0:T(8,128)(2,1)S(1)}, bf16[1312,256]{1,0:T(8,128)(2,1)S(1)}, u32[]{:S(2)}, u32[]{:S(2)}) collective-permute-start(bf16[1312,256]{1,0:T(8,128)(2,1)S(1)} %collective-permute-done.6.refs_3_), channel_id=1, source_target_pairs={{0,4},{4,0},{8,12},{12,8},{16,20},{20,16},{24,28},{28,24},{1,5},{5... | collective-permute-start | bytes 2015240 | tf_op jit(solution)/shard_map/ppermute | solution.py:407
  21.7 1.4 %collective-permute-start.10 = (bf16[16,1024]{1,0:T(8,128)(2,1)S(1)}, bf16[16,1024]{1,0:T(8,128)(2,1)S(1)}, u32[]{:S(2)}, u32[]{:S(2)}) collective-permute-start(bf16[16,1024]{1,0:T(8,128)(2,1)S(1)} %constant_dynamic-update-slice_fusion.2.refs_0_), channel_id=1, source_target_pairs={{0,20},{4,8},{8,4},{12,24},{16,28},{20,0},{24,12},{28,16},{1,21},{... | collective-permute-start | bytes 98312 | tf_op jit(solution)/shard_map/ppermute | solution.py:407
  23.2 0.3 %collective-permute-done.9.refs_4_ = bf16[1312,256]{1,0:T(8,128)(2,1)S(1)} collective-permute-done((bf16[1312,256]{1,0:T(8,128)(2,1)S(1)}, bf16[1312,256]{1,0:T(8,128)(2,1)S(1)}, u32[]{:S(2)}, u32[]{:S(2)}) %collective-permute-start.9) | collective-permute-done | bytes 671776 | tf_op jit(solution)/shard_map/ppermute | solution.py:407
  23.5 0.8 %probs.1 = (f32[8,256,128]{2,1,0:T(8,128)S(1)}, bf16[5,256,256]{2,1,0:T(8,128)(2,1)S(1)}, bf16[5,256,256]{2,1,0:T(8,128)(2,1)S(1)}, bf16[8,128,256]{2,1,0:T(8,128)(2,1)S(1)}, bf16[128,256]{1,0:T(8,128)(2,1)S(1)}) custom-call(s32[8,128]{1,0:T(8,128)S(1)} %get-tuple-element.16.refs_0_, bf16[1312,256]{1,0:T(8,128)(2,1)S(1)} %constant_dynamic-update-slice_fusion.refs_1_, ...), custom_call_target="tpu_custom_call" | custom-call | flops 134217728 | bytes 524288 | tf_op jit(solution)/shard_map/probs/pallas_call | solution.py:524
  24.3 0.8 %collective-permute-done.10.refs_1_ = bf16[16,1024]{1,0:T(8,128)(2,1)S(1)} collective-permute-done((bf16[16,1024]{1,0:T(8,128)(2,1)S(1)}, bf16[16,1024]{1,0:T(8,128)(2,1)S(1)}, u32[]{:S(2)}, u32[]{:S(2)}) %collective-permute-start.10) | collective-permute-done | bytes 32800 | tf_op jit(solution)/shard_map/ppermute | solution.py:407
  25.0 1.8 %grads.1 = (bf16[4,256]{1,0:T(4,128)(2,1)}, bf16[256,256]{1,0:T(8,128)(2,1)}, bf16[256,256]{1,0:T(8,128)(2,1)}) custom-call(f32[8,256,128]{2,1,0:T(8,128)S(1)} %get-tuple-element.24.probs_ref, bf16[5,256,256]{2,1,0:T(8,128)(2,1)S(1)} %get-tuple-element.25.keys_ref, bf16[5,256,256]{2,1,0:T(8,128)(2,1)S(1)} %get-tuple-element.26.values_ref, ...), custom_call_target="tpu_custom_call" | custom-call | tf_op jit(solution)/shard_map/grads/pallas_call | solution.py:542
  (11 shorter events, 0.2 us)
Async XLA Ops:
  0.6 5.5 %collective-permute-start.2 = (bf16[1024,1024]{1,0:T(8,128)(2,1)}, bf16[1024,1024]{1,0:T(8,128)(2,1)S(1)}, u32[]{:S(2)}, u32[]{:S(2)}) collective-permute-start(bf16[1024,1024]{1,0:T(8,128)(2,1)} %param.15), channel_id=1, source_target_pairs={{0,4},{4,0},{8,12},{12,8},{16,20},{20,16},{24,28},{28,24},{1,5},{5... | collective-permute-start | bytes 6291464 | tf_op jit(solution)/shard_map/ppermute | solution.py:407
  2.3 8.6 %collective-permute-start = (bf16[656,256]{1,0:T(8,128)(2,1)S(1)}, bf16[656,256]{1,0:T(8,128)(2,1)S(1)}, u32[]{:S(2)}, u32[]{:S(2)}) collective-permute-start(bf16[656,256]{1,0:T(8,128)(2,1)S(1)} %get-tuple-element.17), channel_id=1, source_target_pairs={{0,12},{4,16},{8,28},{12,0},{16,4},{20,24},{24,20},{28,8},{1,13},{... | collective-permute-start | bytes 1007624 | tf_op jit(solution)/shard_map/ppermute | solution.py:407
  4.9 1.2 %collective-permute-start.1 = (bf16[16,1024]{1,0:T(8,128)(2,1)S(1)}, bf16[16,1024]{1,0:T(8,128)(2,1)S(1)}, u32[]{:S(2)}, u32[]{:S(2)}) collective-permute-start(bf16[16,1024]{1,0:T(8,128)(2,1)S(1)} %get-tuple-element.18.own_ref), channel_id=1, source_target_pairs={{0,4},{4,0},{8,12},{12,8},{16,20},{20,16},{24,28},{28,24},{1,5},{5... | collective-permute-start | bytes 98312 | tf_op jit(solution)/shard_map/ppermute | solution.py:407
  9.1 3.4 %collective-permute-start.3 = (f32[8,1024]{1,0:T(8,128)S(1)}, f32[8,1024]{1,0:T(8,128)S(1)}, u32[]{:S(2)}, u32[]{:S(2)}) collective-permute-start(f32[8,1024]{1,0:T(8,128)S(1)} %mlp.1), channel_id=1, source_target_pairs={{0,5},{1,4},{2,7},{3,6},{4,1},{5,0},{6,3},{7,2},{8,13},{9,12},{10,... | collective-permute-start | bytes 98312 | tf_op jit(solution)/shard_map/ppermute | solution.py:415
  10.9 10.3 %collective-permute-start.6 = (bf16[1312,256]{1,0:T(8,128)(2,1)S(1)}, bf16[1312,256]{1,0:T(8,128)(2,1)S(1)}, u32[]{:S(2)}, u32[]{:S(2)}) collective-permute-start(bf16[1312,256]{1,0:T(8,128)(2,1)S(1)} %constant_dynamic-update-slice_fusion.refs_1_), channel_id=1, source_target_pairs={{0,20},{4,8},{8,4},{12,24},{16,28},{20,0},{24,12},{28,16},{1,21},{... | collective-permute-start | bytes 2015240 | tf_op jit(solution)/shard_map/ppermute | solution.py:407
  12.6 4.9 %collective-permute-start.4 = (bf16[1216,256]{1,0:T(8,128)(2,1)S(1)}, bf16[1216,256]{1,0:T(8,128)(2,1)S(1)}, u32[]{:S(2)}, u32[]{:S(2)}) collective-permute-start(bf16[1216,256]{1,0:T(8,128)(2,1)S(1)} %slice.6), channel_id=1, source_target_pairs={{0,4},{4,0},{8,12},{12,8},{16,20},{20,16},{24,28},{28,24},{1,5},{5... | collective-permute-start | bytes 1867784 | tf_op jit(solution)/shard_map/ppermute | solution.py:407
  13.0 4.7 %collective-permute-start.5 = (bf16[96,256]{1,0:T(8,128)(2,1)S(1)}, bf16[96,256]{1,0:T(8,128)(2,1)S(1)}, u32[]{:S(2)}, u32[]{:S(2)}) collective-permute-start(bf16[96,256]{1,0:T(8,128)(2,1)S(1)} %slice.7), channel_id=1, source_target_pairs={{0,4},{4,0},{8,12},{12,8},{16,20},{20,16},{24,28},{28,24},{1,5},{5... | collective-permute-start | bytes 147464 | tf_op jit(solution)/shard_map/ppermute | solution.py:407
  13.2 4.3 %collective-permute-start.7 = (f32[8,1024]{1,0:T(8,128)S(1)}, f32[8,1024]{1,0:T(8,128)S(1)}, u32[]{:S(2)}, u32[]{:S(2)}) collective-permute-start(f32[8,1024]{1,0:T(8,128)S(1)} %add.3.part_ref), channel_id=1, source_target_pairs={{0,6},{1,7},{2,4},{3,5},{4,2},{5,3},{6,0},{7,1},{8,14},{9,15},{10,... | collective-permute-start | bytes 98312 | tf_op jit(solution)/shard_map/ppermute | solution.py:415
  17.7 3.5 %collective-permute-start.8 = (bf16[8,1024]{1,0:T(8,128)(2,1)S(1)}, bf16[8,1024]{1,0:T(8,128)(2,1)S(1)}, u32[]{:S(2)}, u32[]{:S(2)}) collective-permute-start(bf16[8,1024]{1,0:T(8,128)(2,1)S(1)} %resid.1), channel_id=1, source_target_pairs={{0,12},{4,16},{8,28},{12,0},{16,4},{20,24},{24,20},{28,8},{1,13},{... | collective-permute-start | bytes 49160 | tf_op jit(solution)/shard_map/ppermute | solution.py:407
  21.2 2.3 %collective-permute-start.9 = (bf16[1312,256]{1,0:T(8,128)(2,1)S(1)}, bf16[1312,256]{1,0:T(8,128)(2,1)S(1)}, u32[]{:S(2)}, u32[]{:S(2)}) collective-permute-start(bf16[1312,256]{1,0:T(8,128)(2,1)S(1)} %collective-permute-done.6.refs_3_), channel_id=1, source_target_pairs={{0,4},{4,0},{8,12},{12,8},{16,20},{20,16},{24,28},{28,24},{1,5},{5... | collective-permute-start | bytes 2015240 | tf_op jit(solution)/shard_map/ppermute | solution.py:407
  21.7 3.3 %collective-permute-start.10 = (bf16[16,1024]{1,0:T(8,128)(2,1)S(1)}, bf16[16,1024]{1,0:T(8,128)(2,1)S(1)}, u32[]{:S(2)}, u32[]{:S(2)}) collective-permute-start(bf16[16,1024]{1,0:T(8,128)(2,1)S(1)} %constant_dynamic-update-slice_fusion.2.refs_0_), channel_id=1, source_target_pairs={{0,20},{4,8},{8,4},{12,24},{16,28},{20,0},{24,12},{28,16},{1,21},{... | collective-permute-start | bytes 98312 | tf_op jit(solution)/shard_map/ppermute | solution.py:407

commit v6 on v5

--- a/solution.py
+++ b/solution.py
@@ -155,7 +155,6 @@
 TN = (((0,), (0,)), ((), ()))
 Q_ROWS = 16
 LATE_ROWS = 96
-MLP_PARTS = 2
 
 
 def load_kernel(
@@ -236,28 +235,21 @@
     return inv_rms, rows * inv_rms
 
 
-def mlp_kernel(own_ref, other_ref, w_in_ref, w_out_ref, out_ref, w_in, sems):
-    parts, size = w_in.shape[0], w_in.shape[2]
-    copies = []
-    for part in range(parts):
-        span = pl.ds(part * size, size)
-        copies.append(pltpu.make_async_copy(w_in_ref.at[:, span], w_in.at[part], sems.at[part]))
-    for copy in copies:
-        copy.start()
+def fetch_kernel(w_in_ref, out_ref, sem):
+    copy = pltpu.make_async_copy(w_in_ref, out_ref, sem)
+    copy.start()
+    copy.wait()
+
+
+def mlp_kernel(own_ref, other_ref, w_in_ref, w_out_ref, out_ref):
     cot, rows, gain = chip_rows(own_ref, other_ref)
     normed = (rms_parts(rows)[1] * gain).astype(jnp.bfloat16)
     hidden_grad = lax.dot_general(
         cot.astype(jnp.bfloat16), w_out_ref[...], NT, preferred_element_type=jnp.float32
     )
-    total = jnp.zeros(out_ref.shape, jnp.float32)
-    for part, copy in enumerate(copies):
-        copy.wait()
-        up = w_in[part]
-        pre_act = jnp.dot(normed, up, preferred_element_type=jnp.float32)
-        span = slice(part * size, (part + 1) * size)
-        pre_grad = (hidden_grad[:, span] * gelu_slope(pre_act)).astype(jnp.bfloat16)
-        total += lax.dot_general(pre_grad, up, NT, preferred_element_type=jnp.float32)
-    out_ref[...] = total
+    pre_act = jnp.dot(normed, w_in_ref[...], preferred_element_type=jnp.float32)
+    pre_grad = (hidden_grad * gelu_slope(pre_act)).astype(jnp.bfloat16)
+    out_ref[...] = lax.dot_general(pre_grad, w_in_ref[...], NT, preferred_element_type=jnp.float32)
 
 
 def resid_kernel(part_ref, arrived_ref, own_ref, other_ref, out_ref):
@@ -434,7 +426,6 @@
     lat_dev, width = cot.shape
     latents = lat_dev * ctx
     events_dev, features = keys.shape
-    hidden = w_in.shape[1]
     vmem = pl.BlockSpec(memory_space=pltpu.VMEM)
     hbm = pl.BlockSpec(memory_space=pltpu.HBM)
     pack_rows = 2 * events_dev + w_proj.shape[0] // 2 + Q_ROWS
@@ -474,21 +465,26 @@
     hd_bits = [1 << shift for shift in range(hd.bit_length() - 1)]
     steps = (tuple(bit | 1 for bit in chip_bits), tuple(bit | 1 for bit in reversed(chip_bits)))
     first_piece = swap(pack, *steps[0])
+    near_in = pl.pallas_call(
+        fetch_kernel,
+        out_shape=jax.ShapeDtypeStruct(w_in.shape, jnp.bfloat16),
+        in_specs=[hbm],
+        out_specs=vmem,
+        scratch_shapes=[pltpu.SemaphoreType.DMA(())],
+        compiler_params=params(8),
+        name="fetch",
+    )(in_hbm(after(w_in, own_rows)))
     part = pl.pallas_call(
         mlp_kernel,
         out_shape=jax.ShapeDtypeStruct((2 * lat_dev, width), jnp.float32),
-        in_specs=[vmem] * 2 + [hbm, vmem],
+        in_specs=[vmem] * 4,
         out_specs=vmem,
-        scratch_shapes=[
-            pltpu.VMEM((MLP_PARTS, width, hidden // MLP_PARTS), jnp.bfloat16),
-            pltpu.SemaphoreType.DMA((MLP_PARTS,)),
-        ],
         compiler_params=params(16),
         cost_estimate=pl.CostEstimate(
             flops=12 * lat_dev * w_in.size, bytes_accessed=4 * w_in.size, transcendentals=0
         ),
         name="mlp",
-    )(own_rows, other_rows, in_hbm(w_in), near_out)
+    )(own_rows, other_rows, near_in, near_out)
     first_pair = jnp.concatenate([pack, after(first_piece, part)], axis=0)
     second_pair = swap(first_pair, *steps[1])
     for bit in hd_bits[:-1]:

time: 27 us -> 25.7 us (0.952)
  waiting for transfers between devices: 5.71 us -> 4.55 us
  starting transfers between devices: 13.4 us -> 13.1 us
    pallas_call x0 -> x1, Pallas kernels: none -> 1.6 us  [per_device_packed(): pl.pallas_call(fetch_kernel, out_shape=jax.ShapeDtypeStruct(w_in.shape, j...]
    pallas_call x1, Pallas kernels: 2.96 us -> 1.46 us  [per_device_packed(): pl.pallas_call(mlp_kernel, out_shape=jax.ShapeDtypeStruct((2 * lat_dev, w...]
    ppermute x9, waiting for transfers between devices: 4.04 us -> 2.78 us  [swap(): return lax.ppermute(array, 'ctx', pairs)]
    ppermute x2, starting transfers between devices: 4.46 us -> 4.12 us  [swap_hd(): return lax.ppermute(array, ('ctx', 'hd'), pairs)]
  transfers between devices with their start and end apart: 11 -> 11, of which waited for: 6 -> 5; matrix products, arithmetic and copies ran while one was open for 1% -> 1% of each run, Pallas kernels for 19% -> 20%
where the time goes in v6:
time: 25.7 us; the launch traced here: 25.5 us
  starting transfers between devices  13.1 us (51%)
  Pallas kernels  6.96 us (27%)
  waiting for transfers between devices  4.55 us (18%)
  between operations  0.72 us (3%)
    ppermute x9, starting transfers between devices, swap(): return lax.ppermute(array, 'ctx', pairs)  9 us
    ppermute x2, starting transfers between devices, swap_hd(): return lax.ppermute(array, ('ctx', 'hd'), pairs)  4.12 us
    ppermute x9, waiting for transfers between devices, swap(): return lax.ppermute(array, 'ctx', pairs)  2.78 us
    pallas_call x1, Pallas kernels, per_device_packed(): pl.pallas_call(functools.partial(grads_kernel, row_offsets, pair_offset,...  1.78 us
    ppermute x2, waiting for transfers between devices, swap_hd(): return lax.ppermute(array, ('ctx', 'hd'), pairs)  1.78 us
    pallas_call x1, Pallas kernels, per_device_packed(): pl.pallas_call(fetch_kernel, out_shape=jax.ShapeDtypeStruct(w_in.shape, j...  1.6 us
    pallas_call x1, Pallas kernels, per_device_packed(): pl.pallas_call(mlp_kernel, out_shape=jax.ShapeDtypeStruct((2 * lat_dev, w...  1.46 us
    pallas_call x1, Pallas kernels, per_device_packed(): pl.pallas_call(load_kernel, out_shape=(jax.ShapeDtypeStruct((pack_rows, f...  1.12 us
  transfers between devices with their start and end apart: 11, of which 5 were waited for; matrix products, arithmetic and copies ran while one was open for 1% of the time, Pallas kernels for 20%

profile of v6, /device:TPU:0, one launch (start us, length us, event | category | flops | bytes accessed | tf_op | source)
XLA Modules:
  0.0 25.5 jit_solution(14254773993399427360)
XLA Ops:
  0.6 0.5 %collective-permute-start.2 = (bf16[1024,1024]{1,0:T(8,128)(2,1)}, bf16[1024,1024]{1,0:T(8,128)(2,1)S(1)}, u32[]{:S(2)}, u32[]{:S(2)}) collective-permute-start(bf16[1024,1024]{1,0:T(8,128)(2,1)} %param.15), channel_id=1, source_target_pairs={{0,4},{4,0},{8,12},{12,8},{16,20},{20,16},{24,28},{28,24},{1,5},{5... | collective-permute-start | bytes 6291464 | tf_op jit(solution)/shard_map/ppermute | solution.py:399
  1.2 1.1 %load.1 = (bf16[656,256]{1,0:T(8,128)(2,1)S(1)}, bf16[16,1024]{1,0:T(8,128)(2,1)S(1)}, s32[8,128]{1,0:T(8,128)S(1)}) custom-call(bf16[256,256]{1,0:T(8,128)(2,1)} %k_ref.1, bf16[256,256]{1,0:T(8,128)(2,1)} %v_ref.1, bf16[256,128]{1,0:T(8,128)(2,1)} %w_ref.1, bf16[4,256]{1,0:T(4,128)(2,1)} %q_ref.1, bf16[4,1024]{1,0:T(4,128)(2,1)} %cot_ref.1, ...), custom_call_target="tpu_custom_call" | custom-call | tf_op jit(solution)/shard_map/load/pallas_call | solution.py:433
  2.3 2.7 %collective-permute-start = (bf16[656,256]{1,0:T(8,128)(2,1)S(1)}, bf16[656,256]{1,0:T(8,128)(2,1)S(1)}, u32[]{:S(2)}, u32[]{:S(2)}) collective-permute-start(bf16[656,256]{1,0:T(8,128)(2,1)S(1)} %get-tuple-element.18), channel_id=1, source_target_pairs={{0,12},{4,16},{8,28},{12,0},{16,4},{20,24},{24,20},{28,8},{1,13},{... | collective-permute-start | bytes 1007624 | tf_op jit(solution)/shard_map/ppermute | solution.py:399
  4.9 0.0 collective-permute-start.1
  5.0 1.6 %fetch.1.w_in_ref = bf16[1024,1024]{1,0:T(8,128)(2,1)S(1)} custom-call(bf16[1024,1024]{1,0:T(8,128)(2,1)} %w_in_ref), custom_call_target="tpu_custom_call" | custom-call | tf_op jit(solution)/shard_map/fetch/pallas_call | solution.py:468
  6.7 1.5 %mlp.1 = f32[8,1024]{1,0:T(8,128)S(1)} custom-call(bf16[16,1024]{1,0:T(8,128)(2,1)S(1)} %get-tuple-element.19.own_ref, bf16[16,1024]{1,0:T(8,128)(2,1)S(1)} %collective-permute-done.1.other_ref, bf16[1024,1024]{1,0:T(8,128)(2,1)S(1)} %fetch.1.w_in_ref, bf16[1024,1024]{1,0:T(8,128)(2,1)S(1)} %collective-permute-done.2.w_out_ref), custom_call_target="tpu_custom_call" | custom-call | flops 50331648 | bytes 4194304 | tf_op jit(solution)/shard_map/mlp/pallas_call | solution.py:477
  8.1 1.7 %collective-permute-start.3 = (f32[8,1024]{1,0:T(8,128)S(1)}, f32[8,1024]{1,0:T(8,128)S(1)}, u32[]{:S(2)}, u32[]{:S(2)}) collective-permute-start(f32[8,1024]{1,0:T(8,128)S(1)} %mlp.1), channel_id=1, source_target_pairs={{0,5},{1,4},{2,7},{3,6},{4,1},{5,0},{6,3},{7,2},{8,13},{9,12},{10,... | collective-permute-start | bytes 98312 | tf_op jit(solution)/shard_map/ppermute | solution.py:407
  9.8 0.0 collective-permute-done
  9.8 1.8 %collective-permute-start.6 = (bf16[1312,256]{1,0:T(8,128)(2,1)S(1)}, bf16[1312,256]{1,0:T(8,128)(2,1)S(1)}, u32[]{:S(2)}, u32[]{:S(2)}) collective-permute-start(bf16[1312,256]{1,0:T(8,128)(2,1)S(1)} %constant_dynamic-update-slice_fusion.refs_1_), channel_id=1, source_target_pairs={{0,20},{4,8},{8,4},{12,24},{16,28},{20,0},{24,12},{28,16},{1,21},{... | collective-permute-start | bytes 2015240 | tf_op jit(solution)/shard_map/ppermute | solution.py:399
  11.7 0.3 %collective-permute-start.4 = (bf16[1216,256]{1,0:T(8,128)(2,1)S(1)}, bf16[1216,256]{1,0:T(8,128)(2,1)S(1)}, u32[]{:S(2)}, u32[]{:S(2)}) collective-permute-start(bf16[1216,256]{1,0:T(8,128)(2,1)S(1)} %slice.6), channel_id=1, source_target_pairs={{0,4},{4,0},{8,12},{12,8},{16,20},{20,16},{24,28},{28,24},{1,5},{5... | collective-permute-start | bytes 1867784 | tf_op jit(solution)/shard_map/ppermute | solution.py:399
  12.1 0.2 collective-permute-start.5
  12.3 2.5 %collective-permute-start.7 = (f32[8,1024]{1,0:T(8,128)S(1)}, f32[8,1024]{1,0:T(8,128)S(1)}, u32[]{:S(2)}, u32[]{:S(2)}) collective-permute-start(f32[8,1024]{1,0:T(8,128)S(1)} %add.3.part_ref), channel_id=1, source_target_pairs={{0,6},{1,7},{2,4},{3,5},{4,2},{5,3},{6,0},{7,1},{8,14},{9,15},{10,... | collective-permute-start | bytes 98312 | tf_op jit(solution)/shard_map/ppermute | solution.py:407
  14.8 1.8 %collective-permute-done.7.arrived_ref = f32[8,1024]{1,0:T(8,128)S(1)} collective-permute-done((f32[8,1024]{1,0:T(8,128)S(1)}, f32[8,1024]{1,0:T(8,128)S(1)}, u32[]{:S(2)}, u32[]{:S(2)}) %collective-permute-start.7) | collective-permute-done | bytes 32800 | tf_op jit(solution)/shard_map/ppermute | solution.py:407
  16.5 0.2 resid.1
  16.7 0.0 collective-permute-done.5
  16.7 1.5 %collective-permute-start.8 = (bf16[8,1024]{1,0:T(8,128)(2,1)S(1)}, bf16[8,1024]{1,0:T(8,128)(2,1)S(1)}, u32[]{:S(2)}, u32[]{:S(2)}) collective-permute-start(bf16[8,1024]{1,0:T(8,128)(2,1)S(1)} %resid.1), channel_id=1, source_target_pairs={{0,12},{4,16},{8,28},{12,0},{16,4},{20,24},{24,20},{28,8},{1,13},{... | collective-permute-start | bytes 49160 | tf_op jit(solution)/shard_map/ppermute | solution.py:399
  18.2 1.9 %collective-permute-done.6.refs_3_ = bf16[1312,256]{1,0:T(8,128)(2,1)S(1)} collective-permute-done((bf16[1312,256]{1,0:T(8,128)(2,1)S(1)}, bf16[1312,256]{1,0:T(8,128)(2,1)S(1)}, u32[]{:S(2)}, u32[]{:S(2)}) %collective-permute-start.6) | collective-permute-done | bytes 671776 | tf_op jit(solution)/shard_map/ppermute | solution.py:399
  20.1 0.1 collective-permute-done.8
  20.2 0.2 collective-permute-start.9
  20.4 1.7 %collective-permute-start.10 = (bf16[16,1024]{1,0:T(8,128)(2,1)S(1)}, bf16[16,1024]{1,0:T(8,128)(2,1)S(1)}, u32[]{:S(2)}, u32[]{:S(2)}) collective-permute-start(bf16[16,1024]{1,0:T(8,128)(2,1)S(1)} %constant_dynamic-update-slice_fusion.2.refs_0_), channel_id=1, source_target_pairs={{0,20},{4,8},{8,4},{12,24},{16,28},{20,0},{24,12},{28,16},{1,21},{... | collective-permute-start | bytes 98312 | tf_op jit(solution)/shard_map/ppermute | solution.py:399
  22.2 0.2 collective-permute-done.9.refs_4_
  22.3 0.8 %probs.1 = (f32[8,256,128]{2,1,0:T(8,128)S(1)}, bf16[5,256,256]{2,1,0:T(8,128)(2,1)S(1)}, bf16[5,256,256]{2,1,0:T(8,128)(2,1)S(1)}, bf16[8,128,256]{2,1,0:T(8,128)(2,1)S(1)}, bf16[128,256]{1,0:T(8,128)(2,1)S(1)}) custom-call(s32[8,128]{1,0:T(8,128)S(1)} %get-tuple-element.17.refs_0_, bf16[1312,256]{1,0:T(8,128)(2,1)S(1)} %constant_dynamic-update-slice_fusion.refs_1_, ...), custom_call_target="tpu_custom_call" | custom-call | flops 134217728 | bytes 524288 | tf_op jit(solution)/shard_map/probs/pallas_call | solution.py:520
  23.1 0.6 %collective-permute-done.10.refs_1_ = bf16[16,1024]{1,0:T(8,128)(2,1)S(1)} collective-permute-done((bf16[16,1024]{1,0:T(8,128)(2,1)S(1)}, bf16[16,1024]{1,0:T(8,128)(2,1)S(1)}, u32[]{:S(2)}, u32[]{:S(2)}) %collective-permute-start.10) | collective-permute-done | bytes 32800 | tf_op jit(solution)/shard_map/ppermute | solution.py:399
  23.7 1.8 %grads.1 = (bf16[4,256]{1,0:T(4,128)(2,1)}, bf16[256,256]{1,0:T(8,128)(2,1)}, bf16[256,256]{1,0:T(8,128)(2,1)}) custom-call(f32[8,256,128]{2,1,0:T(8,128)S(1)} %get-tuple-element.26.probs_ref, bf16[5,256,256]{2,1,0:T(8,128)(2,1)S(1)} %get-tuple-element.27.keys_ref, bf16[5,256,256]{2,1,0:T(8,128)(2,1)S(1)} %get-tuple-element.28.values_ref, ...), custom_call_target="tpu_custom_call" | custom-call | tf_op jit(solution)/shard_map/grads/pallas_call | solution.py:538
  (12 shorter events, 0.2 us)
Async XLA Ops:
  0.6 6.0 %collective-permute-start.2 = (bf16[1024,1024]{1,0:T(8,128)(2,1)}, bf16[1024,1024]{1,0:T(8,128)(2,1)S(1)}, u32[]{:S(2)}, u32[]{:S(2)}) collective-permute-start(bf16[1024,1024]{1,0:T(8,128)(2,1)} %param.15), channel_id=1, source_target_pairs={{0,4},{4,0},{8,12},{12,8},{16,20},{20,16},{24,28},{28,24},{1,5},{5... | collective-permute-start | bytes 6291464 | tf_op jit(solution)/shard_map/ppermute | solution.py:399
  2.3 7.5 %collective-permute-start = (bf16[656,256]{1,0:T(8,128)(2,1)S(1)}, bf16[656,256]{1,0:T(8,128)(2,1)S(1)}, u32[]{:S(2)}, u32[]{:S(2)}) collective-permute-start(bf16[656,256]{1,0:T(8,128)(2,1)S(1)} %get-tuple-element.18), channel_id=1, source_target_pairs={{0,12},{4,16},{8,28},{12,0},{16,4},{20,24},{24,20},{28,8},{1,13},{... | collective-permute-start | bytes 1007624 | tf_op jit(solution)/shard_map/ppermute | solution.py:399
  4.9 1.7 %collective-permute-start.1 = (bf16[16,1024]{1,0:T(8,128)(2,1)S(1)}, bf16[16,1024]{1,0:T(8,128)(2,1)S(1)}, u32[]{:S(2)}, u32[]{:S(2)}) collective-permute-start(bf16[16,1024]{1,0:T(8,128)(2,1)S(1)} %get-tuple-element.19.own_ref), channel_id=1, source_target_pairs={{0,4},{4,0},{8,12},{12,8},{16,20},{20,16},{24,28},{28,24},{1,5},{5... | collective-permute-start | bytes 98312 | tf_op jit(solution)/shard_map/ppermute | solution.py:399
  8.1 3.5 %collective-permute-start.3 = (f32[8,1024]{1,0:T(8,128)S(1)}, f32[8,1024]{1,0:T(8,128)S(1)}, u32[]{:S(2)}, u32[]{:S(2)}) collective-permute-start(f32[8,1024]{1,0:T(8,128)S(1)} %mlp.1), channel_id=1, source_target_pairs={{0,5},{1,4},{2,7},{3,6},{4,1},{5,0},{6,3},{7,2},{8,13},{9,12},{10,... | collective-permute-start | bytes 98312 | tf_op jit(solution)/shard_map/ppermute | solution.py:407
  9.8 10.3 %collective-permute-start.6 = (bf16[1312,256]{1,0:T(8,128)(2,1)S(1)}, bf16[1312,256]{1,0:T(8,128)(2,1)S(1)}, u32[]{:S(2)}, u32[]{:S(2)}) collective-permute-start(bf16[1312,256]{1,0:T(8,128)(2,1)S(1)} %constant_dynamic-update-slice_fusion.refs_1_), channel_id=1, source_target_pairs={{0,20},{4,8},{8,4},{12,24},{16,28},{20,0},{24,12},{28,16},{1,21},{... | collective-permute-start | bytes 2015240 | tf_op jit(solution)/shard_map/ppermute | solution.py:399
  11.7 4.8 %collective-permute-start.4 = (bf16[1216,256]{1,0:T(8,128)(2,1)S(1)}, bf16[1216,256]{1,0:T(8,128)(2,1)S(1)}, u32[]{:S(2)}, u32[]{:S(2)}) collective-permute-start(bf16[1216,256]{1,0:T(8,128)(2,1)S(1)} %slice.6), channel_id=1, source_target_pairs={{0,4},{4,0},{8,12},{12,8},{16,20},{20,16},{24,28},{28,24},{1,5},{5... | collective-permute-start | bytes 1867784 | tf_op jit(solution)/shard_map/ppermute | solution.py:399
  12.1 4.7 %collective-permute-start.5 = (bf16[96,256]{1,0:T(8,128)(2,1)S(1)}, bf16[96,256]{1,0:T(8,128)(2,1)S(1)}, u32[]{:S(2)}, u32[]{:S(2)}) collective-permute-start(bf16[96,256]{1,0:T(8,128)(2,1)S(1)} %slice.7), channel_id=1, source_target_pairs={{0,4},{4,0},{8,12},{12,8},{16,20},{20,16},{24,28},{28,24},{1,5},{5... | collective-permute-start | bytes 147464 | tf_op jit(solution)/shard_map/ppermute | solution.py:399
  12.3 4.2 %collective-permute-start.7 = (f32[8,1024]{1,0:T(8,128)S(1)}, f32[8,1024]{1,0:T(8,128)S(1)}, u32[]{:S(2)}, u32[]{:S(2)}) collective-permute-start(f32[8,1024]{1,0:T(8,128)S(1)} %add.3.part_ref), channel_id=1, source_target_pairs={{0,6},{1,7},{2,4},{3,5},{4,2},{5,3},{6,0},{7,1},{8,14},{9,15},{10,... | collective-permute-start | bytes 98312 | tf_op jit(solution)/shard_map/ppermute | solution.py:407
  16.7 3.5 %collective-permute-start.8 = (bf16[8,1024]{1,0:T(8,128)(2,1)S(1)}, bf16[8,1024]{1,0:T(8,128)(2,1)S(1)}, u32[]{:S(2)}, u32[]{:S(2)}) collective-permute-start(bf16[8,1024]{1,0:T(8,128)(2,1)S(1)} %resid.1), channel_id=1, source_target_pairs={{0,12},{4,16},{8,28},{12,0},{16,4},{20,24},{24,20},{28,8},{1,13},{... | collective-permute-start | bytes 49160 | tf_op jit(solution)/shard_map/ppermute | solution.py:399
  20.2 2.1 %collective-permute-start.9 = (bf16[1312,256]{1,0:T(8,128)(2,1)S(1)}, bf16[1312,256]{1,0:T(8,128)(2,1)S(1)}, u32[]{:S(2)}, u32[]{:S(2)}) collective-permute-start(bf16[1312,256]{1,0:T(8,128)(2,1)S(1)} %collective-permute-done.6.refs_3_), channel_id=1, source_target_pairs={{0,4},{4,0},{8,12},{12,8},{16,20},{20,16},{24,28},{28,24},{1,5},{5... | collective-permute-start | bytes 2015240 | tf_op jit(solution)/shard_map/ppermute | solution.py:399
  20.4 3.3 %collective-permute-start.10 = (bf16[16,1024]{1,0:T(8,128)(2,1)S(1)}, bf16[16,1024]{1,0:T(8,128)(2,1)S(1)}, u32[]{:S(2)}, u32[]{:S(2)}) collective-permute-start(bf16[16,1024]{1,0:T(8,128)(2,1)S(1)} %constant_dynamic-update-slice_fusion.2.refs_0_), channel_id=1, source_target_pairs={{0,20},{4,8},{8,4},{12,24},{16,28},{20,0},{24,12},{28,16},{1,21},{... | collective-permute-start | bytes 98312 | tf_op jit(solution)/shard_map/ppermute | solution.py:399
